TPU v7x, 32 devices: a whole 2x2x4 slice. The times are simulated.
32 devices in a mesh: dp: 32 (over z, y, x, core).
Axes of the slice: x: 2, y: 2, z: 4, core: 2. Of those that a mesh axis runs over, the one named last changes fastest.
Arguments:
- images: bfloat16 [64, 197, 384], P('dp'), may hold values from -6 to 6
- cotangent: bfloat16 [64, 197, 384], P('dp'), may hold values from -6 to 6
- present: int32 [64], P('dp'), may hold values 0 or 1
- params: float32 [2, 1777664], P(None, 'dp'), as said below
- first_moment: float32 [2, 1777664], P(None, 'dp'), as said below
- second_moment: float32 [2, 1777664], P(None, 'dp'), as said below
Outputs:
- outputs: float32 [64, 197, 384], P('dp')
- input_grad: float32 [64, 197, 384], P('dp')
- new_params: float32 [2, 1777664], P(None, 'dp')
- new_first: float32 [2, 1777664], P(None, 'dp')
- new_second: float32 [2, 1777664], P(None, 'dp')
Inputs may be any that keep to these rules, and one draw needn't show every extreme that they name: `params`: gains near 1, weights scaled by their fan-in. `first_moment`: both signs. `second_moment`: every entry positive.
All inputs are finite; a program needn't handle non-finite values. No bound on the sum of `present` on one device may be relied on, other than what follows from the above.
Results may differ from a plain program's by a relative error of at most 0.012.
Values may be sent and summed in bfloat16 or wider, within the bound.
No kernel may reach another device: no remote copies, remote signals or barrier semaphores. Data moves between devices by JAX's collectives and lax.ppermute only.
A program may use at most 128 MiB of HBM per device.

v0:
```python
import functools
import math

import jax
import jax.numpy as jnp
from jax import lax
from jax.experimental import pallas as pl
from jax.experimental.pallas import tpu as pltpu
from jax.sharding import PartitionSpec as P

D = 384
FF = 1536
HEADS = 6
HEAD_DIM = 64
SEQ = 197
MICRO = 2
STEP = 10
P_SIZE = 1774080

LANES = 128
ROWS = 208
TOKENS = MICRO * ROWS
PAIRS = HEADS // 2
COST = 1
FORWARD_UNROLL = 6
BACKWARD_UNROLL = 2
VMEM_LIMIT = 10 * 1024 * 1024
BLOCK = 512

eps_norm = 1e-06
beta_one = 0.9
beta_two = 0.999
adam_eps = 1e-08
rate_matrix = 0.1
rate_vector = 0.5
decay_matrix = 0.05
sqrt_half = 0.7071067811865476
inverse_root_tau = 0.3989422804014327

f32 = jnp.float32
bf16 = jnp.bfloat16


def layout():
    return [
        ("ln1_gain", (D,)),
        ("ln1_shift", (D,)),
        ("w_qkv", (D, 3 * D)),
        ("bias_query", (D,)),
        ("bias_value", (D,)),
        ("w_attn_out", (D, D)),
        ("bias_attn_out", (D,)),
        ("ln2_gain", (D,)),
        ("ln2_shift", (D,)),
        ("w_lift", (D, FF)),
        ("bias_lift", (FF,)),
        ("w_drop", (FF, D)),
        ("bias_drop", (D,)),
    ]


def row_offsets():
    offsets, at = {}, 0
    for label, shape in layout():
        offsets[label] = at
        at += math.prod(shape) // LANES
    offsets["end"] = at
    return offsets


ROW = row_offsets()
MLP_ROW = ROW["ln2_gain"]


def matrix_flags(position):
    square = D * D
    lifted = D * FF
    bounds = [
        (2 * D, 2 * D + 3 * square),
        (4 * D + 3 * square, 4 * D + 4 * square),
        (7 * D + 4 * square, 7 * D + 4 * square + lifted),
        (7 * D + 4 * square + lifted + FF, 7 * D + 4 * square + 2 * lifted + FF),
    ]
    flags = jnp.zeros(position.shape, dtype=bool)
    for lower, upper in bounds:
        flags = flags | (position >= lower) & (position < upper)
    return flags


def round_up(value, step):
    return (value + step - 1) // step * step


def dot(a, b, dims):
    return lax.dot_general(a, b, ((dims[0], dims[1]), ((), ())), preferred_element_type=f32)


def dot_nn(a, b):
    return dot(a, b, ((1,), (0,)))


def dot_nt(a, b):
    return dot(a, b, ((1,), (1,)))


def dot_tn(a, b):
    return dot(a, b, ((0,), (0,)))


def read_vector(flat, row, count):
    parts = [flat[row + i : row + i + 1, :] for i in range(count)]
    return jnp.concatenate(parts, axis=1)


def write_vector(flat, row, values):
    for i in range(values.shape[1] // LANES):
        flat[row + i : row + i + 1, :] = values[:, i * LANES : (i + 1) * LANES]


def read_matrix(flat, row, out, depth, width):
    blocks = width // LANES
    for j in range(blocks):
        part = flat[pl.ds(row + j, depth, stride=blocks), :]
        out[:, j * LANES : (j + 1) * LANES] = part.astype(bf16)


def write_matrix(flat, row, values, blocks):
    depth, width = values.shape
    for j in range(width // LANES):
        flat[pl.ds(row + j, depth, stride=blocks), :] = values[:, j * LANES : (j + 1) * LANES]


def normalize(values):
    center = values - jnp.mean(values, -1, keepdims=True)
    rstd = lax.rsqrt(jnp.mean(center * center, -1, keepdims=True) + eps_norm)
    return center * rstd, rstd


def norm_back(incoming, unit, rstd, gain):
    scaled = incoming * gain
    inner = jnp.mean(scaled * unit, -1, keepdims=True)
    back = rstd * (scaled - jnp.mean(scaled, -1, keepdims=True) - unit * inner)
    gain_grad = jnp.sum(incoming * unit, 0, keepdims=True)
    return back, gain_grad, jnp.sum(incoming, 0, keepdims=True)


def head_mask(head):
    lane = lax.broadcasted_iota(jnp.int32, (1, LANES), 1)
    return lane < HEAD_DIM if head == 0 else lane >= HEAD_DIM


def pair_slices(step):
    image, pair = step // PAIRS, step % PAIRS
    rows = pl.ds(pl.multiple_of(image * ROWS, 16), ROWS)
    cols = [pl.ds(pl.multiple_of(t * D + pair * LANES, LANES), LANES) for t in range(3)]
    return rows, cols


def unpack(rows_each, base, chunks, place, near, far, flat):
    count, padded = near.shape[0], near.shape[1]

    def step(chunk, carry):
        at = place[chunk]
        own = lax.rem(at, count)
        rows = jnp.where(at < count, near[own].astype(f32), far[own].astype(f32))
        flat[pl.ds((chunks[2] + chunk) * rows_each - base, padded), :] = rows
        return carry

    lax.fori_loop(chunks[0], chunks[1], step, 0)


def attention_forward(rows_each, first, place, near, far, state, *refs):
    if first:
        kept_state, refs = refs[0], refs[1:]
    w_qkv, w_out, vectors, normed_one, qkv, probs, mixed, hidden, flat = refs
    unpack(rows_each, 0, (0, -(-MLP_ROW // rows_each), 0), place, near, far, flat)
    read_matrix(flat, ROW["w_qkv"], w_qkv, D, 3 * D)
    read_matrix(flat, ROW["w_attn_out"], w_out, D, D)
    labels = ["ln1_gain", "ln1_shift", "bias_query", "bias_value", "bias_attn_out"]
    for at, label in enumerate(labels):
        vectors[at : at + 1, :] = read_vector(flat, ROW[label], 3)
    gain, shift = vectors[0:1, :], vectors[1:2, :]
    if first:
        kept_state[...] = jnp.zeros_like(kept_state)
        for image in range(MICRO):
            kept_state[image * ROWS : image * ROWS + SEQ, :] = state[image].astype(f32)
        x = kept_state[...]
    else:
        x = state[...]
    unit, _ = normalize(x)
    normed_one[...] = (unit * gain + shift).astype(bf16)
    bias_query = vectors[2:3, :]
    bias = jnp.concatenate([bias_query, jnp.zeros_like(bias_query), vectors[3:4, :]], axis=1)
    for t in range(3):
        cols = slice(t * D, (t + 1) * D)
        product = dot_nn(normed_one[...], w_qkv[:, cols]) + bias[:, cols]
        qkv[:, cols] = product.astype(bf16)

    def step(at, carry):
        rows, cols = pair_slices(at)
        query, key_rows, value_rows = qkv[rows, cols[0]], qkv[rows, cols[1]], qkv[rows, cols[2]]
        real = lax.broadcasted_iota(jnp.int32, (ROWS, ROWS), 1) < SEQ
        sides = []
        for head in range(2):
            own_key = jnp.where(head_mask(head), key_rows, jnp.zeros_like(key_rows))
            raw = jnp.where(real, dot_nt(query, own_key), -1e30)
            powers = jnp.exp((raw - jnp.max(raw, -1, keepdims=True)) * HEAD_DIM ** (-0.5))
            weight = powers / jnp.sum(powers, -1, keepdims=True)
            weight = weight.astype(bf16)
            probs[at * 2 + head] = weight
            sides.append(dot_nn(weight, value_rows))
        mixed[rows, pl.ds(pl.multiple_of((at % PAIRS) * LANES, LANES), LANES)] = jnp.where(
            head_mask(0), sides[0], sides[1]
        ).astype(bf16)
        return carry

    lax.fori_loop(0, MICRO * PAIRS, step, 0, unroll=FORWARD_UNROLL)
    hidden[...] = x + dot_nn(mixed[...], w_out[...]) + vectors[4:5, :]


def mlp_forward(rows_each, last, place_low, place_high, low_near, low_far, near, far, hidden, *refs):
    w_lift, w_drop, vectors, normed_two, active, slope, result, flat = refs
    count = 2 * near.shape[0]
    begin = MLP_ROW // rows_each
    base = begin * rows_each
    unpack(rows_each, base, (begin, count, 0), place_low, low_near, low_far, flat)
    unpack(rows_each, base, (0, count, count), place_high, near, far, flat)
    read_matrix(flat, ROW["w_lift"] - base, w_lift, D, FF)
    read_matrix(flat, ROW["w_drop"] - base, w_drop, FF, D)
    for at, label in enumerate(["ln2_gain", "ln2_shift", "bias_drop"]):
        vectors[at : at + 1, :] = read_vector(flat, ROW[label] - base, 3)
    bias_lift = read_vector(flat, ROW["bias_lift"] - base, FF // LANES)
    gain, shift = vectors[0:1, :], vectors[1:2, :]
    unit, _ = normalize(hidden[...])
    normed_two[...] = (unit * gain + shift).astype(bf16)
    total = hidden[...] + vectors[2:3, :]
    for at in range(0, FF, BLOCK):
        cols = slice(at, at + BLOCK)
        lifted = dot_nn(normed_two[...], w_lift[:, cols]) + bias_lift[:, cols]
        below = 0.5 * (1.0 + lax.erf(lifted * sqrt_half))
        active[:, cols] = (lifted * below).astype(bf16)
        bell = jnp.exp(-0.5 * lifted * lifted) * inverse_root_tau
        slope[:, cols] = (below + lifted * bell).astype(bf16)
        total += dot_nn(active[:, cols], w_drop[cols, :])
    if last:
        for image in range(MICRO):
            result[image] = total[image * ROWS : image * ROWS + SEQ, :]
    else:
        result[...] = total


def pack(flat, base, rows_each, first_chunk, places, near, far):
    count, padded = near.shape[1], near.shape[2]
    for quarter, place in enumerate(places):

        def step(chunk, carry):
            at = (first_chunk + quarter * 2 * count + chunk) * rows_each - base
            index = lax.rem(place[chunk], count)

            @pl.when(place[chunk] < count)
            def _():
                near[quarter, index] = flat[pl.ds(at, padded), :].astype(bf16)

            @pl.when(place[chunk] >= count)
            def _():
                far[quarter, index] = flat[pl.ds(at, padded), :].astype(bf16)

            return carry

        lax.fori_loop(0, 2 * count, step, 0)


def mlp_backward(rows_each, last, *refs):
    if last:
        present, refs = refs[0], refs[1:]
    places, refs = refs[:2], refs[2:]
    incoming, hidden, w_lift, w_drop, vectors, normed_two, active, slope = refs[:8]
    refs = refs[8:]
    carry, near, far, g_hidden, flat = refs[:5]
    count = 4 * near.shape[1]
    if last:
        kept = refs[5]
        kept[...] = jnp.zeros_like(kept)
        for image in range(MICRO):
            seed = incoming[image].astype(f32) * present[image].astype(f32)
            kept[image * ROWS : image * ROWS + SEQ, :] = seed
        g = kept[...]
    else:
        g = incoming[...]
    base = MLP_ROW
    end = ROW["end"] - base
    flat[end:, :] = jnp.zeros((flat.shape[0] - end, LANES), f32)
    g_out = g.astype(bf16)
    write_vector(flat, ROW["bias_drop"] - base, jnp.sum(g_out.astype(f32), 0, keepdims=True))
    d_normed = jnp.zeros((TOKENS, D), f32)
    for at in range(0, FF, BLOCK):
        cols = slice(at, at + BLOCK)
        row = ROW["w_drop"] - base + at * (D // LANES)
        write_matrix(flat, row, dot_tn(active[:, cols], g_out), D // LANES)
        d_lifted = (dot_nt(g_out, w_drop[cols, :]) * slope[:, cols].astype(f32)).astype(bf16)
        row = ROW["bias_lift"] - base + at // LANES
        write_vector(flat, row, jnp.sum(d_lifted.astype(f32), 0, keepdims=True))
        row = ROW["w_lift"] - base + at // LANES
        write_matrix(flat, row, dot_tn(normed_two[...], d_lifted), FF // LANES)
        d_normed += dot_nt(d_lifted, w_lift[:, cols])
    unit, rstd = normalize(hidden[...])
    back, gain_grad, shift_grad = norm_back(d_normed, unit, rstd, vectors[0:1, :])
    write_vector(flat, ROW["ln2_gain"] - base, gain_grad)
    write_vector(flat, ROW["ln2_shift"] - base, shift_grad)
    g_hidden[...] = g + back
    carry[...] = flat[: carry.shape[0], :]
    pack(flat, base, rows_each, count, places, near, far)


def attention_backward(g_hidden, w_out, qkv, probs, mixed, d_qkv, d_out, bias_out, d_mixed):
    g_att = g_hidden[...].astype(bf16)
    bias_out[...] = jnp.broadcast_to(jnp.sum(g_att.astype(f32), 0, keepdims=True), bias_out.shape)
    d_out[...] = dot_tn(mixed[...], g_att)
    d_mixed[...] = dot_nt(g_att, w_out[...]).astype(bf16)

    def step(at, carried):
        rows, cols = pair_slices(at)
        query, key_rows, value_rows = qkv[rows, cols[0]], qkv[rows, cols[1]], qkv[rows, cols[2]]
        mixed_grad = d_mixed[rows, pl.ds(pl.multiple_of((at % PAIRS) * LANES, LANES), LANES)]
        d_query, d_key, d_value = [], [], []
        for head in range(2):
            own = jnp.where(head_mask(head), mixed_grad, jnp.zeros_like(mixed_grad))
            weight = probs[at * 2 + head]
            d_value.append(dot_tn(weight, mixed_grad))
            weight = weight.astype(f32)
            d_probs = dot_nt(own, value_rows)
            inner = jnp.sum(weight * d_probs, -1, keepdims=True)
            d_scores = (weight * (d_probs - inner)).astype(bf16)
            d_query.append(dot_nn(d_scores, key_rows))
            d_key.append(dot_tn(d_scores, query))
        scale = HEAD_DIM ** (-0.5)
        mask = head_mask(0)
        d_qkv[rows, cols[0]] = (jnp.where(mask, d_query[0], d_query[1]) * scale).astype(bf16)
        d_qkv[rows, cols[1]] = (jnp.where(mask, d_key[0], d_key[1]) * scale).astype(bf16)
        d_qkv[rows, cols[2]] = jnp.where(mask, d_value[0], d_value[1]).astype(bf16)
        return carried

    lax.fori_loop(0, MICRO * PAIRS, step, 0, unroll=BACKWARD_UNROLL)

def projection_backward(rows_each, first, *refs):
    places, refs = refs[:2], refs[2:]
    g_hidden, state, w_qkv, vectors, normed_one, d_qkv, d_out, bias_out, carry = refs[:9]
    near, far, input_grad, flat = refs[9:]
    flat[MLP_ROW : MLP_ROW + carry.shape[0], :] = carry[...]
    write_vector(flat, ROW["bias_attn_out"], bias_out[0:1, :])
    write_matrix(flat, ROW["w_attn_out"], d_out[...], D // LANES)
    query_sum = jnp.sum(d_qkv[:, :D].astype(f32), 0, keepdims=True)
    write_vector(flat, ROW["bias_query"], query_sum)
    value_sum = jnp.sum(d_qkv[:, 2 * D :].astype(f32), 0, keepdims=True)
    write_vector(flat, ROW["bias_value"], value_sum)
    d_normed = jnp.zeros((TOKENS, D), f32)
    for t in range(3):
        cols = slice(t * D, (t + 1) * D)
        part = d_qkv[:, cols]
        row = ROW["w_qkv"] + t * (D // LANES)
        write_matrix(flat, row, dot_tn(normed_one[...], part), 3 * D // LANES)
        d_normed += dot_nt(part, w_qkv[:, cols])
    unit, rstd = normalize(state[...])
    back, gain_grad, shift_grad = norm_back(d_normed, unit, rstd, vectors[0:1, :])
    write_vector(flat, ROW["ln1_gain"], gain_grad)
    write_vector(flat, ROW["ln1_shift"], shift_grad)
    total = g_hidden[...] + back
    if first:
        for image in range(MICRO):
            input_grad[image] = total[image * ROWS : image * ROWS + SEQ, :]
    else:
        input_grad[...] = total
    pack(flat, 0, rows_each, 0, places, near, far)


def call(body, name, inputs, outputs, scratch, scalars=0, flops=0):
    in_specs = [pl.BlockSpec(memory_space=pltpu.SMEM)] * scalars
    in_specs += [pl.BlockSpec(memory_space=pltpu.VMEM)] * (len(inputs) - scalars)
    shapes = [jax.ShapeDtypeStruct(shape, dtype) for shape, dtype in outputs]
    moved = sum(math.prod(s.shape) * s.dtype.itemsize for s in list(inputs) + shapes)
    return pl.pallas_call(
        body,
        name=name,
        out_shape=shapes,
        in_specs=in_specs,
        out_specs=[pl.BlockSpec(memory_space=pltpu.VMEM)] * len(shapes),
        scratch_shapes=scratch,
        compiler_params=pltpu.CompilerParams(vmem_limit_bytes=VMEM_LIMIT),
        cost_estimate=pl.CostEstimate(flops=flops // COST, bytes_accessed=moved // COST, transcendentals=0),
    )(*inputs)


def tie(values, *before):
    return lax.optimization_barrier((values, before))[0]


def together(*values):
    return lax.optimization_barrier(values)


def swap(values, size, mask):
    return lax.ppermute(values, "dp", [(i, i ^ mask) for i in range(size)])


def gather_masks(bits):
    chain = [1 << bit for bit in range(bits - 2, 2, -1)]
    return [chain + [2, 4, 1], chain + [4, 2, 1]]


def places(me, size, masks):
    relative = me ^ jnp.arange(size // 2, dtype=jnp.int32)
    place = jnp.zeros_like(relative)
    for digit, mask in enumerate(masks):
        place = place | jnp.where(relative & mask != 0, 1 << digit, 0)
    return place


def sent(part, size, mask):
    middle = part.shape[0] // 2
    return part[:middle], swap(part[middle:], size, mask)


def added(pair):
    return (pair[0].astype(f32) + pair[1].astype(f32)).astype(bf16)


def shards(size, images, cotangent, present, params, first_moment, second_moment):
    bits = size.bit_length() - 1
    width = params.shape[1]
    rows_each = width // LANES
    padded = round_up(rows_each, 16)
    half = size // 2
    me = lax.axis_index("dp")
    chain = [1 << bit for bit in range(bits - 2, 2, -1)]
    planes = [(2, 4), (4, 2)]
    place_low, place_high = [places(me, size, chain + [mask, 6 - mask, 1]) for mask in planes[0]]
    place = [places(me, size // 2, chain[1:] + [mask, 6 - mask, 1]) for mask in planes[0]]

    is_low, is_first = (me >> (bits - 1)) & 1 == 0, (me >> (bits - 2)) & 1 == 0
    flags = matrix_flags(me * width + jnp.arange(width, dtype=jnp.int32)).astype(f32)
    early = together(params, is_low, is_first, flags, place_low, place_high, *place)
    params, is_low, is_first, flags, place_low, place_high, *place = early
    compact = params.astype(bf16).reshape(2, rows_each, LANES)
    compact = jnp.pad(compact, ((0, 0), (0, padded - rows_each), (0, 0)))

    low_flat = pltpu.VMEM((-(-MLP_ROW // rows_each) * rows_each + padded, LANES), f32)
    begin = MLP_ROW // rows_each
    high_flat = pltpu.VMEM(((size - begin) * rows_each + padded, LANES), f32)
    square = TOKENS * D * D
    core_flops = 2 * 2 * MICRO * HEADS * ROWS * ROWS * HEAD_DIM

    def attend(first, near, far, state):
        outputs = [((TOKENS, D), f32)] if first else []
        outputs += [
            ((D, 3 * D), bf16),
            ((D, D), bf16),
            ((8, D), f32),
            ((TOKENS, D), bf16),
            ((TOKENS, 3 * D), bf16),
            ((MICRO * HEADS, ROWS, ROWS), bf16),
            ((TOKENS, D), bf16),
            ((TOKENS, D), f32),
        ]
        made = call(
            functools.partial(attention_forward, rows_each, first),
            "attention_forward",
            [place_low, near, far, state],
            outputs,
            [low_flat],
            scalars=1,
            flops=8 * square + core_flops,
        )
        made = made if first else [state, *made]
        return made[:-1], made[-1]

    def lift(last, low_near, low_far, near, far, hidden):
        made = call(
            functools.partial(mlp_forward, rows_each, last),
            "mlp_forward",
            [place_low, place_high, low_near, low_far, near, far, hidden],
            [
                ((D, FF), bf16),
                ((FF, D), bf16),
                ((8, D), f32),
                ((TOKENS, D), bf16),
                ((TOKENS, FF), bf16),
                ((TOKENS, FF), bf16),
                ((MICRO, SEQ, D) if last else (TOKENS, D), f32),
            ],
            [high_flat],
            scalars=2,
            flops=16 * square,
        )
        return (hidden, *made[:-1]), made[-1]

    grads_shape = ((2, size // 8, padded, LANES), bf16)

    def lift_back(last, incoming, kept):
        scratch = [pltpu.VMEM((size * rows_each + padded - MLP_ROW, LANES), f32)]
        if last:
            scratch.append(pltpu.VMEM((TOKENS, D), f32))
        return call(
            functools.partial(mlp_backward, rows_each, last),
            "mlp_backward",
            ([present] if last else []) + [*place, incoming, *kept],
            [((carry_rows, LANES), f32), grads_shape, grads_shape, ((TOKENS, D), f32)],
            scratch,
            scalars=3 if last else 2,
            flops=32 * square,
        )

    def attend_back(g_hidden, kept):
        state, w_qkv, w_out, vectors, normed_one, qkv, probs, mixed = kept
        return call(
            attention_backward,
            "attention_backward",
            [g_hidden, w_out, qkv, probs, mixed],
            [((TOKENS, 3 * D), bf16), ((D, D), f32), ((8, D), f32)],
            [pltpu.VMEM((TOKENS, D), bf16)],
            flops=4 * square + 2 * core_flops,
        )

    def project_back(first, g_hidden, kept, *made):
        state, w_qkv, w_out, vectors, normed_one, qkv, probs, mixed = kept
        return call(
            functools.partial(projection_backward, rows_each, first),
            "projection_backward",
            [*place, g_hidden, state, w_qkv, vectors, normed_one, *made],
            [grads_shape, grads_shape, ((MICRO, SEQ, D) if first else (TOKENS, D), f32)],
            [pltpu.VMEM((MLP_ROW + carry_rows, LANES), f32)],
            scalars=2,
            flops=12 * square,
        )

    def top_gathered(shard, other):
        return jnp.stack([jnp.where(is_low, shard, other), jnp.where(is_low, other, shard)])[None]

    def moved(parts, step):
        return [swap(part, size, mask) for part, mask in zip(parts, planes[step])]

    def joined(parts, received):
        return [jnp.concatenate(pair) for pair in zip(parts, received)]

    def chained(chunks):
        for mask in chain[:-1]:
            chunks = jnp.concatenate([chunks, swap(chunks, size, mask)])
        return chunks, swap(chunks, size, chain[-1])

    def halved(chunks, received):
        chunks = jnp.concatenate([chunks, received])
        return chunks[:, 0], chunks[:, 1]

    other0 = swap(compact[0], size, size // 2)
    row1, other0 = together(compact[1], other0)
    other1 = swap(row1, size, size // 2)
    half0 = halved(*chained(top_gathered(compact[0], other0)))
    received0 = moved(half0, 0)
    *received0, other1 = together(*received0, other1)
    half0 = joined(half0, received0)
    received0 = moved(half0, 1)
    half1 = halved(*chained(top_gathered(row1, other1)))
    received1 = moved(half1, 0)
    *received0, received1[0], received1[1] = together(*received0, *received1)
    near0 = joined(half0, received0)
    far0 = [swap(part, size, 1) for part in near0]
    half1 = joined(half1, received1)
    received1 = moved(half1, 1)
    one0, hidden = attend(True, near0[0], far0[0], images)
    hidden, *received1 = together(hidden, *received1)
    near1 = joined(half1, received1)
    far1 = [swap(part, size, 1) for part in near1]
    two0, state = lift(False, near0[0], far0[0], near0[1], far0[1], hidden)
    state, *far1 = together(state, *far1)
    one1, hidden = attend(False, near1[0], far1[0], state)
    two1, outputs = lift(True, near1[0], far1[0], near1[1], far1[1], hidden)

    carry_rows = round_up(half * rows_each - MLP_ROW + padded - rows_each, 8)

    def to_plane(pairs, step):
        return [sent(added(pair), size, mask) for pair, mask in zip(pairs, planes[step])]

    def to_core(near, far):
        received = swap(far, size, 1)
        return [(near[quarter], received[quarter]) for quarter in range(2)]

    def along(pairs):
        parts = [added(pair) for pair in pairs]
        for mask in reversed(chain[1:]):
            parts = [added(sent(part, size, mask)) for part in parts]
        return parts

    def hold(pairs, *others):
        values = together(*[value for pair in pairs for value in pair], *others)
        count = 2 * len(pairs)
        return [values[i : i + 2] for i in range(0, count, 2)], *values[count:]

    def to_inner(low, high):
        kept = jnp.concatenate([jnp.where(is_first, *part) for part in (low, high)])
        given = jnp.concatenate([jnp.where(is_first, *part[::-1]) for part in (low, high)])
        return kept, swap(given, size, size // 4)

    def to_top(halves):
        kept = jnp.where(is_low, halves[0], halves[1])
        return kept, swap(jnp.where(is_low, halves[1], halves[0]), size, size // 2)

    carry, near, far, g_hidden = lift_back(True, cotangent, two1)
    high1 = to_core(near, far)
    made = attend_back(g_hidden, one1)
    high1, *made = hold(high1, *made)
    near, far, incoming = project_back(False, g_hidden, one1, *made, carry)
    high1 = to_plane(high1, 1)
    low1 = to_core(near, far)
    carry, near, far, g_hidden = lift_back(False, incoming, two0)
    held, g_hidden = hold(high1 + low1, g_hidden)
    high1, low1 = to_plane(held[:2], 0), to_plane(held[2:], 1)
    high0 = to_core(near, far)
    made = attend_back(g_hidden, one0)
    held, *made = hold(high1 + low1 + high0, *made)
    high1, low1, high0 = along(held[:2]), to_plane(held[2:4], 0), to_plane(held[4:], 1)
    near, far, input_grad = project_back(True, g_hidden, one0, *made, carry)
    low1, near, far = hold(low1, near, far)
    low0 = to_core(near, far)
    high0 = to_plane(high0, 0)
    inner1 = to_inner(along(low1), high1)
    low0, = hold(low0)
    low0 = to_plane(low0, 1)
    held, = hold(low0 + high0 + [inner1])
    low0, high0, top1 = to_plane(held[:2], 0), along(held[2:4]), to_top(added(held[4]))
    held, *high0 = hold(low0, *high0)
    inner0 = to_inner(along(held), high0)
    held, outputs, input_grad = hold([inner0, top1], outputs, input_grad)
    inner0, top1 = held
    top0 = to_top(added(inner0))
    sum0, sum1 = [pair[0].astype(f32) + pair[1].astype(f32) for pair in (top0, top1)]
    owned = [total[:rows_each].reshape(width) for total in (sum0, sum1)]

    grads = jnp.stack(owned)
    flags = flags[None, :] > 0
    rate = jnp.where(flags, rate_matrix, rate_vector)
    decay = jnp.where(flags, decay_matrix, 0.0)
    new_first = beta_one * first_moment + (1.0 - beta_one) * grads
    new_second = beta_two * second_moment + (1.0 - beta_two) * grads * grads
    first_hat = new_first / (1.0 - beta_one**STEP)
    second_hat = new_second / (1.0 - beta_two**STEP)
    new_params = params - rate * (first_hat / (jnp.sqrt(second_hat) + adam_eps) + decay * params)
    return (outputs, input_grad, new_params, new_first, new_second)


def solution(mesh):
    in_specs = (
        P("dp", None, None),
        P("dp", None, None),
        P("dp"),
        P(None, "dp"),
        P(None, "dp"),
        P(None, "dp"),
    )
    out_specs = (
        P("dp", None, None),
        P("dp", None, None),
        P(None, "dp"),
        P(None, "dp"),
        P(None, "dp"),
    )
    body = functools.partial(shards, mesh.shape["dp"])
    return jax.shard_map(body, mesh=mesh, in_specs=in_specs, out_specs=out_specs, check_vma=False)
```

profile of v0, /device:TPU:0, one launch (start us, length us, event | category | flops | bytes accessed | tf_op | source)
XLA Modules:
  0.0 154.1 jit_solution(12550671019775432603)
XLA Ops:
  2.5 4.1 %collective-permute-start = (bf16[448,128]{1,0:T(8,128)(2,1)S(1)}, bf16[448,128]{1,0:T(8,128)(2,1)S(1)}, u32[]{:S(2)}, u32[]{:S(2)}) collective-permute-start(bf16[448,128]{1,0:T(8,128)(2,1)S(1)} %get-tuple-element.358), channel_id=1, source_target_pairs={{0,16},{1,17},{2,18},{3,19},{4,20},{5,21},{6,22},{7,23},{8,24},{9,... | collective-permute-start | bytes 344072 | tf_op jit(solution)/shard_map/ppermute | solution.py:402
  6.6 5.6 %collective-permute-done = bf16[448,128]{1,0:T(8,128)(2,1)S(1)} collective-permute-done((bf16[448,128]{1,0:T(8,128)(2,1)S(1)}, bf16[448,128]{1,0:T(8,128)(2,1)S(1)}, u32[]{:S(2)}, u32[]{:S(2)}) %collective-permute-start) | collective-permute-done | bytes 114720 | tf_op jit(solution)/shard_map/ppermute | solution.py:402
  13.1 6.1 %collective-permute-done.1 = bf16[1,2,448,128]{3,2,1,0:T(8,128)(2,1)S(1)} collective-permute-done((bf16[1,2,448,128]{3,2,1,0:T(8,128)(2,1)S(1)}, bf16[1,2,448,128]{3,2,1,0:T(8,128)(2,1)S(1)}, u32[]{:S(2)}, u32[]{:S(2)}) %collective-permute-start.1) | collective-permute-done | bytes 229408 | tf_op jit(solution)/shard_map/ppermute | solution.py:402
  22.0 3.3 %collective-permute-start.4 = (bf16[448,128]{1,0:T(8,128)(2,1)S(1)}, bf16[448,128]{1,0:T(8,128)(2,1)S(1)}, u32[]{:S(2)}, u32[]{:S(2)}) collective-permute-start(bf16[448,128]{1,0:T(8,128)(2,1)S(1)} %get-tuple-element.148), channel_id=1, source_target_pairs={{0,16},{1,17},{2,18},{3,19},{4,20},{5,21},{6,22},{7,23},{8,24},{9,... | collective-permute-start | bytes 344072 | tf_op jit(solution)/shard_map/ppermute | solution.py:402
  25.3 4.7 %collective-permute-done.4 = bf16[448,128]{1,0:T(8,128)(2,1)S(1)} collective-permute-done((bf16[448,128]{1,0:T(8,128)(2,1)S(1)}, bf16[448,128]{1,0:T(8,128)(2,1)S(1)}, u32[]{:S(2)}, u32[]{:S(2)}) %collective-permute-start.4) | collective-permute-done | bytes 114720 | tf_op jit(solution)/shard_map/ppermute | solution.py:402
  32.1 4.1 %collective-permute-done.5 = bf16[1,2,448,128]{3,2,0,1:T(8,128)(2,1)S(1)} collective-permute-done((bf16[1,2,448,128]{3,2,0,1:T(8,128)(2,1)S(1)}, bf16[1,2,448,128]{3,2,0,1:T(8,128)(2,1)S(1)}, u32[]{:S(2)}, u32[]{:S(2)}) %collective-permute-start.5) | collective-permute-done | bytes 229408 | tf_op jit(solution)/shard_map/ppermute | solution.py:402
  37.3 9.6 %collective-permute-done.8 = bf16[2,448,128]{2,1,0:T(8,128)(2,1)S(1)} collective-permute-done((bf16[2,448,128]{2,1,0:T(8,128)(2,1)S(1)}, bf16[2,448,128]{2,1,0:T(8,128)(2,1)S(1)}, u32[]{:S(2)}, u32[]{:S(2)}) %collective-permute-start.8) | collective-permute-done | bytes 229408 | tf_op jit(solution)/shard_map/ppermute | solution.py:402
  50.0 3.7 %attention_forward.2 = (f32[416,384]{1,0:T(8,128)S(1)}, bf16[384,1152]{1,0:T(8,128)(2,1)S(1)}, bf16[384,384]{1,0:T(8,128)(2,1)S(1)}, f32[8,384]{1,0:T(8,128)S(1)...) custom-call(s32[16]{0:T(128)S(1)} %get-tuple-element.145.place.place, ...), custom_call_target="tpu_custom_call" | custom-call | flops 623640576 | bytes 7243328 | tf_op jit(solution)/shard_map/attention_forward/pallas_call | solution.py:381
  53.7 6.8 %collective-permute-done.11 = bf16[4,448,128]{2,1,0:T(8,128)(2,1)S(1)} collective-permute-done((bf16[4,448,128]{2,1,0:T(8,128)(2,1)S(1)}, bf16[4,448,128]{2,1,0:T(8,128)(2,1)S(1)}, u32[]{:S(2)}, u32[]{:S(2)}) %collective-permute-start.11) | collective-permute-done | bytes 458784 | tf_op jit(solution)/shard_map/ppermute | solution.py:402
  61.7 4.3 %mlp_forward.2 = (bf16[384,1536]{1,0:T(8,128)(2,1)S(1)}, bf16[1536,384]{1,0:T(8,128)(2,1)S(1)}, f32[8,384]{1,0:T(8,128)S(1)}, bf16[416,384]{1,0:T(8,128)(2,1)S(1...) custom-call(s32[16]{0:T(128)S(1)} %get-tuple-element.145.place.place_low, ...), custom_call_target="tpu_custom_call" | custom-call | flops 981467136 | bytes 10195072 | tf_op jit(solution)/shard_map/mlp_forward/pallas_call | solution.py:381
  66.1 3.7 %attention_forward.3 = (bf16[384,1152]{1,0:T(8,128)(2,1)S(1)}, bf16[384,384]{1,0:T(8,128)(2,1)S(1)}, f32[8,384]{1,0:T(8,128)S(1)}, bf16[416,384]{1,0:T(8,128)(2,...) custom-call(s32[16]{0:T(128)S(1)} %get-tuple-element.145.place.place, ...), custom_call_target="tpu_custom_call" | custom-call | flops 623640576 | bytes 6940736 | tf_op jit(solution)/shard_map/attention_forward/pallas_call | solution.py:381
  69.8 4.5 %mlp_forward.3 = (bf16[384,1536]{1,0:T(8,128)(2,1)S(1)}, bf16[1536,384]{1,0:T(8,128)(2,1)S(1)}, f32[8,384]{1,0:T(8,128)S(1)}, bf16[416,384]{1,0:T(8,128)(2,1)S(1...) custom-call(s32[16]{0:T(128)S(1)} %get-tuple-element.145.place.place_low, ...), custom_call_target="tpu_custom_call" | custom-call | flops 981467136 | bytes 10161280 | tf_op jit(solution)/shard_map/mlp_forward/pallas_call | solution.py:381
  74.2 4.7 %mlp_backward.2 = (f32[2336,128]{1,0:T(8,128)S(1)}, bf16[2,4,448,128]{3,2,1,0:T(8,128)(2,1)S(1)}, bf16[2,4,448,128]{3,2,1,0:T(8,128)(2,1)S(1)}, f32[416,384]{1,0:T(8,128)S(1)}) custom-call(s32[2]{0:T(128)S(1)} %copy-done, s32[8]{0:T(128)S(1)} %get-tuple-element.143.refs_1_.refs_0_, s32[8]{0:T(128)S(1)} %get-tuple-element.144.refs_2_.refs_1_, ...), custom_call_target="tpu_custom_call" | custom-call | flops 1962934272 | bytes 9858632 | tf_op jit(solution)/shard_map/mlp_backward/pallas_call | solution.py:381
  79.0 5.5 %attention_backward.2 = (bf16[416,1152]{1,0:T(8,128)(2,1)S(1)}, f32[384,384]{1,0:T(8,128)S(1)}, f32[8,384]{1,0:T(8,128)S(1)}) custom-call(f32[416,384]{1,0:T(8,128)S(1)} %get-tuple-element.175.g_hidden.refs_2_, bf16[384,384]{1,0:T(8,128)(2,1)S(1)} %get-tuple-element.176.w_out, bf16[416,1152]{1,0:T(8,128)(2,1)S(1)} %get-tuple-element.177.qkv, ...), custom_call_target="tpu_custom_call" | custom-call | flops 511180800 | bytes 4810752 | tf_op jit(solution)/shard_map/attention_backward/pallas_call | solution.py:381
  84.7 3.1 %projection_backward.2 = (bf16[2,4,448,128]{3,2,1,0:T(8,128)(2,1)S(1)}, bf16[2,4,448,128]{3,2,1,0:T(8,128)(2,1)S(1)}, f32[416,384]{1,0:T(8,128)S(1)}) custom-call(s32[8]{0:T(128)S(1)} %get-tuple-element.143.refs_1_.refs_0_, s32[8]{0:T(128)S(1)} %get-tuple-element.144.refs_2_.refs_1_, f32[416,384]{1,0:T(8,128)S(1)} %get-tuple-element.175.g_hidden.refs_2_, ...), custom_call_target="tpu_custom_call" | custom-call | flops 736100352 | bytes 7725120 | tf_op jit(solution)/shard_map/projection_backward/pallas_call | solution.py:381
  91.8 4.7 %mlp_backward.3 = (f32[2336,128]{1,0:T(8,128)S(1)}, bf16[2,4,448,128]{3,2,1,0:T(8,128)(2,1)S(1)}, bf16[2,4,448,128]{3,2,1,0:T(8,128)(2,1)S(1)}, f32[416,384]{1,0:T(8,128)S(1)}) custom-call(s32[8]{0:T(128)S(1)} %get-tuple-element.143.refs_1_.refs_0_, s32[8]{0:T(128)S(1)} %get-tuple-element.144.refs_2_.refs_1_, f32[416,384]{1,0:T(8,128)S(1)} %get-tuple-element.196.refs_2_, ...), custom_call_target="tpu_custom_call" | custom-call | flops 1962934272 | bytes 10195008 | tf_op jit(solution)/shard_map/mlp_backward/pallas_call | solution.py:381
  102.4 5.5 %attention_backward.3 = (bf16[416,1152]{1,0:T(8,128)(2,1)S(1)}, f32[384,384]{1,0:T(8,128)S(1)}, f32[8,384]{1,0:T(8,128)S(1)}) custom-call(f32[416,384]{1,0:T(8,128)S(1)} %get-tuple-element.214.g_hidden.refs_2_, bf16[384,384]{1,0:T(8,128)(2,1)S(1)} %get-tuple-element.215.w_out, bf16[416,1152]{1,0:T(8,128)(2,1)S(1)} %get-tuple-element.216.qkv, ...), custom_call_target="tpu_custom_call" | custom-call | flops 511180800 | bytes 4810752 | tf_op jit(solution)/shard_map/attention_backward/pallas_call | solution.py:381
  112.8 3.1 %projection_backward.3 = (bf16[2,4,448,128]{3,2,1,0:T(8,128)(2,1)S(1)}, bf16[2,4,448,128]{3,2,1,0:T(8,128)(2,1)S(1)}, f32[2,197,384]{2,1,0:T(8,128)S(1)}) custom-call(s32[8]{0:T(128)S(1)} %get-tuple-element.143.refs_1_.refs_0_, s32[8]{0:T(128)S(1)} %get-tuple-element.144.refs_2_.refs_1_, f32[416,384]{1,0:T(8,128)S(1)} %get-tuple-element.214.g_hidden.refs_2_, ...), custom_call_target="tpu_custom_call" | custom-call | flops 736100352 | bytes 7691328 | tf_op jit(solution)/shard_map/projection_backward/pallas_call | solution.py:381
  123.1 6.2 %collective-permute-done.31 = bf16[1,448,128]{2,1,0:T(8,128)(2,1)S(1)} collective-permute-done((bf16[1,448,128]{2,1,0:T(8,128)(2,1)S(1)}, bf16[1,448,128]{2,1,0:T(8,128)(2,1)S(1)}, u32[]{:S(2)}, u32[]{:S(2)}) %collective-permute-start.31) | collective-permute-done | bytes 114720 | tf_op jit(solution)/shard_map/ppermute | solution.py:402
  131.9 2.4 %collective-permute-done.36 = bf16[1,448,128]{2,1,0:T(8,128)(2,1)S(1)} collective-permute-done((bf16[1,448,128]{2,1,0:T(8,128)(2,1)S(1)}, bf16[1,448,128]{2,1,0:T(8,128)(2,1)S(1)}, u32[]{:S(2)}, u32[]{:S(2)}) %collective-permute-start.36) | collective-permute-done | bytes 114720 | tf_op jit(solution)/shard_map/ppermute | solution.py:402
  137.9 3.6 %collective-permute-start.38 = (bf16[448,128]{1,0:T(8,128)(2,1)S(1)}, bf16[448,128]{1,0:T(8,128)(2,1)S(1)}, u32[]{:S(2)}, u32[]{:S(2)}) collective-permute-start(bf16[448,128]{1,0:T(8,128)(2,1)S(1)} %get-tuple-element.336), channel_id=1, source_target_pairs={{0,16},{1,17},{2,18},{3,19},{4,20},{5,21},{6,22},{7,23},{8,24},{9,... | collective-permute-start | bytes 344072 | tf_op jit(solution)/shard_map/ppermute | solution.py:402
  141.6 3.4 %collective-permute-done.38 = bf16[448,128]{1,0:T(8,128)(2,1)S(1)} collective-permute-done((bf16[448,128]{1,0:T(8,128)(2,1)S(1)}, bf16[448,128]{1,0:T(8,128)(2,1)S(1)}, u32[]{:S(2)}, u32[]{:S(2)}) %collective-permute-start.38) | collective-permute-done | bytes 114720 | tf_op jit(solution)/shard_map/ppermute | solution.py:402
  145.1 2.4 %collective-permute-start.39 = (bf16[448,128]{1,0:T(8,128)(2,1)S(1)}, bf16[448,128]{1,0:T(8,128)(2,1)S(1)}, u32[]{:S(2)}, u32[]{:S(2)}) collective-permute-start(bf16[448,128]{1,0:T(8,128)(2,1)S(1)} %get-tuple-element.334), channel_id=1, source_target_pairs={{0,16},{1,17},{2,18},{3,19},{4,20},{5,21},{6,22},{7,23},{8,24},{9,... | collective-permute-start | bytes 344072 | tf_op jit(solution)/shard_map/ppermute | solution.py:402
  151.3 2.8 %multiply_subtract_fusion = (f32[2,55552]{1,0:T(2,128)}, f32[2,55552]{1,0:T(2,128)}, f32[2,55552]{1,0:T(2,128)}) fusion(f32[2,55552]{1,0:T(2,128)S(1)} %copy-done.1, f32[55552]{0:T(1024)S(1)} %broadcast_select_fusion.8, f32[55552]{0:T(1024)S(1)} %get-tuple-element.292, f32[1,55552]{1,0:T(1,128)S(1)} %bitcast.81, f32[1,55552]{1,0:T(1,128)S(1)} %bitcast.82, ...), kind=kLoop, calls=%fused_computation.49 | loop fusion | flops 1777664 | bytes 3555328 | tf_op jit(solution)/shard_map/sub | solution.py:645
  (163 shorter events, 45.0 us)
Async XLA Ops:
  2.5 9.7 %collective-permute-start = (bf16[448,128]{1,0:T(8,128)(2,1)S(1)}, bf16[448,128]{1,0:T(8,128)(2,1)S(1)}, u32[]{:S(2)}, u32[]{:S(2)}) collective-permute-start(bf16[448,128]{1,0:T(8,128)(2,1)S(1)} %get-tuple-element.358), channel_id=1, source_target_pairs={{0,16},{1,17},{2,18},{3,19},{4,20},{5,21},{6,22},{7,23},{8,24},{9,... | collective-permute-start | bytes 344072 | tf_op jit(solution)/shard_map/ppermute | solution.py:402
  19.2 10.9 %collective-permute-start.2 = (bf16[2,448,128]{2,1,0:T(8,128)(2,1)S(1)}, bf16[2,448,128]{2,1,0:T(8,128)(2,1)S(1)}, u32[]{:S(2)}, u32[]{:S(2)}) collective-permute-start(bf16[2,448,128]{2,1,0:T(8,128)(2,1)S(1)} %get-tuple-element.331), channel_id=1, source_target_pairs={{0,2},{1,3},{2,0},{3,1},{4,6},{5,7},{6,4},{7,5},{8,10},{9,11},{10,... | collective-permute-start | bytes 688136 | tf_op jit(solution)/shard_map/ppermute | solution.py:402
  20.5 9.6 %collective-permute-start.3 = (bf16[2,448,128]{2,1,0:T(8,128)(2,1)S(1)}, bf16[2,448,128]{2,1,0:T(8,128)(2,1)S(1)}, u32[]{:S(2)}, u32[]{:S(2)}) collective-permute-start(bf16[2,448,128]{2,1,0:T(8,128)(2,1)S(1)} %get-tuple-element.330), channel_id=1, source_target_pairs={{0,4},{1,5},{2,6},{3,7},{4,0},{5,1},{6,2},{7,3},{8,12},{9,13},{10,... | collective-permute-start | bytes 688136 | tf_op jit(solution)/shard_map/ppermute | solution.py:402
  22.0 8.0 %collective-permute-start.4 = (bf16[448,128]{1,0:T(8,128)(2,1)S(1)}, bf16[448,128]{1,0:T(8,128)(2,1)S(1)}, u32[]{:S(2)}, u32[]{:S(2)}) collective-permute-start(bf16[448,128]{1,0:T(8,128)(2,1)S(1)} %get-tuple-element.148), channel_id=1, source_target_pairs={{0,16},{1,17},{2,18},{3,19},{4,20},{5,21},{6,22},{7,23},{8,24},{9,... | collective-permute-start | bytes 344072 | tf_op jit(solution)/shard_map/ppermute | solution.py:402
  30.9 16.4 %collective-permute-start.7 = (bf16[4,448,128]{2,1,0:T(8,128)(2,1)S(1)}, bf16[4,448,128]{2,1,0:T(8,128)(2,1)S(1)}, u32[]{:S(2)}, u32[]{:S(2)}) collective-permute-start(bf16[4,448,128]{2,1,0:T(8,128)(2,1)S(1)} %pad_maximum_fusion.5), channel_id=1, source_target_pairs={{0,2},{1,3},{2,0},{3,1},{4,6},{5,7},{6,4},{7,5},{8,10},{9,11},{10,... | collective-permute-start | bytes 1376264 | tf_op jit(solution)/shard_map/ppermute | solution.py:402
  31.5 15.7 %collective-permute-start.6 = (bf16[4,448,128]{2,1,0:T(8,128)(2,1)S(1)}, bf16[4,448,128]{2,1,0:T(8,128)(2,1)S(1)}, u32[]{:S(2)}, u32[]{:S(2)}) collective-permute-start(bf16[4,448,128]{2,1,0:T(8,128)(2,1)S(1)} %pad_maximum_fusion.4), channel_id=1, source_target_pairs={{0,4},{1,5},{2,6},{3,7},{4,0},{5,1},{6,2},{7,3},{8,12},{9,13},{10,... | collective-permute-start | bytes 1376264 | tf_op jit(solution)/shard_map/ppermute | solution.py:402
  36.2 10.7 %collective-permute-start.8 = (bf16[2,448,128]{2,1,0:T(8,128)(2,1)S(1)}, bf16[2,448,128]{2,1,0:T(8,128)(2,1)S(1)}, u32[]{:S(2)}, u32[]{:S(2)}) collective-permute-start(bf16[2,448,128]{2,1,0:T(8,128)(2,1)S(1)} %get-tuple-element.329), channel_id=1, source_target_pairs={{0,2},{1,3},{2,0},{3,1},{4,6},{5,7},{6,4},{7,5},{8,10},{9,11},{10,... | collective-permute-start | bytes 688136 | tf_op jit(solution)/shard_map/ppermute | solution.py:402
  36.8 10.4 %collective-permute-start.9 = (bf16[2,448,128]{2,1,0:T(8,128)(2,1)S(1)}, bf16[2,448,128]{2,1,0:T(8,128)(2,1)S(1)}, u32[]{:S(2)}, u32[]{:S(2)}) collective-permute-start(bf16[2,448,128]{2,1,0:T(8,128)(2,1)S(1)} %get-tuple-element.328), channel_id=1, source_target_pairs={{0,4},{1,5},{2,6},{3,7},{4,0},{5,1},{6,2},{7,3},{8,12},{9,13},{10,... | collective-permute-start | bytes 688136 | tf_op jit(solution)/shard_map/ppermute | solution.py:402
  47.5 13.0 %collective-permute-start.11 = (bf16[4,448,128]{2,1,0:T(8,128)(2,1)S(1)}, bf16[4,448,128]{2,1,0:T(8,128)(2,1)S(1)}, u32[]{:S(2)}, u32[]{:S(2)}) collective-permute-start(bf16[4,448,128]{2,1,0:T(8,128)(2,1)S(1)} %pad_maximum_fusion.6), channel_id=1, source_target_pairs={{0,4},{1,5},{2,6},{3,7},{4,0},{5,1},{6,2},{7,3},{8,12},{9,13},{10,... | collective-permute-start | bytes 1376264 | tf_op jit(solution)/shard_map/ppermute | solution.py:402
  48.1 12.7 %collective-permute-start.12 = (bf16[4,448,128]{2,1,0:T(8,128)(2,1)S(1)}, bf16[4,448,128]{2,1,0:T(8,128)(2,1)S(1)}, u32[]{:S(2)}, u32[]{:S(2)}) collective-permute-start(bf16[4,448,128]{2,1,0:T(8,128)(2,1)S(1)} %pad_maximum_fusion.7), channel_id=1, source_target_pairs={{0,2},{1,3},{2,0},{3,1},{4,6},{5,7},{6,4},{7,5},{8,10},{9,11},{10,... | collective-permute-start | bytes 1376264 | tf_op jit(solution)/shard_map/ppermute | solution.py:402
  49.9 11.8 %collective-permute-start.13 = (bf16[8,448,128]{2,1,0:T(8,128)(2,1)S(1)}, bf16[8,448,128]{2,1,0:T(8,128)(2,1)S(1)}, u32[]{:S(2)}, u32[]{:S(2)}) collective-permute-start(bf16[8,448,128]{2,1,0:T(8,128)(2,1)S(1)} %pad_maximum_fusion.2.near), channel_id=1, source_target_pairs={{0,1},{1,0},{2,3},{3,2},{4,5},{5,4},{6,7},{7,6},{8,9},{9,8},{10,11... | collective-permute-start | bytes 2752520 | tf_op jit(solution)/shard_map/ppermute | solution.py:402
  87.7 8.9 %collective-permute-start.19 = (bf16[2,4,448,128]{3,2,1,0:T(8,128)(2,1)S(1)}, bf16[2,4,448,128]{3,2,1,0:T(8,128)(2,1)S(1)}, u32[]{:S(2)}, u32[]{:S(2)}) collective-permute-start(bf16[2,4,448,128]{3,2,1,0:T(8,128)(2,1)S(1)} %get-tuple-element.195), channel_id=1, source_target_pairs={{0,1},{1,0},{2,3},{3,2},{4,5},{5,4},{6,7},{7,6},{8,9},{9,8},{10,11... | collective-permute-start | bytes 2752520 | tf_op jit(solution)/shard_map/ppermute | solution.py:402
  88.5 8.3 %collective-permute-start.18 = (bf16[2,448,128]{2,1,0:T(8,128)(2,1)S(1)}, bf16[2,448,128]{2,1,0:T(8,128)(2,1)S(1)}, u32[]{:S(2)}, u32[]{:S(2)}) collective-permute-start(bf16[2,448,128]{2,1,0:T(8,128)(2,1)S(1)} %get-tuple-element.324), channel_id=1, source_target_pairs={{0,2},{1,3},{2,0},{3,1},{4,6},{5,7},{6,4},{7,5},{8,10},{9,11},{10,... | collective-permute-start | bytes 688136 | tf_op jit(solution)/shard_map/ppermute | solution.py:402
  90.2 7.3 %collective-permute-start.17 = (bf16[2,448,128]{2,1,0:T(8,128)(2,1)S(1)}, bf16[2,448,128]{2,1,0:T(8,128)(2,1)S(1)}, u32[]{:S(2)}, u32[]{:S(2)}) collective-permute-start(bf16[2,448,128]{2,1,0:T(8,128)(2,1)S(1)} %get-tuple-element.326), channel_id=1, source_target_pairs={{0,4},{1,5},{2,6},{3,7},{4,0},{5,1},{6,2},{7,3},{8,12},{9,13},{10,... | collective-permute-start | bytes 688136 | tf_op jit(solution)/shard_map/ppermute | solution.py:402
  97.7 10.3 %collective-permute-start.23 = (bf16[2,448,128]{2,1,0:T(8,128)(2,1)S(1)}, bf16[2,448,128]{2,1,0:T(8,128)(2,1)S(1)}, u32[]{:S(2)}, u32[]{:S(2)}) collective-permute-start(bf16[2,448,128]{2,1,0:T(8,128)(2,1)S(1)} %get-tuple-element.320), channel_id=1, source_target_pairs={{0,2},{1,3},{2,0},{3,1},{4,6},{5,7},{6,4},{7,5},{8,10},{9,11},{10,... | collective-permute-start | bytes 688136 | tf_op jit(solution)/shard_map/ppermute | solution.py:402
  98.4 9.5 %collective-permute-start.22 = (bf16[2,448,128]{2,1,0:T(8,128)(2,1)S(1)}, bf16[2,448,128]{2,1,0:T(8,128)(2,1)S(1)}, u32[]{:S(2)}, u32[]{:S(2)}) collective-permute-start(bf16[2,448,128]{2,1,0:T(8,128)(2,1)S(1)} %get-tuple-element.322), channel_id=1, source_target_pairs={{0,4},{1,5},{2,6},{3,7},{4,0},{5,1},{6,2},{7,3},{8,12},{9,13},{10,... | collective-permute-start | bytes 688136 | tf_op jit(solution)/shard_map/ppermute | solution.py:402
  100.1 7.8 %collective-permute-start.21 = (bf16[1,448,128]{2,1,0:T(8,128)(2,1)S(1)}, bf16[1,448,128]{2,1,0:T(8,128)(2,1)S(1)}, u32[]{:S(2)}, u32[]{:S(2)}) collective-permute-start(bf16[1,448,128]{2,1,0:T(8,128)(2,1)S(1)} %get-tuple-element.352), channel_id=1, source_target_pairs={{0,4},{1,5},{2,6},{3,7},{4,0},{5,1},{6,2},{7,3},{8,12},{9,13},{10,... | collective-permute-start | bytes 344072 | tf_op jit(solution)/shard_map/ppermute | solution.py:402
  100.8 7.2 %collective-permute-start.20 = (bf16[1,448,128]{2,1,0:T(8,128)(2,1)S(1)}, bf16[1,448,128]{2,1,0:T(8,128)(2,1)S(1)}, u32[]{:S(2)}, u32[]{:S(2)}) collective-permute-start(bf16[1,448,128]{2,1,0:T(8,128)(2,1)S(1)} %get-tuple-element.354), channel_id=1, source_target_pairs={{0,2},{1,3},{2,0},{3,1},{4,6},{5,7},{6,4},{7,5},{8,10},{9,11},{10,... | collective-permute-start | bytes 344072 | tf_op jit(solution)/shard_map/ppermute | solution.py:402
  108.1 7.9 %collective-permute-start.26 = (bf16[1,448,128]{2,1,0:T(8,128)(2,1)S(1)}, bf16[1,448,128]{2,1,0:T(8,128)(2,1)S(1)}, u32[]{:S(2)}, u32[]{:S(2)}) collective-permute-start(bf16[1,448,128]{2,1,0:T(8,128)(2,1)S(1)} %get-tuple-element.348), channel_id=1, source_target_pairs={{0,4},{1,5},{2,6},{3,7},{4,0},{5,1},{6,2},{7,3},{8,12},{9,13},{10,... | collective-permute-start | bytes 344072 | tf_op jit(solution)/shard_map/ppermute | solution.py:402
  119.2 10.1 %collective-permute-start.29 = (bf16[2,448,128]{2,1,0:T(8,128)(2,1)S(1)}, bf16[2,448,128]{2,1,0:T(8,128)(2,1)S(1)}, u32[]{:S(2)}, u32[]{:S(2)}) collective-permute-start(bf16[2,448,128]{2,1,0:T(8,128)(2,1)S(1)} %get-tuple-element.316), channel_id=1, source_target_pairs={{0,2},{1,3},{2,0},{3,1},{4,6},{5,7},{6,4},{7,5},{8,10},{9,11},{10,... | collective-permute-start | bytes 688136 | tf_op jit(solution)/shard_map/ppermute | solution.py:402
  120.9 8.5 %collective-permute-start.28 = (bf16[2,448,128]{2,1,0:T(8,128)(2,1)S(1)}, bf16[2,448,128]{2,1,0:T(8,128)(2,1)S(1)}, u32[]{:S(2)}, u32[]{:S(2)}) collective-permute-start(bf16[2,448,128]{2,1,0:T(8,128)(2,1)S(1)} %get-tuple-element.318), channel_id=1, source_target_pairs={{0,4},{1,5},{2,6},{3,7},{4,0},{5,1},{6,2},{7,3},{8,12},{9,13},{10,... | collective-permute-start | bytes 688136 | tf_op jit(solution)/shard_map/ppermute | solution.py:402
  121.6 7.7 %collective-permute-start.31 = (bf16[1,448,128]{2,1,0:T(8,128)(2,1)S(1)}, bf16[1,448,128]{2,1,0:T(8,128)(2,1)S(1)}, u32[]{:S(2)}, u32[]{:S(2)}) collective-permute-start(bf16[1,448,128]{2,1,0:T(8,128)(2,1)S(1)} %get-tuple-element.346), channel_id=1, source_target_pairs={{0,2},{1,3},{2,0},{3,1},{4,6},{5,7},{6,4},{7,5},{8,10},{9,11},{10,... | collective-permute-start | bytes 344072 | tf_op jit(solution)/shard_map/ppermute | solution.py:402
  136.1 8.9 %collective-permute-start.37 = (bf16[2,448,128]{2,1,0:T(8,128)(2,1)S(1)}, bf16[2,448,128]{2,1,0:T(8,128)(2,1)S(1)}, u32[]{:S(2)}, u32[]{:S(2)}) collective-permute-start(bf16[2,448,128]{2,1,0:T(8,128)(2,1)S(1)} %pad_maximum_fusion.14), channel_id=1, source_target_pairs={{0,8},{1,9},{2,10},{3,11},{4,12},{5,13},{6,14},{7,15},{8,0},{9,1},... | collective-permute-start | bytes 688136 | tf_op jit(solution)/shard_map/ppermute | solution.py:402
  137.9 7.1 %collective-permute-start.38 = (bf16[448,128]{1,0:T(8,128)(2,1)S(1)}, bf16[448,128]{1,0:T(8,128)(2,1)S(1)}, u32[]{:S(2)}, u32[]{:S(2)}) collective-permute-start(bf16[448,128]{1,0:T(8,128)(2,1)S(1)} %get-tuple-element.336), channel_id=1, source_target_pairs={{0,16},{1,17},{2,18},{3,19},{4,20},{5,21},{6,22},{7,23},{8,24},{9,... | collective-permute-start | bytes 344072 | tf_op jit(solution)/shard_map/ppermute | solution.py:402
  (22 other events, 104.0 us)
where the time goes:
time: 154 us
  waiting for transfers between devices  53.7 us (35%)
  starting transfers between devices  45.2 us (29%)
  Pallas kernels  42.6 us (28%)
  other arithmetic  7.13 us (5%)
  local copies, waits for them, and re-layouts  4.08 us (3%)
    ppermute x40, waiting for transfers between devices, swap(): return lax.ppermute(values, 'dp', [(i, i ^ mask) for i in range(size)])  53.7 us
    ppermute x40, starting transfers between devices, swap(): return lax.ppermute(values, 'dp', [(i, i ^ mask) for i in range(size)])  45.2 us
    pallas_call x10, Pallas kernels, call(): pl.pallas_call(body, name=name, out_shape=shapes, in_specs=in_specs, out_...  42.6 us
  transfers between devices with their start and end apart: 40, of which 15 were waited for; matrix products, arithmetic and copies ran while one was open for 4% of the time, Pallas kernels for 17%

commit v1 on v0

--- a/solution.py
+++ b/solution.py
@@ -156,24 +156,31 @@
     return rows, cols
 
 
-def unpack(rows_each, base, chunks, place, near, far, flat):
-    count, padded = near.shape[0], near.shape[1]
-
+def unpack(rows_each, base, chunks, parts, flat):
     def step(chunk, carry):
-        at = place[chunk]
-        own = lax.rem(at, count)
-        rows = jnp.where(at < count, near[own].astype(f32), far[own].astype(f32))
-        flat[pl.ds((chunks[2] + chunk) * rows_each - base, padded), :] = rows
+        begin = (chunks[2] + chunk) * rows_each - base
+        for place, near, far in parts:
+            count, padded = near.shape[0], near.shape[1]
+            at = place[chunk]
+            own = lax.rem(at, count)
+            rows = jnp.where(at < count, near[own].astype(f32), far[own].astype(f32))
+            flat[pl.ds(begin, padded), :] = rows
+            begin = begin + padded
         return carry
 
     lax.fori_loop(chunks[0], chunks[1], step, 0)
 
 
-def attention_forward(rows_each, first, place, near, far, state, *refs):
+def parts_of(places, refs):
+    return [(place, refs[2 * i], refs[2 * i + 1]) for i, place in enumerate(places)], refs[2 * len(places) :]
+
+
+def attention_forward(rows_each, first, count, *refs):
+    parts, (state, *refs) = parts_of(refs[:count], refs[count:])
     if first:
         kept_state, refs = refs[0], refs[1:]
     w_qkv, w_out, vectors, normed_one, qkv, probs, mixed, hidden, flat = refs
-    unpack(rows_each, 0, (0, -(-MLP_ROW // rows_each), 0), place, near, far, flat)
+    unpack(rows_each, 0, (0, -(-MLP_ROW // rows_each), 0), parts, flat)
     read_matrix(flat, ROW["w_qkv"], w_qkv, D, 3 * D)
     read_matrix(flat, ROW["w_attn_out"], w_out, D, D)
     labels = ["ln1_gain", "ln1_shift", "bias_query", "bias_value", "bias_attn_out"]
@@ -218,13 +225,15 @@
     hidden[...] = x + dot_nn(mixed[...], w_out[...]) + vectors[4:5, :]
 
 
-def mlp_forward(rows_each, last, place_low, place_high, low_near, low_far, near, far, hidden, *refs):
+def mlp_forward(rows_each, last, half, count, *refs):
+    low_places, high_places, refs = refs[:count], refs[count : 2 * count], refs[2 * count :]
+    low, refs = parts_of(low_places, refs)
+    high, (hidden, *refs) = parts_of(high_places, refs)
     w_lift, w_drop, vectors, normed_two, active, slope, result, flat = refs
-    count = 2 * near.shape[0]
     begin = MLP_ROW // rows_each
     base = begin * rows_each
-    unpack(rows_each, base, (begin, count, 0), place_low, low_near, low_far, flat)
-    unpack(rows_each, base, (0, count, count), place_high, near, far, flat)
+    unpack(rows_each, base, (begin, half, 0), low, flat)
+    unpack(rows_each, base, (0, half, half), high, flat)
     read_matrix(flat, ROW["w_lift"] - base, w_lift, D, FF)
     read_matrix(flat, ROW["w_drop"] - base, w_drop, FF, D)
     for at, label in enumerate(["ln2_gain", "ln2_shift", "bias_drop"]):
@@ -434,12 +443,13 @@
     chain = [1 << bit for bit in range(bits - 2, 2, -1)]
     planes = [(2, 4), (4, 2)]
     place_low, place_high = [places(me, size, chain + [mask, 6 - mask, 1]) for mask in planes[0]]
+    place_wide = places(me, size, [2, 4] + chain + [1])
     place = [places(me, size // 2, chain[1:] + [mask, 6 - mask, 1]) for mask in planes[0]]
 
     is_low, is_first = (me >> (bits - 1)) & 1 == 0, (me >> (bits - 2)) & 1 == 0
     flags = matrix_flags(me * width + jnp.arange(width, dtype=jnp.int32)).astype(f32)
-    early = together(params, is_low, is_first, flags, place_low, place_high, *place)
-    params, is_low, is_first, flags, place_low, place_high, *place = early
+    early = together(params, is_low, is_first, flags, place_low, place_high, place_wide, *place)
+    params, is_low, is_first, flags, place_low, place_high, place_wide, *place = early
     compact = params.astype(bf16).reshape(2, rows_each, LANES)
     compact = jnp.pad(compact, ((0, 0), (0, padded - rows_each), (0, 0)))
 
@@ -449,7 +459,7 @@
     square = TOKENS * D * D
     core_flops = 2 * 2 * MICRO * HEADS * ROWS * ROWS * HEAD_DIM
 
-    def attend(first, near, far, state):
+    def attend(first, places, low, state):
         outputs = [((TOKENS, D), f32)] if first else []
         outputs += [
             ((D, 3 * D), bf16),
@@ -462,22 +472,22 @@
             ((TOKENS, D), f32),
         ]
         made = call(
-            functools.partial(attention_forward, rows_each, first),
+            functools.partial(attention_forward, rows_each, first, len(places)),
             "attention_forward",
-            [place_low, near, far, state],
+            [*places, *low, state],
             outputs,
             [low_flat],
-            scalars=1,
+            scalars=len(places),
             flops=8 * square + core_flops,
         )
         made = made if first else [state, *made]
         return made[:-1], made[-1]
 
-    def lift(last, low_near, low_far, near, far, hidden):
+    def lift(last, low_places, high_places, low, high, hidden):
         made = call(
-            functools.partial(mlp_forward, rows_each, last),
+            functools.partial(mlp_forward, rows_each, last, half, len(low_places)),
             "mlp_forward",
-            [place_low, place_high, low_near, low_far, near, far, hidden],
+            [*low_places, *high_places, *low, *high, hidden],
             [
                 ((D, FF), bf16),
                 ((FF, D), bf16),
@@ -488,7 +498,7 @@
                 ((MICRO, SEQ, D) if last else (TOKENS, D), f32),
             ],
             [high_flat],
-            scalars=2,
+            scalars=2 * len(low_places),
             flops=16 * square,
         )
         return (hidden, *made[:-1]), made[-1]
@@ -535,6 +545,9 @@
     def top_gathered(shard, other):
         return jnp.stack([jnp.where(is_low, shard, other), jnp.where(is_low, other, shard)])[None]
 
+    def exchanged(*values):
+        return [swap(value, size, bits) for value, bits in zip(values, (size // 4, size // 2, size // 4 * 3))]
+
     def moved(parts, step):
         return [swap(part, size, mask) for part, mask in zip(parts, planes[step])]
 
@@ -550,29 +563,44 @@
         chunks = jnp.concatenate([chunks, received])
         return chunks[:, 0], chunks[:, 1]
 
-    other0 = swap(compact[0], size, size // 2)
-    row1, other0 = together(compact[1], other0)
+    cut = padded - round_up(padded * 5 // 14, 16)
+    row1, wide = compact[1, :cut], compact[1, cut:][None]
+    nearby, other0, far_other0 = exchanged(compact[0], compact[0], compact[0])
+    received = swap(wide, size, 2)
+    row1, nearby, other0, far_other0, received = together(row1, nearby, other0, far_other0, received)
+    wide = jnp.concatenate([wide, received])
     other1 = swap(row1, size, size // 2)
-    half0 = halved(*chained(top_gathered(compact[0], other0)))
+    received = swap(wide, size, 4)
+    chunks0 = top_gathered(jnp.stack([compact[0], nearby]), jnp.stack([other0, far_other0]))[0]
+    half0 = chunks0[0], chunks0[1]
+    for mask in chain[1:]:
+        half0 = [jnp.concatenate([part, swap(part, size, mask)]) for part in half0]
     received0 = moved(half0, 0)
-    *received0, other1 = together(*received0, other1)
+    *received0, other1, received = together(*received0, other1, received)
+    wide = jnp.concatenate([wide, received])
     half0 = joined(half0, received0)
     received0 = moved(half0, 1)
     half1 = halved(*chained(top_gathered(row1, other1)))
     received1 = moved(half1, 0)
-    *received0, received1[0], received1[1] = together(*received0, *received1)
+    received = swap(wide, size, size // 2)
+    *received0, received1[0], received1[1], received = together(*received0, *received1, received)
     near0 = joined(half0, received0)
     far0 = [swap(part, size, 1) for part in near0]
     half1 = joined(half1, received1)
     received1 = moved(half1, 1)
-    one0, hidden = attend(True, near0[0], far0[0], images)
-    hidden, *received1 = together(hidden, *received1)
+    wide = jnp.stack([jnp.where(is_low, wide, received), jnp.where(is_low, received, wide)], axis=1)
+    wide, received = chained(wide)
+    one0, hidden = attend(True, [place_low], [near0[0], far0[0]], images)
+    hidden, *received1, received = together(hidden, *received1, received)
     near1 = joined(half1, received1)
+    near1 = [part for pair in zip(near1, halved(wide, received)) for part in pair]
     far1 = [swap(part, size, 1) for part in near1]
-    two0, state = lift(False, near0[0], far0[0], near0[1], far0[1], hidden)
+    two0, state = lift(False, [place_low], [place_high], [near0[0], far0[0]], [near0[1], far0[1]], hidden)
     state, *far1 = together(state, *far1)
-    one1, hidden = attend(False, near1[0], far1[0], state)
-    two1, outputs = lift(True, near1[0], far1[0], near1[1], far1[1], hidden)
+    both1 = [part for pair in zip(near1, far1) for part in pair]
+    low1, high1 = both1[:4], both1[4:]
+    one1, hidden = attend(False, [place_low, place_wide], low1, state)
+    two1, outputs = lift(True, [place_low, place_wide], [place_high, place_wide], low1, high1, hidden)
 
     carry_rows = round_up(half * rows_each - MLP_ROW + padded - rows_each, 8)
 
@@ -626,12 +654,14 @@
     low0 = to_plane(low0, 1)
     held, = hold(low0 + high0 + [inner1])
     low0, high0, top1 = to_plane(held[:2], 0), along(held[2:4]), to_top(added(held[4]))
-    held, *high0 = hold(low0, *high0)
-    inner0 = to_inner(along(held), high0)
-    held, outputs, input_grad = hold([inner0, top1], outputs, input_grad)
-    inner0, top1 = held
-    top0 = to_top(added(inner0))
-    sum0, sum1 = [pair[0].astype(f32) + pair[1].astype(f32) for pair in (top0, top1)]
+    held, *high0, outputs, input_grad = hold(low0, *high0, outputs, input_grad)
+    low0 = along(held)
+    here, there = [jnp.where(is_low, *pair) for pair in zip(low0, high0)], [jnp.where(is_low, *pair) for pair in zip(high0, low0)]
+    here, there = [[jnp.where(is_first, *pair), jnp.where(is_first, *pair[::-1])] for pair in (here, there)]
+    values = exchanged(here[1][0], there[0][0], there[1][0])
+    (nearby, other, far_other), received = values, top1[1]
+    sum0 = here[0][0].astype(f32) + nearby.astype(f32) + other.astype(f32) + far_other.astype(f32)
+    sum1 = top1[0].astype(f32) + received.astype(f32)
     owned = [total[:rows_each].reshape(width) for total in (sum0, sum1)]
 
     grads = jnp.stack(owned)

time: 154 us -> 145 us (0.942)
  waiting for transfers between devices: 53.7 us -> 37.1 us
  starting transfers between devices: 45.2 us -> 52.1 us
    ppermute x40 -> x48, waiting for transfers between devices: 53.7 us -> 37.1 us  [swap(): return lax.ppermute(values, 'dp', [(i, i ^ mask) for i in range(size)])]
    ppermute x40 -> x48, starting transfers between devices: 45.2 us -> 52.1 us  [swap(): return lax.ppermute(values, 'dp', [(i, i ^ mask) for i in range(size)])]
  transfers between devices with their start and end apart: 40 -> 48, of which waited for: 15 -> 18; matrix products, arithmetic and copies ran while one was open for 4% -> 4% of each run, Pallas kernels for 17% -> 18%
where the time goes in v1:
time: 145 us
  starting transfers between devices  52.1 us (36%)
  Pallas kernels  42.7 us (29%)
  waiting for transfers between devices  37.1 us (26%)
  other arithmetic  7.12 us (5%)
  local copies, waits for them, and re-layouts  4.13 us (3%)
  between operations  1.48 us (1%)
    ppermute x48, starting transfers between devices, swap(): return lax.ppermute(values, 'dp', [(i, i ^ mask) for i in range(size)])  52.1 us
    pallas_call x10, Pallas kernels, call(): pl.pallas_call(body, name=name, out_shape=shapes, in_specs=in_specs, out_...  42.7 us
    ppermute x48, waiting for transfers between devices, swap(): return lax.ppermute(values, 'dp', [(i, i ^ mask) for i in range(size)])  37.1 us
  transfers between devices with their start and end apart: 48, of which 18 were waited for; matrix products, arithmetic and copies ran while one was open for 4% of the time, Pallas kernels for 18%

profile of v1, /device:TPU:0, one launch (start us, length us, event | category | flops | bytes accessed | tf_op | source)
XLA Modules:
  0.0 144.6 jit_solution(665984252465161501)
XLA Ops:
  2.5 3.1 %collective-permute-start = (bf16[448,128]{1,0:T(8,128)(2,1)S(1)}, bf16[448,128]{1,0:T(8,128)(2,1)S(1)}, u32[]{:S(2)}, u32[]{:S(2)}) collective-permute-start(bf16[448,128]{1,0:T(8,128)(2,1)S(1)} %get-tuple-element.372), channel_id=1, source_target_pairs={{0,8},{1,9},{2,10},{3,11},{4,12},{5,13},{6,14},{7,15},{8,0},{9,1},... | collective-permute-start | bytes 344072 | tf_op jit(solution)/shard_map/ppermute | solution.py:411
  5.6 2.6 %collective-permute-start.1 = (bf16[448,128]{1,0:T(8,128)(2,1)S(1)}, bf16[448,128]{1,0:T(8,128)(2,1)S(1)}, u32[]{:S(2)}, u32[]{:S(2)}) collective-permute-start(bf16[448,128]{1,0:T(8,128)(2,1)S(1)} %get-tuple-element.372), channel_id=1, source_target_pairs={{0,16},{1,17},{2,18},{3,19},{4,20},{5,21},{6,22},{7,23},{8,24},{9,... | collective-permute-start | bytes 344072 | tf_op jit(solution)/shard_map/ppermute | solution.py:411
  9.9 2.4 %collective-permute-done.3 = bf16[1,160,128]{2,1,0:T(8,128)(2,1)S(1)} collective-permute-done((bf16[1,160,128]{2,1,0:T(8,128)(2,1)S(1)}, bf16[1,160,128]{2,1,0:T(8,128)(2,1)S(1)}, u32[]{:S(2)}, u32[]{:S(2)}) %collective-permute-start.3) | collective-permute-done | bytes 40992 | tf_op jit(solution)/shard_map/ppermute | solution.py:411
  12.3 5.0 %collective-permute-done.1 = bf16[448,128]{1,0:T(8,128)(2,1)S(1)} collective-permute-done((bf16[448,128]{1,0:T(8,128)(2,1)S(1)}, bf16[448,128]{1,0:T(8,128)(2,1)S(1)}, u32[]{:S(2)}, u32[]{:S(2)}) %collective-permute-start.1) | collective-permute-done | bytes 114720 | tf_op jit(solution)/shard_map/ppermute | solution.py:411
  21.0 2.8 %collective-permute-start.6 = (bf16[288,128]{1,0:T(8,128)(2,1)S(1)}, bf16[288,128]{1,0:T(8,128)(2,1)S(1)}, u32[]{:S(2)}, u32[]{:S(2)}) collective-permute-start(bf16[288,128]{1,0:T(8,128)(2,1)S(1)} %slice_bitcast_fusion.18), channel_id=1, source_target_pairs={{0,16},{1,17},{2,18},{3,19},{4,20},{5,21},{6,22},{7,23},{8,24},{9,... | collective-permute-start | bytes 221192 | tf_op jit(solution)/shard_map/ppermute | solution.py:411
  23.8 2.5 %collective-permute-done.6 = bf16[288,128]{1,0:T(8,128)(2,1)S(1)} collective-permute-done((bf16[288,128]{1,0:T(8,128)(2,1)S(1)}, bf16[288,128]{1,0:T(8,128)(2,1)S(1)}, u32[]{:S(2)}, u32[]{:S(2)}) %collective-permute-start.6) | collective-permute-done | bytes 73760 | tf_op jit(solution)/shard_map/ppermute | solution.py:411
  31.8 2.0 %collective-permute-done.8 = bf16[1,2,288,128]{3,2,0,1:T(8,128)(2,1)S(1)} collective-permute-done((bf16[1,2,288,128]{3,2,0,1:T(8,128)(2,1)S(1)}, bf16[1,2,288,128]{3,2,0,1:T(8,128)(2,1)S(1)}, u32[]{:S(2)}, u32[]{:S(2)}) %collective-permute-start.8) | collective-permute-done | bytes 147488 | tf_op jit(solution)/shard_map/ppermute | solution.py:411
  35.9 2.8 %collective-permute-done.13 = bf16[4,160,128]{2,1,0:T(8,128)(2,1)S(1)} collective-permute-done((bf16[4,160,128]{2,1,0:T(8,128)(2,1)S(1)}, bf16[4,160,128]{2,1,0:T(8,128)(2,1)S(1)}, u32[]{:S(2)}, u32[]{:S(2)}) %collective-permute-start.13) | collective-permute-done | bytes 163872 | tf_op jit(solution)/shard_map/ppermute | solution.py:411
  45.4 3.7 %attention_forward.2 = (f32[416,384]{1,0:T(8,128)S(1)}, bf16[384,1152]{1,0:T(8,128)(2,1)S(1)}, bf16[384,384]{1,0:T(8,128)(2,1)S(1)}, f32[8,384]{1,0:T(8,128)S(1)...) custom-call(s32[16]{0:T(128)S(1)} %get-tuple-element.149.refs_0_, ...), custom_call_target="tpu_custom_call" | custom-call | flops 623640576 | bytes 7243328 | tf_op jit(solution)/shard_map/attention_forward/pallas_call | solution.py:390
  49.1 2.9 %collective-permute-done.15 = bf16[4,288,128]{2,1,0:T(8,128)(2,1)S(1)} collective-permute-done((bf16[4,288,128]{2,1,0:T(8,128)(2,1)S(1)}, bf16[4,288,128]{2,1,0:T(8,128)(2,1)S(1)}, u32[]{:S(2)}, u32[]{:S(2)}) %collective-permute-start.15) | collective-permute-done | bytes 294944 | tf_op jit(solution)/shard_map/ppermute | solution.py:411
  54.1 4.3 %mlp_forward.2 = (bf16[384,1536]{1,0:T(8,128)(2,1)S(1)}, bf16[1536,384]{1,0:T(8,128)(2,1)S(1)}, f32[8,384]{1,0:T(8,128)S(1)}, bf16[416,384]{1,0:T(8,128)(2,1)S(1...) custom-call(s32[16]{0:T(128)S(1)} %get-tuple-element.149.refs_0_, ...), custom_call_target="tpu_custom_call" | custom-call | flops 981467136 | bytes 10195072 | tf_op jit(solution)/shard_map/mlp_forward/pallas_call | solution.py:390
  58.4 3.7 %attention_forward.3 = (bf16[384,1152]{1,0:T(8,128)(2,1)S(1)}, bf16[384,384]{1,0:T(8,128)(2,1)S(1)}, f32[8,384]{1,0:T(8,128)S(1)}, bf16[416,384]{1,0:T(8,128)(2,...) custom-call(s32[16]{0:T(128)S(1)} %get-tuple-element.149.refs_0_, ...), custom_call_target="tpu_custom_call" | custom-call | flops 623640576 | bytes 6940800 | tf_op jit(solution)/shard_map/attention_forward/pallas_call | solution.py:390
  62.1 4.6 %mlp_forward.3 = (bf16[384,1536]{1,0:T(8,128)(2,1)S(1)}, bf16[1536,384]{1,0:T(8,128)(2,1)S(1)}, f32[8,384]{1,0:T(8,128)S(1)}, bf16[416,384]{1,0:T(8,128)(2,1)S(1...) custom-call(s32[16]{0:T(128)S(1)} %get-tuple-element.149.refs_0_, ...), custom_call_target="tpu_custom_call" | custom-call | flops 981467136 | bytes 10161408 | tf_op jit(solution)/shard_map/mlp_forward/pallas_call | solution.py:390
  66.7 4.7 %mlp_backward.2 = (f32[2336,128]{1,0:T(8,128)S(1)}, bf16[2,4,448,128]{3,2,1,0:T(8,128)(2,1)S(1)}, bf16[2,4,448,128]{3,2,1,0:T(8,128)(2,1)S(1)}, f32[416,384]{1,0:T(8,128)S(1)}) custom-call(s32[2]{0:T(128)S(1)} %copy-done, s32[8]{0:T(128)S(1)} %get-tuple-element.147.refs_1_.refs_0_, s32[8]{0:T(128)S(1)} %get-tuple-element.148.refs_2_.refs_1_, ...), custom_call_target="tpu_custom_call" | custom-call | flops 1962934272 | bytes 9858632 | tf_op jit(solution)/shard_map/mlp_backward/pallas_call | solution.py:390
  71.6 5.5 %attention_backward.2 = (bf16[416,1152]{1,0:T(8,128)(2,1)S(1)}, f32[384,384]{1,0:T(8,128)S(1)}, f32[8,384]{1,0:T(8,128)S(1)}) custom-call(f32[416,384]{1,0:T(8,128)S(1)} %get-tuple-element.188.g_hidden.refs_2_, bf16[384,384]{1,0:T(8,128)(2,1)S(1)} %get-tuple-element.189.w_out, bf16[416,1152]{1,0:T(8,128)(2,1)S(1)} %get-tuple-element.190.qkv, ...), custom_call_target="tpu_custom_call" | custom-call | flops 511180800 | bytes 4810752 | tf_op jit(solution)/shard_map/attention_backward/pallas_call | solution.py:390
  77.3 3.1 %projection_backward.2 = (bf16[2,4,448,128]{3,2,1,0:T(8,128)(2,1)S(1)}, bf16[2,4,448,128]{3,2,1,0:T(8,128)(2,1)S(1)}, f32[416,384]{1,0:T(8,128)S(1)}) custom-call(s32[8]{0:T(128)S(1)} %get-tuple-element.147.refs_1_.refs_0_, s32[8]{0:T(128)S(1)} %get-tuple-element.148.refs_2_.refs_1_, f32[416,384]{1,0:T(8,128)S(1)} %get-tuple-element.188.g_hidden.refs_2_, ...), custom_call_target="tpu_custom_call" | custom-call | flops 736100352 | bytes 7725120 | tf_op jit(solution)/shard_map/projection_backward/pallas_call | solution.py:390
  83.3 4.7 %mlp_backward.3 = (f32[2336,128]{1,0:T(8,128)S(1)}, bf16[2,4,448,128]{3,2,1,0:T(8,128)(2,1)S(1)}, bf16[2,4,448,128]{3,2,1,0:T(8,128)(2,1)S(1)}, f32[416,384]{1,0:T(8,128)S(1)}) custom-call(s32[8]{0:T(128)S(1)} %get-tuple-element.147.refs_1_.refs_0_, s32[8]{0:T(128)S(1)} %get-tuple-element.148.refs_2_.refs_1_, f32[416,384]{1,0:T(8,128)S(1)} %get-tuple-element.209.refs_2_, ...), custom_call_target="tpu_custom_call" | custom-call | flops 1962934272 | bytes 10195008 | tf_op jit(solution)/shard_map/mlp_backward/pallas_call | solution.py:390
  95.0 5.5 %attention_backward.3 = (bf16[416,1152]{1,0:T(8,128)(2,1)S(1)}, f32[384,384]{1,0:T(8,128)S(1)}, f32[8,384]{1,0:T(8,128)S(1)}) custom-call(f32[416,384]{1,0:T(8,128)S(1)} %get-tuple-element.227.g_hidden.refs_2_, bf16[384,384]{1,0:T(8,128)(2,1)S(1)} %get-tuple-element.228.w_out, bf16[416,1152]{1,0:T(8,128)(2,1)S(1)} %get-tuple-element.229.qkv, ...), custom_call_target="tpu_custom_call" | custom-call | flops 511180800 | bytes 4810752 | tf_op jit(solution)/shard_map/attention_backward/pallas_call | solution.py:390
  105.5 3.1 %projection_backward.3 = (bf16[2,4,448,128]{3,2,1,0:T(8,128)(2,1)S(1)}, bf16[2,4,448,128]{3,2,1,0:T(8,128)(2,1)S(1)}, f32[2,197,384]{2,1,0:T(8,128)S(1)}) custom-call(s32[8]{0:T(128)S(1)} %get-tuple-element.147.refs_1_.refs_0_, s32[8]{0:T(128)S(1)} %get-tuple-element.148.refs_2_.refs_1_, f32[416,384]{1,0:T(8,128)S(1)} %get-tuple-element.227.g_hidden.refs_2_, ...), custom_call_target="tpu_custom_call" | custom-call | flops 736100352 | bytes 7691328 | tf_op jit(solution)/shard_map/projection_backward/pallas_call | solution.py:390
  115.0 6.9 %collective-permute-done.38 = bf16[1,448,128]{2,1,0:T(8,128)(2,1)S(1)} collective-permute-done((bf16[1,448,128]{2,1,0:T(8,128)(2,1)S(1)}, bf16[1,448,128]{2,1,0:T(8,128)(2,1)S(1)}, u32[]{:S(2)}, u32[]{:S(2)}) %collective-permute-start.38) | collective-permute-done | bytes 114720 | tf_op jit(solution)/shard_map/ppermute | solution.py:411
  124.3 2.8 %collective-permute-start.47 = (bf16[448,128]{1,0:T(8,128)(2,1)S(1)}, bf16[448,128]{1,0:T(8,128)(2,1)S(1)}, u32[]{:S(2)}, u32[]{:S(2)}) collective-permute-start(bf16[448,128]{1,0:T(8,128)(2,1)S(1)} %get-tuple-element.353), channel_id=1, source_target_pairs={{0,16},{1,17},{2,18},{3,19},{4,20},{5,21},{6,22},{7,23},{8,24},{9,... | collective-permute-start | bytes 344072 | tf_op jit(solution)/shard_map/ppermute | solution.py:411
  128.0 3.6 %collective-permute-start.46 = (bf16[448,128]{1,0:T(8,128)(2,1)S(1)}, bf16[448,128]{1,0:T(8,128)(2,1)S(1)}, u32[]{:S(2)}, u32[]{:S(2)}) collective-permute-start(bf16[448,128]{1,0:T(8,128)(2,1)S(1)} %select_bitcast_fusion.4), channel_id=1, source_target_pairs={{0,24},{1,25},{2,26},{3,27},{4,28},{5,29},{6,30},{7,31},{8,16},{9,... | collective-permute-start | bytes 344072 | tf_op jit(solution)/shard_map/ppermute | solution.py:411
  136.7 4.7 %collective-permute-done.45 = bf16[448,128]{1,0:T(8,128)(2,1)S(1)} collective-permute-done((bf16[448,128]{1,0:T(8,128)(2,1)S(1)}, bf16[448,128]{1,0:T(8,128)(2,1)S(1)}, u32[]{:S(2)}, u32[]{:S(2)}) %collective-permute-start.45) | collective-permute-done | bytes 114720 | tf_op jit(solution)/shard_map/ppermute | solution.py:411
  141.7 2.8 %multiply_subtract_fusion = (f32[2,55552]{1,0:T(2,128)}, f32[2,55552]{1,0:T(2,128)}, f32[2,55552]{1,0:T(2,128)}) fusion(f32[2,55552]{1,0:T(2,128)S(1)} %copy-done.1, f32[55552]{0:T(1024)S(1)} %broadcast_select_fusion.10, f32[55552]{0:T(1024)S(1)} %get-tuple-element.302, f32[1,55552]{1,0:T(1,128)S(1)} %bitcast.83, f32[1,55552]{1,0:T(1,128)S(1)} %bitcast.84, ...), kind=kLoop, calls=%fused_computation.43 | loop fusion | flops 1777664 | bytes 3555328 | tf_op jit(solution)/shard_map/sub | solution.py:675
  (183 shorter events, 53.4 us)
Async XLA Ops:
  2.5 9.8 %collective-permute-start = (bf16[448,128]{1,0:T(8,128)(2,1)S(1)}, bf16[448,128]{1,0:T(8,128)(2,1)S(1)}, u32[]{:S(2)}, u32[]{:S(2)}) collective-permute-start(bf16[448,128]{1,0:T(8,128)(2,1)S(1)} %get-tuple-element.372), channel_id=1, source_target_pairs={{0,8},{1,9},{2,10},{3,11},{4,12},{5,13},{6,14},{7,15},{8,0},{9,1},... | collective-permute-start | bytes 344072 | tf_op jit(solution)/shard_map/ppermute | solution.py:411
  5.6 11.7 %collective-permute-start.1 = (bf16[448,128]{1,0:T(8,128)(2,1)S(1)}, bf16[448,128]{1,0:T(8,128)(2,1)S(1)}, u32[]{:S(2)}, u32[]{:S(2)}) collective-permute-start(bf16[448,128]{1,0:T(8,128)(2,1)S(1)} %get-tuple-element.372), channel_id=1, source_target_pairs={{0,16},{1,17},{2,18},{3,19},{4,20},{5,21},{6,22},{7,23},{8,24},{9,... | collective-permute-start | bytes 344072 | tf_op jit(solution)/shard_map/ppermute | solution.py:411
  8.2 9.1 %collective-permute-start.2 = (bf16[448,128]{1,0:T(8,128)(2,1)S(1)}, bf16[448,128]{1,0:T(8,128)(2,1)S(1)}, u32[]{:S(2)}, u32[]{:S(2)}) collective-permute-start(bf16[448,128]{1,0:T(8,128)(2,1)S(1)} %get-tuple-element.372), channel_id=1, source_target_pairs={{0,24},{1,25},{2,26},{3,27},{4,28},{5,29},{6,30},{7,31},{8,16},{9,... | collective-permute-start | bytes 344072 | tf_op jit(solution)/shard_map/ppermute | solution.py:411
  17.3 8.9 %collective-permute-start.4 = (bf16[2,448,128]{2,1,0:T(8,128)(2,1)S(1)}, bf16[2,448,128]{2,1,0:T(8,128)(2,1)S(1)}, u32[]{:S(2)}, u32[]{:S(2)}) collective-permute-start(bf16[2,448,128]{2,1,0:T(8,128)(2,1)S(1)} %get-tuple-element.348), channel_id=1, source_target_pairs={{0,2},{1,3},{2,0},{3,1},{4,6},{5,7},{6,4},{7,5},{8,10},{9,11},{10,... | collective-permute-start | bytes 688136 | tf_op jit(solution)/shard_map/ppermute | solution.py:411
  26.3 14.2 %collective-permute-start.10 = (bf16[4,448,128]{2,1,0:T(8,128)(2,1)S(1)}, bf16[4,448,128]{2,1,0:T(8,128)(2,1)S(1)}, u32[]{:S(2)}, u32[]{:S(2)}) collective-permute-start(bf16[4,448,128]{2,1,0:T(8,128)(2,1)S(1)} %pad_maximum_fusion.6), channel_id=1, source_target_pairs={{0,2},{1,3},{2,0},{3,1},{4,6},{5,7},{6,4},{7,5},{8,10},{9,11},{10,... | collective-permute-start | bytes 1376264 | tf_op jit(solution)/shard_map/ppermute | solution.py:411
  27.0 13.6 %collective-permute-start.9 = (bf16[4,448,128]{2,1,0:T(8,128)(2,1)S(1)}, bf16[4,448,128]{2,1,0:T(8,128)(2,1)S(1)}, u32[]{:S(2)}, u32[]{:S(2)}) collective-permute-start(bf16[4,448,128]{2,1,0:T(8,128)(2,1)S(1)} %pad_maximum_fusion.5), channel_id=1, source_target_pairs={{0,4},{1,5},{2,6},{3,7},{4,0},{5,1},{6,2},{7,3},{8,12},{9,13},{10,... | collective-permute-start | bytes 1376264 | tf_op jit(solution)/shard_map/ppermute | solution.py:411
  30.6 8.0 %collective-permute-start.13 = (bf16[4,160,128]{2,1,0:T(8,128)(2,1)S(1)}, bf16[4,160,128]{2,1,0:T(8,128)(2,1)S(1)}, u32[]{:S(2)}, u32[]{:S(2)}) collective-permute-start(bf16[4,160,128]{2,1,0:T(8,128)(2,1)S(1)} %pad_maximum_fusion.15), channel_id=1, source_target_pairs={{0,16},{1,17},{2,18},{3,19},{4,20},{5,21},{6,22},{7,23},{8,24},{9,... | collective-permute-start | bytes 491528 | tf_op jit(solution)/shard_map/ppermute | solution.py:411
  40.8 11.7 %collective-permute-start.17 = (bf16[4,2,160,128]{3,2,0,1:T(8,128)(2,1)S(1)}, bf16[4,2,160,128]{3,2,0,1:T(8,128)(2,1)S(1)}, u32[]{:S(2)}, u32[]{:S(2)}) collective-permute-start(bf16[4,2,160,128]{3,2,0,1:T(8,128)(2,1)S(1)} %pad_maximum_fusion.8), channel_id=1, source_target_pairs={{0,8},{1,9},{2,10},{3,11},{4,12},{5,13},{6,14},{7,15},{8,0},{9,1},... | collective-permute-start | bytes 983048 | tf_op jit(solution)/shard_map/ppermute | solution.py:411
  42.8 9.2 %collective-permute-start.15 = (bf16[4,288,128]{2,1,0:T(8,128)(2,1)S(1)}, bf16[4,288,128]{2,1,0:T(8,128)(2,1)S(1)}, u32[]{:S(2)}, u32[]{:S(2)}) collective-permute-start(bf16[4,288,128]{2,1,0:T(8,128)(2,1)S(1)} %pad_maximum_fusion.9), channel_id=1, source_target_pairs={{0,4},{1,5},{2,6},{3,7},{4,0},{5,1},{6,2},{7,3},{8,12},{9,13},{10,... | collective-permute-start | bytes 884744 | tf_op jit(solution)/shard_map/ppermute | solution.py:411
  43.6 8.9 %collective-permute-start.16 = (bf16[4,288,128]{2,1,0:T(8,128)(2,1)S(1)}, bf16[4,288,128]{2,1,0:T(8,128)(2,1)S(1)}, u32[]{:S(2)}, u32[]{:S(2)}) collective-permute-start(bf16[4,288,128]{2,1,0:T(8,128)(2,1)S(1)} %pad_maximum_fusion.10), channel_id=1, source_target_pairs={{0,2},{1,3},{2,0},{3,1},{4,6},{5,7},{6,4},{7,5},{8,10},{9,11},{10,... | collective-permute-start | bytes 884744 | tf_op jit(solution)/shard_map/ppermute | solution.py:411
  45.3 8.8 %collective-permute-start.18 = (bf16[8,448,128]{2,1,0:T(8,128)(2,1)S(1)}, bf16[8,448,128]{2,1,0:T(8,128)(2,1)S(1)}, u32[]{:S(2)}, u32[]{:S(2)}) collective-permute-start(bf16[8,448,128]{2,1,0:T(8,128)(2,1)S(1)} %pad_maximum_fusion.1.refs_4_), channel_id=1, source_target_pairs={{0,1},{1,0},{2,3},{3,2},{4,5},{5,4},{6,7},{7,6},{8,9},{9,8},{10,11... | collective-permute-start | bytes 2752520 | tf_op jit(solution)/shard_map/ppermute | solution.py:411
  80.4 7.8 %collective-permute-start.26 = (bf16[2,4,448,128]{3,2,1,0:T(8,128)(2,1)S(1)}, bf16[2,4,448,128]{3,2,1,0:T(8,128)(2,1)S(1)}, u32[]{:S(2)}, u32[]{:S(2)}) collective-permute-start(bf16[2,4,448,128]{3,2,1,0:T(8,128)(2,1)S(1)} %get-tuple-element.208), channel_id=1, source_target_pairs={{0,1},{1,0},{2,3},{3,2},{4,5},{5,4},{6,7},{7,6},{8,9},{9,8},{10,11... | collective-permute-start | bytes 2752520 | tf_op jit(solution)/shard_map/ppermute | solution.py:411
  81.0 7.7 %collective-permute-start.25 = (bf16[2,448,128]{2,1,0:T(8,128)(2,1)S(1)}, bf16[2,448,128]{2,1,0:T(8,128)(2,1)S(1)}, u32[]{:S(2)}, u32[]{:S(2)}) collective-permute-start(bf16[2,448,128]{2,1,0:T(8,128)(2,1)S(1)} %get-tuple-element.343), channel_id=1, source_target_pairs={{0,2},{1,3},{2,0},{3,1},{4,6},{5,7},{6,4},{7,5},{8,10},{9,11},{10,... | collective-permute-start | bytes 688136 | tf_op jit(solution)/shard_map/ppermute | solution.py:411
  82.7 7.4 %collective-permute-start.24 = (bf16[2,448,128]{2,1,0:T(8,128)(2,1)S(1)}, bf16[2,448,128]{2,1,0:T(8,128)(2,1)S(1)}, u32[]{:S(2)}, u32[]{:S(2)}) collective-permute-start(bf16[2,448,128]{2,1,0:T(8,128)(2,1)S(1)} %get-tuple-element.345), channel_id=1, source_target_pairs={{0,4},{1,5},{2,6},{3,7},{4,0},{5,1},{6,2},{7,3},{8,12},{9,13},{10,... | collective-permute-start | bytes 688136 | tf_op jit(solution)/shard_map/ppermute | solution.py:411
  90.3 10.3 %collective-permute-start.30 = (bf16[2,448,128]{2,1,0:T(8,128)(2,1)S(1)}, bf16[2,448,128]{2,1,0:T(8,128)(2,1)S(1)}, u32[]{:S(2)}, u32[]{:S(2)}) collective-permute-start(bf16[2,448,128]{2,1,0:T(8,128)(2,1)S(1)} %get-tuple-element.339), channel_id=1, source_target_pairs={{0,2},{1,3},{2,0},{3,1},{4,6},{5,7},{6,4},{7,5},{8,10},{9,11},{10,... | collective-permute-start | bytes 688136 | tf_op jit(solution)/shard_map/ppermute | solution.py:411
  91.1 9.5 %collective-permute-start.29 = (bf16[2,448,128]{2,1,0:T(8,128)(2,1)S(1)}, bf16[2,448,128]{2,1,0:T(8,128)(2,1)S(1)}, u32[]{:S(2)}, u32[]{:S(2)}) collective-permute-start(bf16[2,448,128]{2,1,0:T(8,128)(2,1)S(1)} %get-tuple-element.341), channel_id=1, source_target_pairs={{0,4},{1,5},{2,6},{3,7},{4,0},{5,1},{6,2},{7,3},{8,12},{9,13},{10,... | collective-permute-start | bytes 688136 | tf_op jit(solution)/shard_map/ppermute | solution.py:411
  92.6 8.0 %collective-permute-start.28 = (bf16[1,448,128]{2,1,0:T(8,128)(2,1)S(1)}, bf16[1,448,128]{2,1,0:T(8,128)(2,1)S(1)}, u32[]{:S(2)}, u32[]{:S(2)}) collective-permute-start(bf16[1,448,128]{2,1,0:T(8,128)(2,1)S(1)} %get-tuple-element.367), channel_id=1, source_target_pairs={{0,4},{1,5},{2,6},{3,7},{4,0},{5,1},{6,2},{7,3},{8,12},{9,13},{10,... | collective-permute-start | bytes 344072 | tf_op jit(solution)/shard_map/ppermute | solution.py:411
  100.7 7.9 %collective-permute-start.33 = (bf16[1,448,128]{2,1,0:T(8,128)(2,1)S(1)}, bf16[1,448,128]{2,1,0:T(8,128)(2,1)S(1)}, u32[]{:S(2)}, u32[]{:S(2)}) collective-permute-start(bf16[1,448,128]{2,1,0:T(8,128)(2,1)S(1)} %get-tuple-element.363), channel_id=1, source_target_pairs={{0,4},{1,5},{2,6},{3,7},{4,0},{5,1},{6,2},{7,3},{8,12},{9,13},{10,... | collective-permute-start | bytes 344072 | tf_op jit(solution)/shard_map/ppermute | solution.py:411
  111.8 10.2 %collective-permute-start.36 = (bf16[2,448,128]{2,1,0:T(8,128)(2,1)S(1)}, bf16[2,448,128]{2,1,0:T(8,128)(2,1)S(1)}, u32[]{:S(2)}, u32[]{:S(2)}) collective-permute-start(bf16[2,448,128]{2,1,0:T(8,128)(2,1)S(1)} %get-tuple-element.335), channel_id=1, source_target_pairs={{0,2},{1,3},{2,0},{3,1},{4,6},{5,7},{6,4},{7,5},{8,10},{9,11},{10,... | collective-permute-start | bytes 688136 | tf_op jit(solution)/shard_map/ppermute | solution.py:411
  112.7 9.2 %collective-permute-start.35 = (bf16[2,448,128]{2,1,0:T(8,128)(2,1)S(1)}, bf16[2,448,128]{2,1,0:T(8,128)(2,1)S(1)}, u32[]{:S(2)}, u32[]{:S(2)}) collective-permute-start(bf16[2,448,128]{2,1,0:T(8,128)(2,1)S(1)} %get-tuple-element.337), channel_id=1, source_target_pairs={{0,4},{1,5},{2,6},{3,7},{4,0},{5,1},{6,2},{7,3},{8,12},{9,13},{10,... | collective-permute-start | bytes 688136 | tf_op jit(solution)/shard_map/ppermute | solution.py:411
  114.0 7.9 %collective-permute-start.38 = (bf16[1,448,128]{2,1,0:T(8,128)(2,1)S(1)}, bf16[1,448,128]{2,1,0:T(8,128)(2,1)S(1)}, u32[]{:S(2)}, u32[]{:S(2)}) collective-permute-start(bf16[1,448,128]{2,1,0:T(8,128)(2,1)S(1)} %get-tuple-element.361), channel_id=1, source_target_pairs={{0,2},{1,3},{2,0},{3,1},{4,6},{5,7},{6,4},{7,5},{8,10},{9,11},{10,... | collective-permute-start | bytes 344072 | tf_op jit(solution)/shard_map/ppermute | solution.py:411
  124.3 9.1 %collective-permute-start.47 = (bf16[448,128]{1,0:T(8,128)(2,1)S(1)}, bf16[448,128]{1,0:T(8,128)(2,1)S(1)}, u32[]{:S(2)}, u32[]{:S(2)}) collective-permute-start(bf16[448,128]{1,0:T(8,128)(2,1)S(1)} %get-tuple-element.353), channel_id=1, source_target_pairs={{0,16},{1,17},{2,18},{3,19},{4,20},{5,21},{6,22},{7,23},{8,24},{9,... | collective-permute-start | bytes 344072 | tf_op jit(solution)/shard_map/ppermute | solution.py:411
  128.0 7.9 %collective-permute-start.46 = (bf16[448,128]{1,0:T(8,128)(2,1)S(1)}, bf16[448,128]{1,0:T(8,128)(2,1)S(1)}, u32[]{:S(2)}, u32[]{:S(2)}) collective-permute-start(bf16[448,128]{1,0:T(8,128)(2,1)S(1)} %select_bitcast_fusion.4), channel_id=1, source_target_pairs={{0,24},{1,25},{2,26},{3,27},{4,28},{5,29},{6,30},{7,31},{8,16},{9,... | collective-permute-start | bytes 344072 | tf_op jit(solution)/shard_map/ppermute | solution.py:411
  131.6 9.8 %collective-permute-start.45 = (bf16[448,128]{1,0:T(8,128)(2,1)S(1)}, bf16[448,128]{1,0:T(8,128)(2,1)S(1)}, u32[]{:S(2)}, u32[]{:S(2)}) collective-permute-start(bf16[448,128]{1,0:T(8,128)(2,1)S(1)} %get-tuple-element.326), channel_id=1, source_target_pairs={{0,16},{1,17},{2,18},{3,19},{4,20},{5,21},{6,22},{7,23},{8,24},{9,... | collective-permute-start | bytes 344072 | tf_op jit(solution)/shard_map/ppermute | solution.py:411
  (30 other events, 165.3 us)

commit v2 on v1

--- a/solution.py
+++ b/solution.py
@@ -382,6 +382,27 @@
     pack(flat, 0, rows_each, 0, places, near, far)
 
 
+def adam(rows_each, *refs):
+    offset, refs = refs[0], refs[1:]
+    parts0, parts1, refs = refs[:4], refs[4:6], refs[6:]
+    params, first_moment, second_moment, new_params, new_first, new_second = refs
+    shape = (rows_each, LANES)
+    row = lax.broadcasted_iota(jnp.int32, shape, 0)
+    flags = matrix_flags((offset[0] + row) * LANES + lax.broadcasted_iota(jnp.int32, shape, 1))
+    rate = jnp.where(flags, rate_matrix, rate_vector)
+    decay = jnp.where(flags, decay_matrix, 0.0)
+    for layer, parts in enumerate((parts0, parts1)):
+        grads = sum(part[:rows_each, :].astype(f32) for part in parts)
+        first = beta_one * first_moment[:, layer, :] + (1.0 - beta_one) * grads
+        second = beta_two * second_moment[:, layer, :] + (1.0 - beta_two) * grads * grads
+        new_first[:, layer, :] = first
+        new_second[:, layer, :] = second
+        first_hat = first / (1.0 - beta_one**STEP)
+        second_hat = second / (1.0 - beta_two**STEP)
+        old = params[:, layer, :]
+        new_params[:, layer, :] = old - rate * (first_hat / (jnp.sqrt(second_hat) + adam_eps) + decay * old)
+
+
 def call(body, name, inputs, outputs, scratch, scalars=0, flops=0):
     in_specs = [pl.BlockSpec(memory_space=pltpu.SMEM)] * scalars
     in_specs += [pl.BlockSpec(memory_space=pltpu.VMEM)] * (len(inputs) - scalars)
@@ -446,10 +467,13 @@
     place_wide = places(me, size, [2, 4] + chain + [1])
     place = [places(me, size // 2, chain[1:] + [mask, 6 - mask, 1]) for mask in planes[0]]
 
+    def alternating(value):
+        return jnp.swapaxes(value.reshape(2, rows_each, LANES), 0, 1)
+
     is_low, is_first = (me >> (bits - 1)) & 1 == 0, (me >> (bits - 2)) & 1 == 0
-    flags = matrix_flags(me * width + jnp.arange(width, dtype=jnp.int32)).astype(f32)
-    early = together(params, is_low, is_first, flags, place_low, place_high, place_wide, *place)
-    params, is_low, is_first, flags, place_low, place_high, place_wide, *place = early
+    offset = me[None] * rows_each
+    early = together(params, is_low, is_first, offset, place_low, place_high, place_wide, *place)
+    params, is_low, is_first, offset, place_low, place_high, place_wide, *place = early
     compact = params.astype(bf16).reshape(2, rows_each, LANES)
     compact = jnp.pad(compact, ((0, 0), (0, padded - rows_each), (0, 0)))
 
@@ -652,27 +676,25 @@
     inner1 = to_inner(along(low1), high1)
     low0, = hold(low0)
     low0 = to_plane(low0, 1)
-    held, = hold(low0 + high0 + [inner1])
-    low0, high0, top1 = to_plane(held[:2], 0), along(held[2:4]), to_top(added(held[4]))
+    held, = hold(low0 + high0 + [to_top(added(inner1))])
+    low0, high0, top1 = to_plane(held[:2], 0), along(held[2:4]), held[4]
     held, *high0, outputs, input_grad = hold(low0, *high0, outputs, input_grad)
     low0 = along(held)
     here, there = [jnp.where(is_low, *pair) for pair in zip(low0, high0)], [jnp.where(is_low, *pair) for pair in zip(high0, low0)]
     here, there = [[jnp.where(is_first, *pair), jnp.where(is_first, *pair[::-1])] for pair in (here, there)]
     values = exchanged(here[1][0], there[0][0], there[1][0])
     (nearby, other, far_other), received = values, top1[1]
-    sum0 = here[0][0].astype(f32) + nearby.astype(f32) + other.astype(f32) + far_other.astype(f32)
-    sum1 = top1[0].astype(f32) + received.astype(f32)
-    owned = [total[:rows_each].reshape(width) for total in (sum0, sum1)]
-
-    grads = jnp.stack(owned)
-    flags = flags[None, :] > 0
-    rate = jnp.where(flags, rate_matrix, rate_vector)
-    decay = jnp.where(flags, decay_matrix, 0.0)
-    new_first = beta_one * first_moment + (1.0 - beta_one) * grads
-    new_second = beta_two * second_moment + (1.0 - beta_two) * grads * grads
-    first_hat = new_first / (1.0 - beta_one**STEP)
-    second_hat = new_second / (1.0 - beta_two**STEP)
-    new_params = params - rate * (first_hat / (jnp.sqrt(second_hat) + adam_eps) + decay * params)
+    updated = call(
+        functools.partial(adam, rows_each),
+        "adam",
+        [offset, here[0][0], nearby, other, far_other, top1[0], received, *map(alternating, (params, first_moment, second_moment))],
+        [((rows_each, 2, LANES), f32)] * 3,
+        [],
+        scalars=1,
+    )
+    new_params, new_first, new_second = [
+        jnp.swapaxes(value, 0, 1).reshape(2, width) for value in updated
+    ]
     return (outputs, input_grad, new_params, new_first, new_second)
 
 

time: 145 us -> 143 us (0.986)
  other arithmetic: 7.12 us -> 3.9 us
  Pallas kernels: 42.7 us -> 45.6 us
    pallas_call x10 -> x11, Pallas kernels: 42.7 us -> 45.6 us  [call(): pl.pallas_call(body, name=name, out_shape=shapes, in_specs=in_specs, out_...]
    sub x1 -> x0, other arithmetic: 2.83 us -> none  [shards(): params - rate * (first_hat / (jnp.sqrt(second_hat) + adam_eps) + decay *...]
  transfers between devices with their start and end apart: 48 -> 48, of which waited for: 18 -> 19; matrix products, arithmetic and copies ran while one was open for 4% -> 4% of each run, Pallas kernels for 18% -> 19%
where the time goes in v2:
time: 143 us
  starting transfers between devices  52.1 us (36%)
  Pallas kernels  45.6 us (32%)
  waiting for transfers between devices  36.1 us (25%)
  other arithmetic  3.9 us (3%)
  local copies, waits for them, and re-layouts  3.68 us (3%)
    ppermute x48, starting transfers between devices, swap(): return lax.ppermute(values, 'dp', [(i, i ^ mask) for i in range(size)])  52.1 us
    pallas_call x11, Pallas kernels, call(): pl.pallas_call(body, name=name, out_shape=shapes, in_specs=in_specs, out_...  45.6 us
    ppermute x48, waiting for transfers between devices, swap(): return lax.ppermute(values, 'dp', [(i, i ^ mask) for i in range(size)])  36.1 us
  transfers between devices with their start and end apart: 48, of which 19 were waited for; matrix products, arithmetic and copies ran while one was open for 4% of the time, Pallas kernels for 19%

profile of v2, /device:TPU:0, one launch (start us, length us, event | category | flops | bytes accessed | tf_op | source)
XLA Modules:
  0.0 142.9 jit_solution(5516255958622020863)
XLA Ops:
  2.3 3.1 %collective-permute-start = (bf16[448,128]{1,0:T(8,128)(2,1)S(1)}, bf16[448,128]{1,0:T(8,128)(2,1)S(1)}, u32[]{:S(2)}, u32[]{:S(2)}) collective-permute-start(bf16[448,128]{1,0:T(8,128)(2,1)S(1)} %get-tuple-element.373), channel_id=1, source_target_pairs={{0,8},{1,9},{2,10},{3,11},{4,12},{5,13},{6,14},{7,15},{8,0},{9,1},... | collective-permute-start | bytes 344072 | tf_op jit(solution)/shard_map/ppermute | solution.py:432
  5.4 2.6 %collective-permute-start.1 = (bf16[448,128]{1,0:T(8,128)(2,1)S(1)}, bf16[448,128]{1,0:T(8,128)(2,1)S(1)}, u32[]{:S(2)}, u32[]{:S(2)}) collective-permute-start(bf16[448,128]{1,0:T(8,128)(2,1)S(1)} %get-tuple-element.373), channel_id=1, source_target_pairs={{0,16},{1,17},{2,18},{3,19},{4,20},{5,21},{6,22},{7,23},{8,24},{9,... | collective-permute-start | bytes 344072 | tf_op jit(solution)/shard_map/ppermute | solution.py:432
  9.7 2.4 %collective-permute-done.3 = bf16[1,160,128]{2,1,0:T(8,128)(2,1)S(1)} collective-permute-done((bf16[1,160,128]{2,1,0:T(8,128)(2,1)S(1)}, bf16[1,160,128]{2,1,0:T(8,128)(2,1)S(1)}, u32[]{:S(2)}, u32[]{:S(2)}) %collective-permute-start.3) | collective-permute-done | bytes 40992 | tf_op jit(solution)/shard_map/ppermute | solution.py:432
  12.0 5.0 %collective-permute-done.1 = bf16[448,128]{1,0:T(8,128)(2,1)S(1)} collective-permute-done((bf16[448,128]{1,0:T(8,128)(2,1)S(1)}, bf16[448,128]{1,0:T(8,128)(2,1)S(1)}, u32[]{:S(2)}, u32[]{:S(2)}) %collective-permute-start.1) | collective-permute-done | bytes 114720 | tf_op jit(solution)/shard_map/ppermute | solution.py:432
  20.8 2.8 %collective-permute-start.6 = (bf16[288,128]{1,0:T(8,128)(2,1)S(1)}, bf16[288,128]{1,0:T(8,128)(2,1)S(1)}, u32[]{:S(2)}, u32[]{:S(2)}) collective-permute-start(bf16[288,128]{1,0:T(8,128)(2,1)S(1)} %slice_bitcast_fusion.18), channel_id=1, source_target_pairs={{0,16},{1,17},{2,18},{3,19},{4,20},{5,21},{6,22},{7,23},{8,24},{9,... | collective-permute-start | bytes 221192 | tf_op jit(solution)/shard_map/ppermute | solution.py:432
  23.6 2.5 %collective-permute-done.6 = bf16[288,128]{1,0:T(8,128)(2,1)S(1)} collective-permute-done((bf16[288,128]{1,0:T(8,128)(2,1)S(1)}, bf16[288,128]{1,0:T(8,128)(2,1)S(1)}, u32[]{:S(2)}, u32[]{:S(2)}) %collective-permute-start.6) | collective-permute-done | bytes 73760 | tf_op jit(solution)/shard_map/ppermute | solution.py:432
  35.7 2.8 %collective-permute-done.13 = bf16[4,160,128]{2,1,0:T(8,128)(2,1)S(1)} collective-permute-done((bf16[4,160,128]{2,1,0:T(8,128)(2,1)S(1)}, bf16[4,160,128]{2,1,0:T(8,128)(2,1)S(1)}, u32[]{:S(2)}, u32[]{:S(2)}) %collective-permute-start.13) | collective-permute-done | bytes 163872 | tf_op jit(solution)/shard_map/ppermute | solution.py:432
  45.2 3.7 %attention_forward.2 = (f32[416,384]{1,0:T(8,128)S(1)}, bf16[384,1152]{1,0:T(8,128)(2,1)S(1)}, bf16[384,384]{1,0:T(8,128)(2,1)S(1)}, f32[8,384]{1,0:T(8,128)S(1)...) custom-call(s32[16]{0:T(128)S(1)} %get-tuple-element.152.refs_0_, ...), custom_call_target="tpu_custom_call" | custom-call | flops 623640576 | bytes 7243328 | tf_op jit(solution)/shard_map/attention_forward/pallas_call | solution.py:411
  48.9 2.9 %collective-permute-done.15 = bf16[4,288,128]{2,1,0:T(8,128)(2,1)S(1)} collective-permute-done((bf16[4,288,128]{2,1,0:T(8,128)(2,1)S(1)}, bf16[4,288,128]{2,1,0:T(8,128)(2,1)S(1)}, u32[]{:S(2)}, u32[]{:S(2)}) %collective-permute-start.15) | collective-permute-done | bytes 294944 | tf_op jit(solution)/shard_map/ppermute | solution.py:432
  53.8 4.3 %mlp_forward.2 = (bf16[384,1536]{1,0:T(8,128)(2,1)S(1)}, bf16[1536,384]{1,0:T(8,128)(2,1)S(1)}, f32[8,384]{1,0:T(8,128)S(1)}, bf16[416,384]{1,0:T(8,128)(2,1)S(1...) custom-call(s32[16]{0:T(128)S(1)} %get-tuple-element.152.refs_0_, ...), custom_call_target="tpu_custom_call" | custom-call | flops 981467136 | bytes 10195072 | tf_op jit(solution)/shard_map/mlp_forward/pallas_call | solution.py:411
  58.2 3.7 %attention_forward.3 = (bf16[384,1152]{1,0:T(8,128)(2,1)S(1)}, bf16[384,384]{1,0:T(8,128)(2,1)S(1)}, f32[8,384]{1,0:T(8,128)S(1)}, bf16[416,384]{1,0:T(8,128)(2,...) custom-call(s32[16]{0:T(128)S(1)} %get-tuple-element.152.refs_0_, ...), custom_call_target="tpu_custom_call" | custom-call | flops 623640576 | bytes 6940800 | tf_op jit(solution)/shard_map/attention_forward/pallas_call | solution.py:411
  61.9 4.6 %mlp_forward.3 = (bf16[384,1536]{1,0:T(8,128)(2,1)S(1)}, bf16[1536,384]{1,0:T(8,128)(2,1)S(1)}, f32[8,384]{1,0:T(8,128)S(1)}, bf16[416,384]{1,0:T(8,128)(2,1)S(1...) custom-call(s32[16]{0:T(128)S(1)} %get-tuple-element.152.refs_0_, ...), custom_call_target="tpu_custom_call" | custom-call | flops 981467136 | bytes 10161408 | tf_op jit(solution)/shard_map/mlp_forward/pallas_call | solution.py:411
  66.5 4.7 %mlp_backward.2 = (f32[2336,128]{1,0:T(8,128)S(1)}, bf16[2,4,448,128]{3,2,1,0:T(8,128)(2,1)S(1)}, bf16[2,4,448,128]{3,2,1,0:T(8,128)(2,1)S(1)}, f32[416,384]{1,0:T(8,128)S(1)}) custom-call(s32[2]{0:T(128)S(1)} %copy-done.3, s32[8]{0:T(128)S(1)} %get-tuple-element.150.refs_1_.refs_0_, s32[8]{0:T(128)S(1)} %get-tuple-element.151.refs_2_.refs_1_, ...), custom_call_target="tpu_custom_call" | custom-call | flops 1962934272 | bytes 9858632 | tf_op jit(solution)/shard_map/mlp_backward/pallas_call | solution.py:411
  71.4 5.5 %attention_backward.2 = (bf16[416,1152]{1,0:T(8,128)(2,1)S(1)}, f32[384,384]{1,0:T(8,128)S(1)}, f32[8,384]{1,0:T(8,128)S(1)}) custom-call(f32[416,384]{1,0:T(8,128)S(1)} %get-tuple-element.191.g_hidden.refs_2_, bf16[384,384]{1,0:T(8,128)(2,1)S(1)} %get-tuple-element.192.w_out, bf16[416,1152]{1,0:T(8,128)(2,1)S(1)} %get-tuple-element.193.qkv, ...), custom_call_target="tpu_custom_call" | custom-call | flops 511180800 | bytes 4810752 | tf_op jit(solution)/shard_map/attention_backward/pallas_call | solution.py:411
  77.0 3.1 %projection_backward.2 = (bf16[2,4,448,128]{3,2,1,0:T(8,128)(2,1)S(1)}, bf16[2,4,448,128]{3,2,1,0:T(8,128)(2,1)S(1)}, f32[416,384]{1,0:T(8,128)S(1)}) custom-call(s32[8]{0:T(128)S(1)} %get-tuple-element.150.refs_1_.refs_0_, s32[8]{0:T(128)S(1)} %get-tuple-element.151.refs_2_.refs_1_, f32[416,384]{1,0:T(8,128)S(1)} %get-tuple-element.191.g_hidden.refs_2_, ...), custom_call_target="tpu_custom_call" | custom-call | flops 736100352 | bytes 7725120 | tf_op jit(solution)/shard_map/projection_backward/pallas_call | solution.py:411
  83.0 4.7 %mlp_backward.3 = (f32[2336,128]{1,0:T(8,128)S(1)}, bf16[2,4,448,128]{3,2,1,0:T(8,128)(2,1)S(1)}, bf16[2,4,448,128]{3,2,1,0:T(8,128)(2,1)S(1)}, f32[416,384]{1,0:T(8,128)S(1)}) custom-call(s32[8]{0:T(128)S(1)} %get-tuple-element.150.refs_1_.refs_0_, s32[8]{0:T(128)S(1)} %get-tuple-element.151.refs_2_.refs_1_, f32[416,384]{1,0:T(8,128)S(1)} %get-tuple-element.212.refs_2_, ...), custom_call_target="tpu_custom_call" | custom-call | flops 1962934272 | bytes 10195008 | tf_op jit(solution)/shard_map/mlp_backward/pallas_call | solution.py:411
  94.8 5.5 %attention_backward.3 = (bf16[416,1152]{1,0:T(8,128)(2,1)S(1)}, f32[384,384]{1,0:T(8,128)S(1)}, f32[8,384]{1,0:T(8,128)S(1)}) custom-call(f32[416,384]{1,0:T(8,128)S(1)} %get-tuple-element.230.g_hidden.refs_2_, bf16[384,384]{1,0:T(8,128)(2,1)S(1)} %get-tuple-element.231.w_out, bf16[416,1152]{1,0:T(8,128)(2,1)S(1)} %get-tuple-element.232.qkv, ...), custom_call_target="tpu_custom_call" | custom-call | flops 511180800 | bytes 4810752 | tf_op jit(solution)/shard_map/attention_backward/pallas_call | solution.py:411
  105.2 3.1 %projection_backward.3 = (bf16[2,4,448,128]{3,2,1,0:T(8,128)(2,1)S(1)}, bf16[2,4,448,128]{3,2,1,0:T(8,128)(2,1)S(1)}, f32[2,197,384]{2,1,0:T(8,128)S(1)}) custom-call(s32[8]{0:T(128)S(1)} %get-tuple-element.150.refs_1_.refs_0_, s32[8]{0:T(128)S(1)} %get-tuple-element.151.refs_2_.refs_1_, f32[416,384]{1,0:T(8,128)S(1)} %get-tuple-element.230.g_hidden.refs_2_, ...), custom_call_target="tpu_custom_call" | custom-call | flops 736100352 | bytes 7691328 | tf_op jit(solution)/shard_map/projection_backward/pallas_call | solution.py:411
  111.5 3.0 %collective-permute-done.41 = bf16[2,448,128]{2,1,0:T(8,128)(2,1)S(1)} collective-permute-done((bf16[2,448,128]{2,1,0:T(8,128)(2,1)S(1)}, bf16[2,448,128]{2,1,0:T(8,128)(2,1)S(1)}, u32[]{:S(2)}, u32[]{:S(2)}) %collective-permute-start.41) | collective-permute-done | bytes 229408 | tf_op jit(solution)/shard_map/ppermute | solution.py:432
  117.0 2.7 %collective-permute-start.42 = (bf16[448,128]{1,0:T(8,128)(2,1)S(1)}, bf16[448,128]{1,0:T(8,128)(2,1)S(1)}, u32[]{:S(2)}, u32[]{:S(2)}) collective-permute-start(bf16[448,128]{1,0:T(8,128)(2,1)S(1)} %get-tuple-element.358), channel_id=1, source_target_pairs={{0,16},{1,17},{2,18},{3,19},{4,20},{5,21},{6,22},{7,23},{8,24},{9,... | collective-permute-start | bytes 344072 | tf_op jit(solution)/shard_map/ppermute | solution.py:432
  119.7 4.1 %collective-permute-done.42.refs_6_ = bf16[448,128]{1,0:T(8,128)(2,1)S(1)} collective-permute-done((bf16[448,128]{1,0:T(8,128)(2,1)S(1)}, bf16[448,128]{1,0:T(8,128)(2,1)S(1)}, u32[]{:S(2)}, u32[]{:S(2)}) %collective-permute-start.42) | collective-permute-done | bytes 114720 | tf_op jit(solution)/shard_map/ppermute | solution.py:432
  126.3 2.4 %collective-permute-done.44 = bf16[1,448,128]{2,1,0:T(8,128)(2,1)S(1)} collective-permute-done((bf16[1,448,128]{2,1,0:T(8,128)(2,1)S(1)}, bf16[1,448,128]{2,1,0:T(8,128)(2,1)S(1)}, u32[]{:S(2)}, u32[]{:S(2)}) %collective-permute-start.44) | collective-permute-done | bytes 114720 | tf_op jit(solution)/shard_map/ppermute | solution.py:432
  130.0 2.2 %collective-permute-start.46 = (bf16[448,128]{1,0:T(8,128)(2,1)S(1)}, bf16[448,128]{1,0:T(8,128)(2,1)S(1)}, u32[]{:S(2)}, u32[]{:S(2)}) collective-permute-start(bf16[448,128]{1,0:T(8,128)(2,1)S(1)} %select_bitcast_fusion.3), channel_id=1, source_target_pairs={{0,16},{1,17},{2,18},{3,19},{4,20},{5,21},{6,22},{7,23},{8,24},{9,... | collective-permute-start | bytes 344072 | tf_op jit(solution)/shard_map/ppermute | solution.py:432
  140.0 2.9 %adam.1 = (f32[434,2,128]{2,1,0:T(2,128)}, f32[434,2,128]{2,1,0:T(2,128)}, f32[434,2,128]{2,1,0:T(2,128)}) custom-call(s32[1]{0:T(128)} %bitcast.refs_0_, bf16[448,128]{1,0:T(8,128)(2,1)S(1)} %select_bitcast_fusion.5.refs_1_, bf16[448,128]{1,0:T(8,128)(2,1)S(1)} %collective-permute-done.45.refs_2_, bf16[448,128]{1,0:T(8,128)(2,1)S(1)} %collective-permute-done.46.refs_3_, ...), custom_call_target="tpu_custom_call" | custom-call | bytes 3354628 | tf_op jit(solution)/shard_map/adam/pallas_call | solution.py:411
  (175 shorter events, 57.5 us)
Async XLA Ops:
  2.3 9.8 %collective-permute-start = (bf16[448,128]{1,0:T(8,128)(2,1)S(1)}, bf16[448,128]{1,0:T(8,128)(2,1)S(1)}, u32[]{:S(2)}, u32[]{:S(2)}) collective-permute-start(bf16[448,128]{1,0:T(8,128)(2,1)S(1)} %get-tuple-element.373), channel_id=1, source_target_pairs={{0,8},{1,9},{2,10},{3,11},{4,12},{5,13},{6,14},{7,15},{8,0},{9,1},... | collective-permute-start | bytes 344072 | tf_op jit(solution)/shard_map/ppermute | solution.py:432
  5.4 11.7 %collective-permute-start.1 = (bf16[448,128]{1,0:T(8,128)(2,1)S(1)}, bf16[448,128]{1,0:T(8,128)(2,1)S(1)}, u32[]{:S(2)}, u32[]{:S(2)}) collective-permute-start(bf16[448,128]{1,0:T(8,128)(2,1)S(1)} %get-tuple-element.373), channel_id=1, source_target_pairs={{0,16},{1,17},{2,18},{3,19},{4,20},{5,21},{6,22},{7,23},{8,24},{9,... | collective-permute-start | bytes 344072 | tf_op jit(solution)/shard_map/ppermute | solution.py:432
  8.0 9.1 %collective-permute-start.2 = (bf16[448,128]{1,0:T(8,128)(2,1)S(1)}, bf16[448,128]{1,0:T(8,128)(2,1)S(1)}, u32[]{:S(2)}, u32[]{:S(2)}) collective-permute-start(bf16[448,128]{1,0:T(8,128)(2,1)S(1)} %get-tuple-element.373), channel_id=1, source_target_pairs={{0,24},{1,25},{2,26},{3,27},{4,28},{5,29},{6,30},{7,31},{8,16},{9,... | collective-permute-start | bytes 344072 | tf_op jit(solution)/shard_map/ppermute | solution.py:432
  17.1 8.9 %collective-permute-start.4 = (bf16[2,448,128]{2,1,0:T(8,128)(2,1)S(1)}, bf16[2,448,128]{2,1,0:T(8,128)(2,1)S(1)}, u32[]{:S(2)}, u32[]{:S(2)}) collective-permute-start(bf16[2,448,128]{2,1,0:T(8,128)(2,1)S(1)} %get-tuple-element.349), channel_id=1, source_target_pairs={{0,2},{1,3},{2,0},{3,1},{4,6},{5,7},{6,4},{7,5},{8,10},{9,11},{10,... | collective-permute-start | bytes 688136 | tf_op jit(solution)/shard_map/ppermute | solution.py:432
  18.7 7.4 %collective-permute-start.5 = (bf16[2,448,128]{2,1,0:T(8,128)(2,1)S(1)}, bf16[2,448,128]{2,1,0:T(8,128)(2,1)S(1)}, u32[]{:S(2)}, u32[]{:S(2)}) collective-permute-start(bf16[2,448,128]{2,1,0:T(8,128)(2,1)S(1)} %get-tuple-element.348), channel_id=1, source_target_pairs={{0,4},{1,5},{2,6},{3,7},{4,0},{5,1},{6,2},{7,3},{8,12},{9,13},{10,... | collective-permute-start | bytes 688136 | tf_op jit(solution)/shard_map/ppermute | solution.py:432
  26.1 14.2 %collective-permute-start.10 = (bf16[4,448,128]{2,1,0:T(8,128)(2,1)S(1)}, bf16[4,448,128]{2,1,0:T(8,128)(2,1)S(1)}, u32[]{:S(2)}, u32[]{:S(2)}) collective-permute-start(bf16[4,448,128]{2,1,0:T(8,128)(2,1)S(1)} %pad_maximum_fusion.6), channel_id=1, source_target_pairs={{0,2},{1,3},{2,0},{3,1},{4,6},{5,7},{6,4},{7,5},{8,10},{9,11},{10,... | collective-permute-start | bytes 1376264 | tf_op jit(solution)/shard_map/ppermute | solution.py:432
  26.8 13.6 %collective-permute-start.9 = (bf16[4,448,128]{2,1,0:T(8,128)(2,1)S(1)}, bf16[4,448,128]{2,1,0:T(8,128)(2,1)S(1)}, u32[]{:S(2)}, u32[]{:S(2)}) collective-permute-start(bf16[4,448,128]{2,1,0:T(8,128)(2,1)S(1)} %pad_maximum_fusion.5), channel_id=1, source_target_pairs={{0,4},{1,5},{2,6},{3,7},{4,0},{5,1},{6,2},{7,3},{8,12},{9,13},{10,... | collective-permute-start | bytes 1376264 | tf_op jit(solution)/shard_map/ppermute | solution.py:432
  30.4 8.0 %collective-permute-start.13 = (bf16[4,160,128]{2,1,0:T(8,128)(2,1)S(1)}, bf16[4,160,128]{2,1,0:T(8,128)(2,1)S(1)}, u32[]{:S(2)}, u32[]{:S(2)}) collective-permute-start(bf16[4,160,128]{2,1,0:T(8,128)(2,1)S(1)} %pad_maximum_fusion.13), channel_id=1, source_target_pairs={{0,16},{1,17},{2,18},{3,19},{4,20},{5,21},{6,22},{7,23},{8,24},{9,... | collective-permute-start | bytes 491528 | tf_op jit(solution)/shard_map/ppermute | solution.py:432
  40.6 11.7 %collective-permute-start.17 = (bf16[4,2,160,128]{3,2,0,1:T(8,128)(2,1)S(1)}, bf16[4,2,160,128]{3,2,0,1:T(8,128)(2,1)S(1)}, u32[]{:S(2)}, u32[]{:S(2)}) collective-permute-start(bf16[4,2,160,128]{3,2,0,1:T(8,128)(2,1)S(1)} %pad_maximum_fusion.7), channel_id=1, source_target_pairs={{0,8},{1,9},{2,10},{3,11},{4,12},{5,13},{6,14},{7,15},{8,0},{9,1},... | collective-permute-start | bytes 983048 | tf_op jit(solution)/shard_map/ppermute | solution.py:432
  42.6 9.2 %collective-permute-start.15 = (bf16[4,288,128]{2,1,0:T(8,128)(2,1)S(1)}, bf16[4,288,128]{2,1,0:T(8,128)(2,1)S(1)}, u32[]{:S(2)}, u32[]{:S(2)}) collective-permute-start(bf16[4,288,128]{2,1,0:T(8,128)(2,1)S(1)} %pad_maximum_fusion.8), channel_id=1, source_target_pairs={{0,4},{1,5},{2,6},{3,7},{4,0},{5,1},{6,2},{7,3},{8,12},{9,13},{10,... | collective-permute-start | bytes 884744 | tf_op jit(solution)/shard_map/ppermute | solution.py:432
  43.4 8.9 %collective-permute-start.16 = (bf16[4,288,128]{2,1,0:T(8,128)(2,1)S(1)}, bf16[4,288,128]{2,1,0:T(8,128)(2,1)S(1)}, u32[]{:S(2)}, u32[]{:S(2)}) collective-permute-start(bf16[4,288,128]{2,1,0:T(8,128)(2,1)S(1)} %pad_maximum_fusion.9), channel_id=1, source_target_pairs={{0,2},{1,3},{2,0},{3,1},{4,6},{5,7},{6,4},{7,5},{8,10},{9,11},{10,... | collective-permute-start | bytes 884744 | tf_op jit(solution)/shard_map/ppermute | solution.py:432
  45.1 8.7 %collective-permute-start.18 = (bf16[8,448,128]{2,1,0:T(8,128)(2,1)S(1)}, bf16[8,448,128]{2,1,0:T(8,128)(2,1)S(1)}, u32[]{:S(2)}, u32[]{:S(2)}) collective-permute-start(bf16[8,448,128]{2,1,0:T(8,128)(2,1)S(1)} %pad_maximum_fusion.1.refs_4_), channel_id=1, source_target_pairs={{0,1},{1,0},{2,3},{3,2},{4,5},{5,4},{6,7},{7,6},{8,9},{9,8},{10,11... | collective-permute-start | bytes 2752520 | tf_op jit(solution)/shard_map/ppermute | solution.py:432
  80.1 7.7 %collective-permute-start.26 = (bf16[2,4,448,128]{3,2,1,0:T(8,128)(2,1)S(1)}, bf16[2,4,448,128]{3,2,1,0:T(8,128)(2,1)S(1)}, u32[]{:S(2)}, u32[]{:S(2)}) collective-permute-start(bf16[2,4,448,128]{3,2,1,0:T(8,128)(2,1)S(1)} %get-tuple-element.211), channel_id=1, source_target_pairs={{0,1},{1,0},{2,3},{3,2},{4,5},{5,4},{6,7},{7,6},{8,9},{9,8},{10,11... | collective-permute-start | bytes 2752520 | tf_op jit(solution)/shard_map/ppermute | solution.py:432
  80.7 7.8 %collective-permute-start.25 = (bf16[2,448,128]{2,1,0:T(8,128)(2,1)S(1)}, bf16[2,448,128]{2,1,0:T(8,128)(2,1)S(1)}, u32[]{:S(2)}, u32[]{:S(2)}) collective-permute-start(bf16[2,448,128]{2,1,0:T(8,128)(2,1)S(1)} %get-tuple-element.344), channel_id=1, source_target_pairs={{0,2},{1,3},{2,0},{3,1},{4,6},{5,7},{6,4},{7,5},{8,10},{9,11},{10,... | collective-permute-start | bytes 688136 | tf_op jit(solution)/shard_map/ppermute | solution.py:432
  82.4 7.5 %collective-permute-start.24 = (bf16[2,448,128]{2,1,0:T(8,128)(2,1)S(1)}, bf16[2,448,128]{2,1,0:T(8,128)(2,1)S(1)}, u32[]{:S(2)}, u32[]{:S(2)}) collective-permute-start(bf16[2,448,128]{2,1,0:T(8,128)(2,1)S(1)} %get-tuple-element.346), channel_id=1, source_target_pairs={{0,4},{1,5},{2,6},{3,7},{4,0},{5,1},{6,2},{7,3},{8,12},{9,13},{10,... | collective-permute-start | bytes 688136 | tf_op jit(solution)/shard_map/ppermute | solution.py:432
  90.0 10.3 %collective-permute-start.30 = (bf16[2,448,128]{2,1,0:T(8,128)(2,1)S(1)}, bf16[2,448,128]{2,1,0:T(8,128)(2,1)S(1)}, u32[]{:S(2)}, u32[]{:S(2)}) collective-permute-start(bf16[2,448,128]{2,1,0:T(8,128)(2,1)S(1)} %get-tuple-element.340), channel_id=1, source_target_pairs={{0,2},{1,3},{2,0},{3,1},{4,6},{5,7},{6,4},{7,5},{8,10},{9,11},{10,... | collective-permute-start | bytes 688136 | tf_op jit(solution)/shard_map/ppermute | solution.py:432
  90.8 9.5 %collective-permute-start.29 = (bf16[2,448,128]{2,1,0:T(8,128)(2,1)S(1)}, bf16[2,448,128]{2,1,0:T(8,128)(2,1)S(1)}, u32[]{:S(2)}, u32[]{:S(2)}) collective-permute-start(bf16[2,448,128]{2,1,0:T(8,128)(2,1)S(1)} %get-tuple-element.342), channel_id=1, source_target_pairs={{0,4},{1,5},{2,6},{3,7},{4,0},{5,1},{6,2},{7,3},{8,12},{9,13},{10,... | collective-permute-start | bytes 688136 | tf_op jit(solution)/shard_map/ppermute | solution.py:432
  92.3 8.0 %collective-permute-start.28 = (bf16[1,448,128]{2,1,0:T(8,128)(2,1)S(1)}, bf16[1,448,128]{2,1,0:T(8,128)(2,1)S(1)}, u32[]{:S(2)}, u32[]{:S(2)}) collective-permute-start(bf16[1,448,128]{2,1,0:T(8,128)(2,1)S(1)} %get-tuple-element.368), channel_id=1, source_target_pairs={{0,4},{1,5},{2,6},{3,7},{4,0},{5,1},{6,2},{7,3},{8,12},{9,13},{10,... | collective-permute-start | bytes 344072 | tf_op jit(solution)/shard_map/ppermute | solution.py:432
  93.1 7.1 %collective-permute-start.27 = (bf16[1,448,128]{2,1,0:T(8,128)(2,1)S(1)}, bf16[1,448,128]{2,1,0:T(8,128)(2,1)S(1)}, u32[]{:S(2)}, u32[]{:S(2)}) collective-permute-start(bf16[1,448,128]{2,1,0:T(8,128)(2,1)S(1)} %get-tuple-element.370), channel_id=1, source_target_pairs={{0,2},{1,3},{2,0},{3,1},{4,6},{5,7},{6,4},{7,5},{8,10},{9,11},{10,... | collective-permute-start | bytes 344072 | tf_op jit(solution)/shard_map/ppermute | solution.py:432
  100.4 7.9 %collective-permute-start.33 = (bf16[1,448,128]{2,1,0:T(8,128)(2,1)S(1)}, bf16[1,448,128]{2,1,0:T(8,128)(2,1)S(1)}, u32[]{:S(2)}, u32[]{:S(2)}) collective-permute-start(bf16[1,448,128]{2,1,0:T(8,128)(2,1)S(1)} %get-tuple-element.364), channel_id=1, source_target_pairs={{0,4},{1,5},{2,6},{3,7},{4,0},{5,1},{6,2},{7,3},{8,12},{9,13},{10,... | collective-permute-start | bytes 344072 | tf_op jit(solution)/shard_map/ppermute | solution.py:432
  109.4 10.3 %collective-permute-start.40 = (bf16[1,448,128]{2,1,0:T(8,128)(2,1)S(1)}, bf16[1,448,128]{2,1,0:T(8,128)(2,1)S(1)}, u32[]{:S(2)}, u32[]{:S(2)}) collective-permute-start(bf16[1,448,128]{2,1,0:T(8,128)(2,1)S(1)} %get-tuple-element.360), channel_id=1, source_target_pairs={{0,4},{1,5},{2,6},{3,7},{4,0},{5,1},{6,2},{7,3},{8,12},{9,13},{10,... | collective-permute-start | bytes 344072 | tf_op jit(solution)/shard_map/ppermute | solution.py:432
  110.5 9.2 %collective-permute-start.38 = (bf16[1,448,128]{2,1,0:T(8,128)(2,1)S(1)}, bf16[1,448,128]{2,1,0:T(8,128)(2,1)S(1)}, u32[]{:S(2)}, u32[]{:S(2)}) collective-permute-start(bf16[1,448,128]{2,1,0:T(8,128)(2,1)S(1)} %get-tuple-element.362), channel_id=1, source_target_pairs={{0,2},{1,3},{2,0},{3,1},{4,6},{5,7},{6,4},{7,5},{8,10},{9,11},{10,... | collective-permute-start | bytes 344072 | tf_op jit(solution)/shard_map/ppermute | solution.py:432
  114.8 9.0 %collective-permute-start.36 = (bf16[2,448,128]{2,1,0:T(8,128)(2,1)S(1)}, bf16[2,448,128]{2,1,0:T(8,128)(2,1)S(1)}, u32[]{:S(2)}, u32[]{:S(2)}) collective-permute-start(bf16[2,448,128]{2,1,0:T(8,128)(2,1)S(1)} %get-tuple-element.336), channel_id=1, source_target_pairs={{0,2},{1,3},{2,0},{3,1},{4,6},{5,7},{6,4},{7,5},{8,10},{9,11},{10,... | collective-permute-start | bytes 688136 | tf_op jit(solution)/shard_map/ppermute | solution.py:432
  115.9 7.9 %collective-permute-start.35 = (bf16[2,448,128]{2,1,0:T(8,128)(2,1)S(1)}, bf16[2,448,128]{2,1,0:T(8,128)(2,1)S(1)}, u32[]{:S(2)}, u32[]{:S(2)}) collective-permute-start(bf16[2,448,128]{2,1,0:T(8,128)(2,1)S(1)} %get-tuple-element.338), channel_id=1, source_target_pairs={{0,4},{1,5},{2,6},{3,7},{4,0},{5,1},{6,2},{7,3},{8,12},{9,13},{10,... | collective-permute-start | bytes 688136 | tf_op jit(solution)/shard_map/ppermute | solution.py:432
  (30 other events, 164.7 us)

commit v3 on v2

--- a/solution.py
+++ b/solution.py
@@ -382,25 +382,36 @@
     pack(flat, 0, rows_each, 0, places, near, far)
 
 
-def adam(rows_each, *refs):
-    offset, refs = refs[0], refs[1:]
-    parts0, parts1, refs = refs[:4], refs[4:6], refs[6:]
-    params, first_moment, second_moment, new_params, new_first, new_second = refs
-    shape = (rows_each, LANES)
+def updated(offset, grads, params, first_moment, second_moment):
+    shape = grads.shape
     row = lax.broadcasted_iota(jnp.int32, shape, 0)
     flags = matrix_flags((offset[0] + row) * LANES + lax.broadcasted_iota(jnp.int32, shape, 1))
     rate = jnp.where(flags, rate_matrix, rate_vector)
     decay = jnp.where(flags, decay_matrix, 0.0)
-    for layer, parts in enumerate((parts0, parts1)):
-        grads = sum(part[:rows_each, :].astype(f32) for part in parts)
-        first = beta_one * first_moment[:, layer, :] + (1.0 - beta_one) * grads
-        second = beta_two * second_moment[:, layer, :] + (1.0 - beta_two) * grads * grads
-        new_first[:, layer, :] = first
-        new_second[:, layer, :] = second
-        first_hat = first / (1.0 - beta_one**STEP)
-        second_hat = second / (1.0 - beta_two**STEP)
-        old = params[:, layer, :]
-        new_params[:, layer, :] = old - rate * (first_hat / (jnp.sqrt(second_hat) + adam_eps) + decay * old)
+    first = beta_one * first_moment + (1.0 - beta_one) * grads
+    second = beta_two * second_moment + (1.0 - beta_two) * grads * grads
+    first_hat = first / (1.0 - beta_one**STEP)
+    second_hat = second / (1.0 - beta_two**STEP)
+    moved = rate * (first_hat / (jnp.sqrt(second_hat) + adam_eps) + decay * params)
+    return params - moved, first, second
+
+
+def adam_early(rows_each, offset, kept, received, *refs):
+    old, new1, old0 = refs[:3], refs[3:6], refs[6:9]
+    grads = kept[:rows_each, :].astype(f32) + received[:rows_each, :].astype(f32)
+    for out, value in zip(new1, updated(offset, grads, *[ref[:, 1, :] for ref in old])):
+        out[...] = value
+    for out, ref in zip(old0, old):
+        out[...] = ref[:, 0, :]
+
+
+def adam_late(rows_each, offset, *refs):
+    parts, new1, old0, new = refs[:4], refs[4:7], refs[7:10], refs[10:13]
+    grads = sum(part[:rows_each, :].astype(f32) for part in parts)
+    for out, value in zip(new, updated(offset, grads, *[ref[...] for ref in old0])):
+        out[:, 0, :] = value
+    for out, ref in zip(new, new1):
+        out[:, 1, :] = ref[...]
 
 
 def call(body, name, inputs, outputs, scratch, scalars=0, flops=0):
@@ -684,16 +695,25 @@
     here, there = [[jnp.where(is_first, *pair), jnp.where(is_first, *pair[::-1])] for pair in (here, there)]
     values = exchanged(here[1][0], there[0][0], there[1][0])
     (nearby, other, far_other), received = values, top1[1]
-    updated = call(
-        functools.partial(adam, rows_each),
-        "adam",
-        [offset, here[0][0], nearby, other, far_other, top1[0], received, *map(alternating, (params, first_moment, second_moment))],
+    early = call(
+        functools.partial(adam_early, rows_each),
+        "adam_early",
+        [offset, top1[0], received, *map(alternating, (params, first_moment, second_moment))],
+        [((rows_each, LANES), f32)] * 6,
+        [],
+        scalars=1,
+    )
+    nearby, other, far_other, *early = together(nearby, other, far_other, *early)
+    results = call(
+        functools.partial(adam_late, rows_each),
+        "adam_late",
+        [offset, here[0][0], nearby, other, far_other, *early],
         [((rows_each, 2, LANES), f32)] * 3,
         [],
         scalars=1,
     )
     new_params, new_first, new_second = [
-        jnp.swapaxes(value, 0, 1).reshape(2, width) for value in updated
+        jnp.swapaxes(value, 0, 1).reshape(2, width) for value in results
     ]
     return (outputs, input_grad, new_params, new_first, new_second)
 

time: 143 us -> 142 us (level)
    pallas_call x11 -> x12, Pallas kernels: 45.6 us -> 46 us  [call(): pl.pallas_call(body, name=name, out_shape=shapes, in_specs=in_specs, out_...]
  transfers between devices with their start and end apart: 48 -> 48, of which waited for: 19 -> 19; matrix products, arithmetic and copies ran while one was open for 4% -> 4% of each run, Pallas kernels for 19% -> 20%
where the time goes in v3:
time: 142 us
  starting transfers between devices  52.1 us (37%)
  Pallas kernels  46 us (32%)
  waiting for transfers between devices  34.8 us (25%)
  other arithmetic  3.91 us (3%)
  local copies, waits for them, and re-layouts  3.68 us (3%)
  between operations  1.43 us (1%)
    ppermute x48, starting transfers between devices, swap(): return lax.ppermute(values, 'dp', [(i, i ^ mask) for i in range(size)])  52.1 us
    pallas_call x12, Pallas kernels, call(): pl.pallas_call(body, name=name, out_shape=shapes, in_specs=in_specs, out_...  46 us
    ppermute x48, waiting for transfers between devices, swap(): return lax.ppermute(values, 'dp', [(i, i ^ mask) for i in range(size)])  34.8 us
  transfers between devices with their start and end apart: 48, of which 19 were waited for; matrix products, arithmetic and copies ran while one was open for 4% of the time, Pallas kernels for 20%

profile of v3, /device:TPU:0, one launch (start us, length us, event | category | flops | bytes accessed | tf_op | source)
XLA Modules:
  0.0 141.9 jit_solution(26264891556424266)
XLA Ops:
  2.3 3.1 %collective-permute-start = (bf16[448,128]{1,0:T(8,128)(2,1)S(1)}, bf16[448,128]{1,0:T(8,128)(2,1)S(1)}, u32[]{:S(2)}, u32[]{:S(2)}) collective-permute-start(bf16[448,128]{1,0:T(8,128)(2,1)S(1)} %get-tuple-element.403), channel_id=1, source_target_pairs={{0,8},{1,9},{2,10},{3,11},{4,12},{5,13},{6,14},{7,15},{8,0},{9,1},... | collective-permute-start | bytes 344072 | tf_op jit(solution)/shard_map/ppermute | solution.py:443
  5.4 2.6 %collective-permute-start.1 = (bf16[448,128]{1,0:T(8,128)(2,1)S(1)}, bf16[448,128]{1,0:T(8,128)(2,1)S(1)}, u32[]{:S(2)}, u32[]{:S(2)}) collective-permute-start(bf16[448,128]{1,0:T(8,128)(2,1)S(1)} %get-tuple-element.403), channel_id=1, source_target_pairs={{0,16},{1,17},{2,18},{3,19},{4,20},{5,21},{6,22},{7,23},{8,24},{9,... | collective-permute-start | bytes 344072 | tf_op jit(solution)/shard_map/ppermute | solution.py:443
  9.7 2.4 %collective-permute-done.3 = bf16[1,160,128]{2,1,0:T(8,128)(2,1)S(1)} collective-permute-done((bf16[1,160,128]{2,1,0:T(8,128)(2,1)S(1)}, bf16[1,160,128]{2,1,0:T(8,128)(2,1)S(1)}, u32[]{:S(2)}, u32[]{:S(2)}) %collective-permute-start.3) | collective-permute-done | bytes 40992 | tf_op jit(solution)/shard_map/ppermute | solution.py:443
  12.0 5.0 %collective-permute-done.1 = bf16[448,128]{1,0:T(8,128)(2,1)S(1)} collective-permute-done((bf16[448,128]{1,0:T(8,128)(2,1)S(1)}, bf16[448,128]{1,0:T(8,128)(2,1)S(1)}, u32[]{:S(2)}, u32[]{:S(2)}) %collective-permute-start.1) | collective-permute-done | bytes 114720 | tf_op jit(solution)/shard_map/ppermute | solution.py:443
  20.8 2.8 %collective-permute-start.6 = (bf16[288,128]{1,0:T(8,128)(2,1)S(1)}, bf16[288,128]{1,0:T(8,128)(2,1)S(1)}, u32[]{:S(2)}, u32[]{:S(2)}) collective-permute-start(bf16[288,128]{1,0:T(8,128)(2,1)S(1)} %slice_bitcast_fusion.18), channel_id=1, source_target_pairs={{0,16},{1,17},{2,18},{3,19},{4,20},{5,21},{6,22},{7,23},{8,24},{9,... | collective-permute-start | bytes 221192 | tf_op jit(solution)/shard_map/ppermute | solution.py:443
  23.6 2.5 %collective-permute-done.6 = bf16[288,128]{1,0:T(8,128)(2,1)S(1)} collective-permute-done((bf16[288,128]{1,0:T(8,128)(2,1)S(1)}, bf16[288,128]{1,0:T(8,128)(2,1)S(1)}, u32[]{:S(2)}, u32[]{:S(2)}) %collective-permute-start.6) | collective-permute-done | bytes 73760 | tf_op jit(solution)/shard_map/ppermute | solution.py:443
  31.5 2.0 %collective-permute-done.8 = bf16[1,2,288,128]{3,2,0,1:T(8,128)(2,1)S(1)} collective-permute-done((bf16[1,2,288,128]{3,2,0,1:T(8,128)(2,1)S(1)}, bf16[1,2,288,128]{3,2,0,1:T(8,128)(2,1)S(1)}, u32[]{:S(2)}, u32[]{:S(2)}) %collective-permute-start.8) | collective-permute-done | bytes 147488 | tf_op jit(solution)/shard_map/ppermute | solution.py:443
  35.7 2.8 %collective-permute-done.13 = bf16[4,160,128]{2,1,0:T(8,128)(2,1)S(1)} collective-permute-done((bf16[4,160,128]{2,1,0:T(8,128)(2,1)S(1)}, bf16[4,160,128]{2,1,0:T(8,128)(2,1)S(1)}, u32[]{:S(2)}, u32[]{:S(2)}) %collective-permute-start.13) | collective-permute-done | bytes 163872 | tf_op jit(solution)/shard_map/ppermute | solution.py:443
  40.6 2.0 %collective-permute-start.17 = (bf16[4,2,160,128]{3,2,0,1:T(8,128)(2,1)S(1)}, bf16[4,2,160,128]{3,2,0,1:T(8,128)(2,1)S(1)}, u32[]{:S(2)}, u32[]{:S(2)}) collective-permute-start(bf16[4,2,160,128]{3,2,0,1:T(8,128)(2,1)S(1)} %pad_maximum_fusion.7), channel_id=1, source_target_pairs={{0,8},{1,9},{2,10},{3,11},{4,12},{5,13},{6,14},{7,15},{8,0},{9,1},... | collective-permute-start | bytes 983048 | tf_op jit(solution)/shard_map/ppermute | solution.py:443
  45.2 3.7 %attention_forward.2 = (f32[416,384]{1,0:T(8,128)S(1)}, bf16[384,1152]{1,0:T(8,128)(2,1)S(1)}, bf16[384,384]{1,0:T(8,128)(2,1)S(1)}, f32[8,384]{1,0:T(8,128)S(1)...) custom-call(s32[16]{0:T(128)S(1)} %get-tuple-element.167.refs_0_, ...), custom_call_target="tpu_custom_call" | custom-call | flops 623640576 | bytes 7243328 | tf_op jit(solution)/shard_map/attention_forward/pallas_call | solution.py:422
  48.9 2.9 %collective-permute-done.15 = bf16[4,288,128]{2,1,0:T(8,128)(2,1)S(1)} collective-permute-done((bf16[4,288,128]{2,1,0:T(8,128)(2,1)S(1)}, bf16[4,288,128]{2,1,0:T(8,128)(2,1)S(1)}, u32[]{:S(2)}, u32[]{:S(2)}) %collective-permute-start.15) | collective-permute-done | bytes 294944 | tf_op jit(solution)/shard_map/ppermute | solution.py:443
  53.8 4.3 %mlp_forward.2 = (bf16[384,1536]{1,0:T(8,128)(2,1)S(1)}, bf16[1536,384]{1,0:T(8,128)(2,1)S(1)}, f32[8,384]{1,0:T(8,128)S(1)}, bf16[416,384]{1,0:T(8,128)(2,1)S(1...) custom-call(s32[16]{0:T(128)S(1)} %get-tuple-element.167.refs_0_, ...), custom_call_target="tpu_custom_call" | custom-call | flops 981467136 | bytes 10195072 | tf_op jit(solution)/shard_map/mlp_forward/pallas_call | solution.py:422
  58.2 3.7 %attention_forward.3 = (bf16[384,1152]{1,0:T(8,128)(2,1)S(1)}, bf16[384,384]{1,0:T(8,128)(2,1)S(1)}, f32[8,384]{1,0:T(8,128)S(1)}, bf16[416,384]{1,0:T(8,128)(2,...) custom-call(s32[16]{0:T(128)S(1)} %get-tuple-element.167.refs_0_, ...), custom_call_target="tpu_custom_call" | custom-call | flops 623640576 | bytes 6940800 | tf_op jit(solution)/shard_map/attention_forward/pallas_call | solution.py:422
  61.9 4.6 %mlp_forward.3 = (bf16[384,1536]{1,0:T(8,128)(2,1)S(1)}, bf16[1536,384]{1,0:T(8,128)(2,1)S(1)}, f32[8,384]{1,0:T(8,128)S(1)}, bf16[416,384]{1,0:T(8,128)(2,1)S(1...) custom-call(s32[16]{0:T(128)S(1)} %get-tuple-element.167.refs_0_, ...), custom_call_target="tpu_custom_call" | custom-call | flops 981467136 | bytes 10161408 | tf_op jit(solution)/shard_map/mlp_forward/pallas_call | solution.py:422
  66.5 4.7 %mlp_backward.2 = (f32[2336,128]{1,0:T(8,128)S(1)}, bf16[2,4,448,128]{3,2,1,0:T(8,128)(2,1)S(1)}, bf16[2,4,448,128]{3,2,1,0:T(8,128)(2,1)S(1)}, f32[416,384]{1,0:T(8,128)S(1)}) custom-call(s32[2]{0:T(128)S(1)} %copy-done.3, s32[8]{0:T(128)S(1)} %get-tuple-element.165.refs_1_.refs_0_, s32[8]{0:T(128)S(1)} %get-tuple-element.166.refs_2_.refs_1_, ...), custom_call_target="tpu_custom_call" | custom-call | flops 1962934272 | bytes 9858632 | tf_op jit(solution)/shard_map/mlp_backward/pallas_call | solution.py:422
  71.4 5.5 %attention_backward.2 = (bf16[416,1152]{1,0:T(8,128)(2,1)S(1)}, f32[384,384]{1,0:T(8,128)S(1)}, f32[8,384]{1,0:T(8,128)S(1)}) custom-call(f32[416,384]{1,0:T(8,128)S(1)} %get-tuple-element.206.g_hidden.refs_2_, bf16[384,384]{1,0:T(8,128)(2,1)S(1)} %get-tuple-element.207.w_out, bf16[416,1152]{1,0:T(8,128)(2,1)S(1)} %get-tuple-element.208.qkv, ...), custom_call_target="tpu_custom_call" | custom-call | flops 511180800 | bytes 4810752 | tf_op jit(solution)/shard_map/attention_backward/pallas_call | solution.py:422
  77.0 3.1 %projection_backward.2 = (bf16[2,4,448,128]{3,2,1,0:T(8,128)(2,1)S(1)}, bf16[2,4,448,128]{3,2,1,0:T(8,128)(2,1)S(1)}, f32[416,384]{1,0:T(8,128)S(1)}) custom-call(s32[8]{0:T(128)S(1)} %get-tuple-element.165.refs_1_.refs_0_, s32[8]{0:T(128)S(1)} %get-tuple-element.166.refs_2_.refs_1_, f32[416,384]{1,0:T(8,128)S(1)} %get-tuple-element.206.g_hidden.refs_2_, ...), custom_call_target="tpu_custom_call" | custom-call | flops 736100352 | bytes 7725120 | tf_op jit(solution)/shard_map/projection_backward/pallas_call | solution.py:422
  83.0 4.7 %mlp_backward.3 = (f32[2336,128]{1,0:T(8,128)S(1)}, bf16[2,4,448,128]{3,2,1,0:T(8,128)(2,1)S(1)}, bf16[2,4,448,128]{3,2,1,0:T(8,128)(2,1)S(1)}, f32[416,384]{1,0:T(8,128)S(1)}) custom-call(s32[8]{0:T(128)S(1)} %get-tuple-element.165.refs_1_.refs_0_, s32[8]{0:T(128)S(1)} %get-tuple-element.166.refs_2_.refs_1_, f32[416,384]{1,0:T(8,128)S(1)} %get-tuple-element.227.refs_2_, ...), custom_call_target="tpu_custom_call" | custom-call | flops 1962934272 | bytes 10195008 | tf_op jit(solution)/shard_map/mlp_backward/pallas_call | solution.py:422
  94.8 5.5 %attention_backward.3 = (bf16[416,1152]{1,0:T(8,128)(2,1)S(1)}, f32[384,384]{1,0:T(8,128)S(1)}, f32[8,384]{1,0:T(8,128)S(1)}) custom-call(f32[416,384]{1,0:T(8,128)S(1)} %get-tuple-element.245.g_hidden.refs_2_, bf16[384,384]{1,0:T(8,128)(2,1)S(1)} %get-tuple-element.246.w_out, bf16[416,1152]{1,0:T(8,128)(2,1)S(1)} %get-tuple-element.247.qkv, ...), custom_call_target="tpu_custom_call" | custom-call | flops 511180800 | bytes 4810752 | tf_op jit(solution)/shard_map/attention_backward/pallas_call | solution.py:422
  105.2 3.1 %projection_backward.3 = (bf16[2,4,448,128]{3,2,1,0:T(8,128)(2,1)S(1)}, bf16[2,4,448,128]{3,2,1,0:T(8,128)(2,1)S(1)}, f32[2,197,384]{2,1,0:T(8,128)S(1)}) custom-call(s32[8]{0:T(128)S(1)} %get-tuple-element.165.refs_1_.refs_0_, s32[8]{0:T(128)S(1)} %get-tuple-element.166.refs_2_.refs_1_, f32[416,384]{1,0:T(8,128)S(1)} %get-tuple-element.245.g_hidden.refs_2_, ...), custom_call_target="tpu_custom_call" | custom-call | flops 736100352 | bytes 7691328 | tf_op jit(solution)/shard_map/projection_backward/pallas_call | solution.py:422
  111.5 3.0 %collective-permute-done.41 = bf16[2,448,128]{2,1,0:T(8,128)(2,1)S(1)} collective-permute-done((bf16[2,448,128]{2,1,0:T(8,128)(2,1)S(1)}, bf16[2,448,128]{2,1,0:T(8,128)(2,1)S(1)}, u32[]{:S(2)}, u32[]{:S(2)}) %collective-permute-start.41) | collective-permute-done | bytes 229408 | tf_op jit(solution)/shard_map/ppermute | solution.py:443
  117.0 2.7 %collective-permute-start.42 = (bf16[448,128]{1,0:T(8,128)(2,1)S(1)}, bf16[448,128]{1,0:T(8,128)(2,1)S(1)}, u32[]{:S(2)}, u32[]{:S(2)}) collective-permute-start(bf16[448,128]{1,0:T(8,128)(2,1)S(1)} %get-tuple-element.388), channel_id=1, source_target_pairs={{0,16},{1,17},{2,18},{3,19},{4,20},{5,21},{6,22},{7,23},{8,24},{9,... | collective-permute-start | bytes 344072 | tf_op jit(solution)/shard_map/ppermute | solution.py:443
  119.7 4.1 %collective-permute-done.42.received = bf16[448,128]{1,0:T(8,128)(2,1)S(1)} collective-permute-done((bf16[448,128]{1,0:T(8,128)(2,1)S(1)}, bf16[448,128]{1,0:T(8,128)(2,1)S(1)}, u32[]{:S(2)}, u32[]{:S(2)}) %collective-permute-start.42) | collective-permute-done | bytes 114720 | tf_op jit(solution)/shard_map/ppermute | solution.py:443
  130.0 2.1 %collective-permute-start.46 = (bf16[448,128]{1,0:T(8,128)(2,1)S(1)}, bf16[448,128]{1,0:T(8,128)(2,1)S(1)}, u32[]{:S(2)}, u32[]{:S(2)}) collective-permute-start(bf16[448,128]{1,0:T(8,128)(2,1)S(1)} %select_bitcast_fusion.3), channel_id=1, source_target_pairs={{0,16},{1,17},{2,18},{3,19},{4,20},{5,21},{6,22},{7,23},{8,24},{9,... | collective-permute-start | bytes 344072 | tf_op jit(solution)/shard_map/ppermute | solution.py:443
  (176 shorter events, 57.9 us)
Async XLA Ops:
  2.3 9.8 %collective-permute-start = (bf16[448,128]{1,0:T(8,128)(2,1)S(1)}, bf16[448,128]{1,0:T(8,128)(2,1)S(1)}, u32[]{:S(2)}, u32[]{:S(2)}) collective-permute-start(bf16[448,128]{1,0:T(8,128)(2,1)S(1)} %get-tuple-element.403), channel_id=1, source_target_pairs={{0,8},{1,9},{2,10},{3,11},{4,12},{5,13},{6,14},{7,15},{8,0},{9,1},... | collective-permute-start | bytes 344072 | tf_op jit(solution)/shard_map/ppermute | solution.py:443
  5.4 11.7 %collective-permute-start.1 = (bf16[448,128]{1,0:T(8,128)(2,1)S(1)}, bf16[448,128]{1,0:T(8,128)(2,1)S(1)}, u32[]{:S(2)}, u32[]{:S(2)}) collective-permute-start(bf16[448,128]{1,0:T(8,128)(2,1)S(1)} %get-tuple-element.403), channel_id=1, source_target_pairs={{0,16},{1,17},{2,18},{3,19},{4,20},{5,21},{6,22},{7,23},{8,24},{9,... | collective-permute-start | bytes 344072 | tf_op jit(solution)/shard_map/ppermute | solution.py:443
  8.0 9.1 %collective-permute-start.2 = (bf16[448,128]{1,0:T(8,128)(2,1)S(1)}, bf16[448,128]{1,0:T(8,128)(2,1)S(1)}, u32[]{:S(2)}, u32[]{:S(2)}) collective-permute-start(bf16[448,128]{1,0:T(8,128)(2,1)S(1)} %get-tuple-element.403), channel_id=1, source_target_pairs={{0,24},{1,25},{2,26},{3,27},{4,28},{5,29},{6,30},{7,31},{8,16},{9,... | collective-permute-start | bytes 344072 | tf_op jit(solution)/shard_map/ppermute | solution.py:443
  17.1 8.9 %collective-permute-start.4 = (bf16[2,448,128]{2,1,0:T(8,128)(2,1)S(1)}, bf16[2,448,128]{2,1,0:T(8,128)(2,1)S(1)}, u32[]{:S(2)}, u32[]{:S(2)}) collective-permute-start(bf16[2,448,128]{2,1,0:T(8,128)(2,1)S(1)} %get-tuple-element.379), channel_id=1, source_target_pairs={{0,2},{1,3},{2,0},{3,1},{4,6},{5,7},{6,4},{7,5},{8,10},{9,11},{10,... | collective-permute-start | bytes 688136 | tf_op jit(solution)/shard_map/ppermute | solution.py:443
  18.7 7.4 %collective-permute-start.5 = (bf16[2,448,128]{2,1,0:T(8,128)(2,1)S(1)}, bf16[2,448,128]{2,1,0:T(8,128)(2,1)S(1)}, u32[]{:S(2)}, u32[]{:S(2)}) collective-permute-start(bf16[2,448,128]{2,1,0:T(8,128)(2,1)S(1)} %get-tuple-element.378), channel_id=1, source_target_pairs={{0,4},{1,5},{2,6},{3,7},{4,0},{5,1},{6,2},{7,3},{8,12},{9,13},{10,... | collective-permute-start | bytes 688136 | tf_op jit(solution)/shard_map/ppermute | solution.py:443
  26.1 14.2 %collective-permute-start.10 = (bf16[4,448,128]{2,1,0:T(8,128)(2,1)S(1)}, bf16[4,448,128]{2,1,0:T(8,128)(2,1)S(1)}, u32[]{:S(2)}, u32[]{:S(2)}) collective-permute-start(bf16[4,448,128]{2,1,0:T(8,128)(2,1)S(1)} %pad_maximum_fusion.6), channel_id=1, source_target_pairs={{0,2},{1,3},{2,0},{3,1},{4,6},{5,7},{6,4},{7,5},{8,10},{9,11},{10,... | collective-permute-start | bytes 1376264 | tf_op jit(solution)/shard_map/ppermute | solution.py:443
  26.8 13.6 %collective-permute-start.9 = (bf16[4,448,128]{2,1,0:T(8,128)(2,1)S(1)}, bf16[4,448,128]{2,1,0:T(8,128)(2,1)S(1)}, u32[]{:S(2)}, u32[]{:S(2)}) collective-permute-start(bf16[4,448,128]{2,1,0:T(8,128)(2,1)S(1)} %pad_maximum_fusion.5), channel_id=1, source_target_pairs={{0,4},{1,5},{2,6},{3,7},{4,0},{5,1},{6,2},{7,3},{8,12},{9,13},{10,... | collective-permute-start | bytes 1376264 | tf_op jit(solution)/shard_map/ppermute | solution.py:443
  30.4 8.0 %collective-permute-start.13 = (bf16[4,160,128]{2,1,0:T(8,128)(2,1)S(1)}, bf16[4,160,128]{2,1,0:T(8,128)(2,1)S(1)}, u32[]{:S(2)}, u32[]{:S(2)}) collective-permute-start(bf16[4,160,128]{2,1,0:T(8,128)(2,1)S(1)} %pad_maximum_fusion.13), channel_id=1, source_target_pairs={{0,16},{1,17},{2,18},{3,19},{4,20},{5,21},{6,22},{7,23},{8,24},{9,... | collective-permute-start | bytes 491528 | tf_op jit(solution)/shard_map/ppermute | solution.py:443
  40.6 11.7 %collective-permute-start.17 = (bf16[4,2,160,128]{3,2,0,1:T(8,128)(2,1)S(1)}, bf16[4,2,160,128]{3,2,0,1:T(8,128)(2,1)S(1)}, u32[]{:S(2)}, u32[]{:S(2)}) collective-permute-start(bf16[4,2,160,128]{3,2,0,1:T(8,128)(2,1)S(1)} %pad_maximum_fusion.7), channel_id=1, source_target_pairs={{0,8},{1,9},{2,10},{3,11},{4,12},{5,13},{6,14},{7,15},{8,0},{9,1},... | collective-permute-start | bytes 983048 | tf_op jit(solution)/shard_map/ppermute | solution.py:443
  42.6 9.2 %collective-permute-start.15 = (bf16[4,288,128]{2,1,0:T(8,128)(2,1)S(1)}, bf16[4,288,128]{2,1,0:T(8,128)(2,1)S(1)}, u32[]{:S(2)}, u32[]{:S(2)}) collective-permute-start(bf16[4,288,128]{2,1,0:T(8,128)(2,1)S(1)} %pad_maximum_fusion.8), channel_id=1, source_target_pairs={{0,4},{1,5},{2,6},{3,7},{4,0},{5,1},{6,2},{7,3},{8,12},{9,13},{10,... | collective-permute-start | bytes 884744 | tf_op jit(solution)/shard_map/ppermute | solution.py:443
  43.4 8.9 %collective-permute-start.16 = (bf16[4,288,128]{2,1,0:T(8,128)(2,1)S(1)}, bf16[4,288,128]{2,1,0:T(8,128)(2,1)S(1)}, u32[]{:S(2)}, u32[]{:S(2)}) collective-permute-start(bf16[4,288,128]{2,1,0:T(8,128)(2,1)S(1)} %pad_maximum_fusion.9), channel_id=1, source_target_pairs={{0,2},{1,3},{2,0},{3,1},{4,6},{5,7},{6,4},{7,5},{8,10},{9,11},{10,... | collective-permute-start | bytes 884744 | tf_op jit(solution)/shard_map/ppermute | solution.py:443
  45.1 8.7 %collective-permute-start.18 = (bf16[8,448,128]{2,1,0:T(8,128)(2,1)S(1)}, bf16[8,448,128]{2,1,0:T(8,128)(2,1)S(1)}, u32[]{:S(2)}, u32[]{:S(2)}) collective-permute-start(bf16[8,448,128]{2,1,0:T(8,128)(2,1)S(1)} %pad_maximum_fusion.1.refs_4_), channel_id=1, source_target_pairs={{0,1},{1,0},{2,3},{3,2},{4,5},{5,4},{6,7},{7,6},{8,9},{9,8},{10,11... | collective-permute-start | bytes 2752520 | tf_op jit(solution)/shard_map/ppermute | solution.py:443
  80.1 7.7 %collective-permute-start.26 = (bf16[2,4,448,128]{3,2,1,0:T(8,128)(2,1)S(1)}, bf16[2,4,448,128]{3,2,1,0:T(8,128)(2,1)S(1)}, u32[]{:S(2)}, u32[]{:S(2)}) collective-permute-start(bf16[2,4,448,128]{3,2,1,0:T(8,128)(2,1)S(1)} %get-tuple-element.226), channel_id=1, source_target_pairs={{0,1},{1,0},{2,3},{3,2},{4,5},{5,4},{6,7},{7,6},{8,9},{9,8},{10,11... | collective-permute-start | bytes 2752520 | tf_op jit(solution)/shard_map/ppermute | solution.py:443
  80.7 7.8 %collective-permute-start.25 = (bf16[2,448,128]{2,1,0:T(8,128)(2,1)S(1)}, bf16[2,448,128]{2,1,0:T(8,128)(2,1)S(1)}, u32[]{:S(2)}, u32[]{:S(2)}) collective-permute-start(bf16[2,448,128]{2,1,0:T(8,128)(2,1)S(1)} %get-tuple-element.374), channel_id=1, source_target_pairs={{0,2},{1,3},{2,0},{3,1},{4,6},{5,7},{6,4},{7,5},{8,10},{9,11},{10,... | collective-permute-start | bytes 688136 | tf_op jit(solution)/shard_map/ppermute | solution.py:443
  82.4 7.5 %collective-permute-start.24 = (bf16[2,448,128]{2,1,0:T(8,128)(2,1)S(1)}, bf16[2,448,128]{2,1,0:T(8,128)(2,1)S(1)}, u32[]{:S(2)}, u32[]{:S(2)}) collective-permute-start(bf16[2,448,128]{2,1,0:T(8,128)(2,1)S(1)} %get-tuple-element.376), channel_id=1, source_target_pairs={{0,4},{1,5},{2,6},{3,7},{4,0},{5,1},{6,2},{7,3},{8,12},{9,13},{10,... | collective-permute-start | bytes 688136 | tf_op jit(solution)/shard_map/ppermute | solution.py:443
  90.0 10.3 %collective-permute-start.30 = (bf16[2,448,128]{2,1,0:T(8,128)(2,1)S(1)}, bf16[2,448,128]{2,1,0:T(8,128)(2,1)S(1)}, u32[]{:S(2)}, u32[]{:S(2)}) collective-permute-start(bf16[2,448,128]{2,1,0:T(8,128)(2,1)S(1)} %get-tuple-element.370), channel_id=1, source_target_pairs={{0,2},{1,3},{2,0},{3,1},{4,6},{5,7},{6,4},{7,5},{8,10},{9,11},{10,... | collective-permute-start | bytes 688136 | tf_op jit(solution)/shard_map/ppermute | solution.py:443
  90.8 9.5 %collective-permute-start.29 = (bf16[2,448,128]{2,1,0:T(8,128)(2,1)S(1)}, bf16[2,448,128]{2,1,0:T(8,128)(2,1)S(1)}, u32[]{:S(2)}, u32[]{:S(2)}) collective-permute-start(bf16[2,448,128]{2,1,0:T(8,128)(2,1)S(1)} %get-tuple-element.372), channel_id=1, source_target_pairs={{0,4},{1,5},{2,6},{3,7},{4,0},{5,1},{6,2},{7,3},{8,12},{9,13},{10,... | collective-permute-start | bytes 688136 | tf_op jit(solution)/shard_map/ppermute | solution.py:443
  92.3 8.0 %collective-permute-start.28 = (bf16[1,448,128]{2,1,0:T(8,128)(2,1)S(1)}, bf16[1,448,128]{2,1,0:T(8,128)(2,1)S(1)}, u32[]{:S(2)}, u32[]{:S(2)}) collective-permute-start(bf16[1,448,128]{2,1,0:T(8,128)(2,1)S(1)} %get-tuple-element.398), channel_id=1, source_target_pairs={{0,4},{1,5},{2,6},{3,7},{4,0},{5,1},{6,2},{7,3},{8,12},{9,13},{10,... | collective-permute-start | bytes 344072 | tf_op jit(solution)/shard_map/ppermute | solution.py:443
  93.1 7.1 %collective-permute-start.27 = (bf16[1,448,128]{2,1,0:T(8,128)(2,1)S(1)}, bf16[1,448,128]{2,1,0:T(8,128)(2,1)S(1)}, u32[]{:S(2)}, u32[]{:S(2)}) collective-permute-start(bf16[1,448,128]{2,1,0:T(8,128)(2,1)S(1)} %get-tuple-element.400), channel_id=1, source_target_pairs={{0,2},{1,3},{2,0},{3,1},{4,6},{5,7},{6,4},{7,5},{8,10},{9,11},{10,... | collective-permute-start | bytes 344072 | tf_op jit(solution)/shard_map/ppermute | solution.py:443
  100.4 7.9 %collective-permute-start.33 = (bf16[1,448,128]{2,1,0:T(8,128)(2,1)S(1)}, bf16[1,448,128]{2,1,0:T(8,128)(2,1)S(1)}, u32[]{:S(2)}, u32[]{:S(2)}) collective-permute-start(bf16[1,448,128]{2,1,0:T(8,128)(2,1)S(1)} %get-tuple-element.394), channel_id=1, source_target_pairs={{0,4},{1,5},{2,6},{3,7},{4,0},{5,1},{6,2},{7,3},{8,12},{9,13},{10,... | collective-permute-start | bytes 344072 | tf_op jit(solution)/shard_map/ppermute | solution.py:443
  109.4 10.3 %collective-permute-start.40 = (bf16[1,448,128]{2,1,0:T(8,128)(2,1)S(1)}, bf16[1,448,128]{2,1,0:T(8,128)(2,1)S(1)}, u32[]{:S(2)}, u32[]{:S(2)}) collective-permute-start(bf16[1,448,128]{2,1,0:T(8,128)(2,1)S(1)} %get-tuple-element.390), channel_id=1, source_target_pairs={{0,4},{1,5},{2,6},{3,7},{4,0},{5,1},{6,2},{7,3},{8,12},{9,13},{10,... | collective-permute-start | bytes 344072 | tf_op jit(solution)/shard_map/ppermute | solution.py:443
  110.5 9.2 %collective-permute-start.38 = (bf16[1,448,128]{2,1,0:T(8,128)(2,1)S(1)}, bf16[1,448,128]{2,1,0:T(8,128)(2,1)S(1)}, u32[]{:S(2)}, u32[]{:S(2)}) collective-permute-start(bf16[1,448,128]{2,1,0:T(8,128)(2,1)S(1)} %get-tuple-element.392), channel_id=1, source_target_pairs={{0,2},{1,3},{2,0},{3,1},{4,6},{5,7},{6,4},{7,5},{8,10},{9,11},{10,... | collective-permute-start | bytes 344072 | tf_op jit(solution)/shard_map/ppermute | solution.py:443
  114.8 9.0 %collective-permute-start.36 = (bf16[2,448,128]{2,1,0:T(8,128)(2,1)S(1)}, bf16[2,448,128]{2,1,0:T(8,128)(2,1)S(1)}, u32[]{:S(2)}, u32[]{:S(2)}) collective-permute-start(bf16[2,448,128]{2,1,0:T(8,128)(2,1)S(1)} %get-tuple-element.366), channel_id=1, source_target_pairs={{0,2},{1,3},{2,0},{3,1},{4,6},{5,7},{6,4},{7,5},{8,10},{9,11},{10,... | collective-permute-start | bytes 688136 | tf_op jit(solution)/shard_map/ppermute | solution.py:443
  115.9 7.9 %collective-permute-start.35 = (bf16[2,448,128]{2,1,0:T(8,128)(2,1)S(1)}, bf16[2,448,128]{2,1,0:T(8,128)(2,1)S(1)}, u32[]{:S(2)}, u32[]{:S(2)}) collective-permute-start(bf16[2,448,128]{2,1,0:T(8,128)(2,1)S(1)} %get-tuple-element.368), channel_id=1, source_target_pairs={{0,4},{1,5},{2,6},{3,7},{4,0},{5,1},{6,2},{7,3},{8,12},{9,13},{10,... | collective-permute-start | bytes 688136 | tf_op jit(solution)/shard_map/ppermute | solution.py:443
  (30 other events, 155.7 us)

commit v4 on v3

--- a/solution.py
+++ b/solution.py
@@ -23,9 +23,9 @@
 PAIRS = HEADS // 2
 COST = 1
 FORWARD_UNROLL = 6
-BACKWARD_UNROLL = 2
-VMEM_LIMIT = 10 * 1024 * 1024
-BLOCK = 512
+BACKWARD_UNROLL = 3
+VMEM_LIMIT = 14 * 1024 * 1024
+BLOCK = 768
 
 eps_norm = 1e-06
 beta_one = 0.9
@@ -198,10 +198,7 @@
     normed_one[...] = (unit * gain + shift).astype(bf16)
     bias_query = vectors[2:3, :]
     bias = jnp.concatenate([bias_query, jnp.zeros_like(bias_query), vectors[3:4, :]], axis=1)
-    for t in range(3):
-        cols = slice(t * D, (t + 1) * D)
-        product = dot_nn(normed_one[...], w_qkv[:, cols]) + bias[:, cols]
-        qkv[:, cols] = product.astype(bf16)
+    qkv[...] = (dot_nn(normed_one[...], w_qkv[...]) + bias).astype(bf16)
 
     def step(at, carry):
         rows, cols = pair_slices(at)
@@ -362,13 +359,8 @@
     write_vector(flat, ROW["bias_query"], query_sum)
     value_sum = jnp.sum(d_qkv[:, 2 * D :].astype(f32), 0, keepdims=True)
     write_vector(flat, ROW["bias_value"], value_sum)
-    d_normed = jnp.zeros((TOKENS, D), f32)
-    for t in range(3):
-        cols = slice(t * D, (t + 1) * D)
-        part = d_qkv[:, cols]
-        row = ROW["w_qkv"] + t * (D // LANES)
-        write_matrix(flat, row, dot_tn(normed_one[...], part), 3 * D // LANES)
-        d_normed += dot_nt(part, w_qkv[:, cols])
+    write_matrix(flat, ROW["w_qkv"], dot_tn(normed_one[...], d_qkv[...]), 3 * D // LANES)
+    d_normed = dot_nt(d_qkv[...], w_qkv[...])
     unit, rstd = normalize(state[...])
     back, gain_grad, shift_grad = norm_back(d_normed, unit, rstd, vectors[0:1, :])
     write_vector(flat, ROW["ln1_gain"], gain_grad)

time: 142 us -> 140 us (0.986)
  Pallas kernels: 46 us -> 43.9 us
    pallas_call x12, Pallas kernels: 46 us -> 43.9 us  [call(): pl.pallas_call(body, name=name, out_shape=shapes, in_specs=in_specs, out_...]
  transfers between devices with their start and end apart: 48 -> 48, of which waited for: 19 -> 19; matrix products, arithmetic and copies ran while one was open for 4% -> 4% of each run, Pallas kernels for 20% -> 19%
where the time goes in v4:
time: 140 us
  starting transfers between devices  52.4 us (37%)
  Pallas kernels  43.9 us (31%)
  waiting for transfers between devices  35 us (25%)
  other arithmetic  3.91 us (3%)
  local copies, waits for them, and re-layouts  3.68 us (3%)
  between operations  1.43 us (1%)
    ppermute x48, starting transfers between devices, swap(): return lax.ppermute(values, 'dp', [(i, i ^ mask) for i in range(size)])  52.4 us
    pallas_call x12, Pallas kernels, call(): pl.pallas_call(body, name=name, out_shape=shapes, in_specs=in_specs, out_...  43.9 us
    ppermute x48, waiting for transfers between devices, swap(): return lax.ppermute(values, 'dp', [(i, i ^ mask) for i in range(size)])  35 us
  transfers between devices with their start and end apart: 48, of which 19 were waited for; matrix products, arithmetic and copies ran while one was open for 4% of the time, Pallas kernels for 19%

profile of v4, /device:TPU:0, one launch (start us, length us, event | category | flops | bytes accessed | tf_op | source)
XLA Modules:
  0.0 140.3 jit_solution(7191098979353999519)
XLA Ops:
  2.3 3.1 %collective-permute-start = (bf16[448,128]{1,0:T(8,128)(2,1)S(1)}, bf16[448,128]{1,0:T(8,128)(2,1)S(1)}, u32[]{:S(2)}, u32[]{:S(2)}) collective-permute-start(bf16[448,128]{1,0:T(8,128)(2,1)S(1)} %get-tuple-element.403), channel_id=1, source_target_pairs={{0,8},{1,9},{2,10},{3,11},{4,12},{5,13},{6,14},{7,15},{8,0},{9,1},... | collective-permute-start | bytes 344072 | tf_op jit(solution)/shard_map/ppermute | solution.py:435
  5.4 2.6 %collective-permute-start.1 = (bf16[448,128]{1,0:T(8,128)(2,1)S(1)}, bf16[448,128]{1,0:T(8,128)(2,1)S(1)}, u32[]{:S(2)}, u32[]{:S(2)}) collective-permute-start(bf16[448,128]{1,0:T(8,128)(2,1)S(1)} %get-tuple-element.403), channel_id=1, source_target_pairs={{0,16},{1,17},{2,18},{3,19},{4,20},{5,21},{6,22},{7,23},{8,24},{9,... | collective-permute-start | bytes 344072 | tf_op jit(solution)/shard_map/ppermute | solution.py:435
  9.7 2.4 %collective-permute-done.3 = bf16[1,160,128]{2,1,0:T(8,128)(2,1)S(1)} collective-permute-done((bf16[1,160,128]{2,1,0:T(8,128)(2,1)S(1)}, bf16[1,160,128]{2,1,0:T(8,128)(2,1)S(1)}, u32[]{:S(2)}, u32[]{:S(2)}) %collective-permute-start.3) | collective-permute-done | bytes 40992 | tf_op jit(solution)/shard_map/ppermute | solution.py:435
  12.0 5.0 %collective-permute-done.1 = bf16[448,128]{1,0:T(8,128)(2,1)S(1)} collective-permute-done((bf16[448,128]{1,0:T(8,128)(2,1)S(1)}, bf16[448,128]{1,0:T(8,128)(2,1)S(1)}, u32[]{:S(2)}, u32[]{:S(2)}) %collective-permute-start.1) | collective-permute-done | bytes 114720 | tf_op jit(solution)/shard_map/ppermute | solution.py:435
  20.8 2.8 %collective-permute-start.6 = (bf16[288,128]{1,0:T(8,128)(2,1)S(1)}, bf16[288,128]{1,0:T(8,128)(2,1)S(1)}, u32[]{:S(2)}, u32[]{:S(2)}) collective-permute-start(bf16[288,128]{1,0:T(8,128)(2,1)S(1)} %slice_bitcast_fusion.18), channel_id=1, source_target_pairs={{0,16},{1,17},{2,18},{3,19},{4,20},{5,21},{6,22},{7,23},{8,24},{9,... | collective-permute-start | bytes 221192 | tf_op jit(solution)/shard_map/ppermute | solution.py:435
  23.6 2.5 %collective-permute-done.6 = bf16[288,128]{1,0:T(8,128)(2,1)S(1)} collective-permute-done((bf16[288,128]{1,0:T(8,128)(2,1)S(1)}, bf16[288,128]{1,0:T(8,128)(2,1)S(1)}, u32[]{:S(2)}, u32[]{:S(2)}) %collective-permute-start.6) | collective-permute-done | bytes 73760 | tf_op jit(solution)/shard_map/ppermute | solution.py:435
  28.4 2.0 %collective-permute-start.8 = (bf16[1,2,288,128]{3,2,0,1:T(8,128)(2,1)S(1)}, bf16[1,2,288,128]{3,2,0,1:T(8,128)(2,1)S(1)}, u32[]{:S(2)}, u32[]{:S(2)}) collective-permute-start(bf16[1,2,288,128]{3,2,0,1:T(8,128)(2,1)S(1)} %maximum_bitcast_fusion), channel_id=1, source_target_pairs={{0,8},{1,9},{2,10},{3,11},{4,12},{5,13},{6,14},{7,15},{8,0},{9,1},... | collective-permute-start | bytes 442376 | tf_op jit(solution)/shard_map/ppermute | solution.py:435
  31.6 2.0 %collective-permute-done.8 = bf16[1,2,288,128]{3,2,0,1:T(8,128)(2,1)S(1)} collective-permute-done((bf16[1,2,288,128]{3,2,0,1:T(8,128)(2,1)S(1)}, bf16[1,2,288,128]{3,2,0,1:T(8,128)(2,1)S(1)}, u32[]{:S(2)}, u32[]{:S(2)}) %collective-permute-start.8) | collective-permute-done | bytes 147488 | tf_op jit(solution)/shard_map/ppermute | solution.py:435
  35.7 2.8 %collective-permute-done.13 = bf16[4,160,128]{2,1,0:T(8,128)(2,1)S(1)} collective-permute-done((bf16[4,160,128]{2,1,0:T(8,128)(2,1)S(1)}, bf16[4,160,128]{2,1,0:T(8,128)(2,1)S(1)}, u32[]{:S(2)}, u32[]{:S(2)}) %collective-permute-start.13) | collective-permute-done | bytes 163872 | tf_op jit(solution)/shard_map/ppermute | solution.py:435
  45.2 3.6 %attention_forward.2 = (f32[416,384]{1,0:T(8,128)S(1)}, bf16[384,1152]{1,0:T(8,128)(2,1)S(1)}, bf16[384,384]{1,0:T(8,128)(2,1)S(1)}, f32[8,384]{1,0:T(8,128)S(1)...) custom-call(s32[16]{0:T(128)S(1)} %get-tuple-element.167.refs_0_, ...), custom_call_target="tpu_custom_call" | custom-call | flops 623640576 | bytes 7243328 | tf_op jit(solution)/shard_map/attention_forward/pallas_call | solution.py:414
  48.8 3.0 %collective-permute-done.15 = bf16[4,288,128]{2,1,0:T(8,128)(2,1)S(1)} collective-permute-done((bf16[4,288,128]{2,1,0:T(8,128)(2,1)S(1)}, bf16[4,288,128]{2,1,0:T(8,128)(2,1)S(1)}, u32[]{:S(2)}, u32[]{:S(2)}) %collective-permute-start.15) | collective-permute-done | bytes 294944 | tf_op jit(solution)/shard_map/ppermute | solution.py:435
  53.8 4.0 %mlp_forward.2 = (bf16[384,1536]{1,0:T(8,128)(2,1)S(1)}, bf16[1536,384]{1,0:T(8,128)(2,1)S(1)}, f32[8,384]{1,0:T(8,128)S(1)}, bf16[416,384]{1,0:T(8,128)(2,1)S(1...) custom-call(s32[16]{0:T(128)S(1)} %get-tuple-element.167.refs_0_, ...), custom_call_target="tpu_custom_call" | custom-call | flops 981467136 | bytes 10195072 | tf_op jit(solution)/shard_map/mlp_forward/pallas_call | solution.py:414
  57.8 3.6 %attention_forward.3 = (bf16[384,1152]{1,0:T(8,128)(2,1)S(1)}, bf16[384,384]{1,0:T(8,128)(2,1)S(1)}, f32[8,384]{1,0:T(8,128)S(1)}, bf16[416,384]{1,0:T(8,128)(2,...) custom-call(s32[16]{0:T(128)S(1)} %get-tuple-element.167.refs_0_, ...), custom_call_target="tpu_custom_call" | custom-call | flops 623640576 | bytes 6940800 | tf_op jit(solution)/shard_map/attention_forward/pallas_call | solution.py:414
  61.5 4.2 %mlp_forward.3 = (bf16[384,1536]{1,0:T(8,128)(2,1)S(1)}, bf16[1536,384]{1,0:T(8,128)(2,1)S(1)}, f32[8,384]{1,0:T(8,128)S(1)}, bf16[416,384]{1,0:T(8,128)(2,1)S(1...) custom-call(s32[16]{0:T(128)S(1)} %get-tuple-element.167.refs_0_, ...), custom_call_target="tpu_custom_call" | custom-call | flops 981467136 | bytes 10161408 | tf_op jit(solution)/shard_map/mlp_forward/pallas_call | solution.py:414
  65.7 4.5 %mlp_backward.2 = (f32[2336,128]{1,0:T(8,128)S(1)}, bf16[2,4,448,128]{3,2,1,0:T(8,128)(2,1)S(1)}, bf16[2,4,448,128]{3,2,1,0:T(8,128)(2,1)S(1)}, f32[416,384]{1,0:T(8,128)S(1)}) custom-call(s32[2]{0:T(128)S(1)} %copy-done.3, s32[8]{0:T(128)S(1)} %get-tuple-element.165.refs_1_.refs_0_, s32[8]{0:T(128)S(1)} %get-tuple-element.166.refs_2_.refs_1_, ...), custom_call_target="tpu_custom_call" | custom-call | flops 1962934272 | bytes 9858632 | tf_op jit(solution)/shard_map/mlp_backward/pallas_call | solution.py:414
  70.4 5.3 %attention_backward.2 = (bf16[416,1152]{1,0:T(8,128)(2,1)S(1)}, f32[384,384]{1,0:T(8,128)S(1)}, f32[8,384]{1,0:T(8,128)S(1)}) custom-call(f32[416,384]{1,0:T(8,128)S(1)} %get-tuple-element.206.g_hidden.refs_2_, bf16[384,384]{1,0:T(8,128)(2,1)S(1)} %get-tuple-element.207.w_out, bf16[416,1152]{1,0:T(8,128)(2,1)S(1)} %get-tuple-element.208.qkv, ...), custom_call_target="tpu_custom_call" | custom-call | flops 511180800 | bytes 4810752 | tf_op jit(solution)/shard_map/attention_backward/pallas_call | solution.py:414
  75.9 2.8 %projection_backward.2 = (bf16[2,4,448,128]{3,2,1,0:T(8,128)(2,1)S(1)}, bf16[2,4,448,128]{3,2,1,0:T(8,128)(2,1)S(1)}, f32[416,384]{1,0:T(8,128)S(1)}) custom-call(s32[8]{0:T(128)S(1)} %get-tuple-element.165.refs_1_.refs_0_, s32[8]{0:T(128)S(1)} %get-tuple-element.166.refs_2_.refs_1_, f32[416,384]{1,0:T(8,128)S(1)} %get-tuple-element.206.g_hidden.refs_2_, ...), custom_call_target="tpu_custom_call" | custom-call | flops 736100352 | bytes 7725120 | tf_op jit(solution)/shard_map/projection_backward/pallas_call | solution.py:414
  81.5 4.5 %mlp_backward.3 = (f32[2336,128]{1,0:T(8,128)S(1)}, bf16[2,4,448,128]{3,2,1,0:T(8,128)(2,1)S(1)}, bf16[2,4,448,128]{3,2,1,0:T(8,128)(2,1)S(1)}, f32[416,384]{1,0:T(8,128)S(1)}) custom-call(s32[8]{0:T(128)S(1)} %get-tuple-element.165.refs_1_.refs_0_, s32[8]{0:T(128)S(1)} %get-tuple-element.166.refs_2_.refs_1_, f32[416,384]{1,0:T(8,128)S(1)} %get-tuple-element.227.refs_2_, ...), custom_call_target="tpu_custom_call" | custom-call | flops 1962934272 | bytes 10195008 | tf_op jit(solution)/shard_map/mlp_backward/pallas_call | solution.py:414
  93.4 5.3 %attention_backward.3 = (bf16[416,1152]{1,0:T(8,128)(2,1)S(1)}, f32[384,384]{1,0:T(8,128)S(1)}, f32[8,384]{1,0:T(8,128)S(1)}) custom-call(f32[416,384]{1,0:T(8,128)S(1)} %get-tuple-element.245.g_hidden.refs_2_, bf16[384,384]{1,0:T(8,128)(2,1)S(1)} %get-tuple-element.246.w_out, bf16[416,1152]{1,0:T(8,128)(2,1)S(1)} %get-tuple-element.247.qkv, ...), custom_call_target="tpu_custom_call" | custom-call | flops 511180800 | bytes 4810752 | tf_op jit(solution)/shard_map/attention_backward/pallas_call | solution.py:414
  103.6 2.9 %projection_backward.3 = (bf16[2,4,448,128]{3,2,1,0:T(8,128)(2,1)S(1)}, bf16[2,4,448,128]{3,2,1,0:T(8,128)(2,1)S(1)}, f32[2,197,384]{2,1,0:T(8,128)S(1)}) custom-call(s32[8]{0:T(128)S(1)} %get-tuple-element.165.refs_1_.refs_0_, s32[8]{0:T(128)S(1)} %get-tuple-element.166.refs_2_.refs_1_, f32[416,384]{1,0:T(8,128)S(1)} %get-tuple-element.245.g_hidden.refs_2_, ...), custom_call_target="tpu_custom_call" | custom-call | flops 736100352 | bytes 7691328 | tf_op jit(solution)/shard_map/projection_backward/pallas_call | solution.py:414
  109.9 2.7 %collective-permute-done.41 = bf16[2,448,128]{2,1,0:T(8,128)(2,1)S(1)} collective-permute-done((bf16[2,448,128]{2,1,0:T(8,128)(2,1)S(1)}, bf16[2,448,128]{2,1,0:T(8,128)(2,1)S(1)}, u32[]{:S(2)}, u32[]{:S(2)}) %collective-permute-start.41) | collective-permute-done | bytes 229408 | tf_op jit(solution)/shard_map/ppermute | solution.py:435
  115.2 2.7 %collective-permute-start.42 = (bf16[448,128]{1,0:T(8,128)(2,1)S(1)}, bf16[448,128]{1,0:T(8,128)(2,1)S(1)}, u32[]{:S(2)}, u32[]{:S(2)}) collective-permute-start(bf16[448,128]{1,0:T(8,128)(2,1)S(1)} %get-tuple-element.388), channel_id=1, source_target_pairs={{0,16},{1,17},{2,18},{3,19},{4,20},{5,21},{6,22},{7,23},{8,24},{9,... | collective-permute-start | bytes 344072 | tf_op jit(solution)/shard_map/ppermute | solution.py:435
  117.9 4.1 %collective-permute-done.42.received = bf16[448,128]{1,0:T(8,128)(2,1)S(1)} collective-permute-done((bf16[448,128]{1,0:T(8,128)(2,1)S(1)}, bf16[448,128]{1,0:T(8,128)(2,1)S(1)}, u32[]{:S(2)}, u32[]{:S(2)}) %collective-permute-start.42) | collective-permute-done | bytes 114720 | tf_op jit(solution)/shard_map/ppermute | solution.py:435
  136.0 2.5 %collective-permute-done.47.refs_3_ = bf16[448,128]{1,0:T(8,128)(2,1)S(1)} collective-permute-done((bf16[448,128]{1,0:T(8,128)(2,1)S(1)}, bf16[448,128]{1,0:T(8,128)(2,1)S(1)}, u32[]{:S(2)}, u32[]{:S(2)}) %collective-permute-start.47) | collective-permute-done | bytes 114720 | tf_op jit(solution)/shard_map/ppermute | solution.py:435
  (176 shorter events, 58.3 us)
Async XLA Ops:
  2.3 9.8 %collective-permute-start = (bf16[448,128]{1,0:T(8,128)(2,1)S(1)}, bf16[448,128]{1,0:T(8,128)(2,1)S(1)}, u32[]{:S(2)}, u32[]{:S(2)}) collective-permute-start(bf16[448,128]{1,0:T(8,128)(2,1)S(1)} %get-tuple-element.403), channel_id=1, source_target_pairs={{0,8},{1,9},{2,10},{3,11},{4,12},{5,13},{6,14},{7,15},{8,0},{9,1},... | collective-permute-start | bytes 344072 | tf_op jit(solution)/shard_map/ppermute | solution.py:435
  5.4 11.7 %collective-permute-start.1 = (bf16[448,128]{1,0:T(8,128)(2,1)S(1)}, bf16[448,128]{1,0:T(8,128)(2,1)S(1)}, u32[]{:S(2)}, u32[]{:S(2)}) collective-permute-start(bf16[448,128]{1,0:T(8,128)(2,1)S(1)} %get-tuple-element.403), channel_id=1, source_target_pairs={{0,16},{1,17},{2,18},{3,19},{4,20},{5,21},{6,22},{7,23},{8,24},{9,... | collective-permute-start | bytes 344072 | tf_op jit(solution)/shard_map/ppermute | solution.py:435
  8.0 9.1 %collective-permute-start.2 = (bf16[448,128]{1,0:T(8,128)(2,1)S(1)}, bf16[448,128]{1,0:T(8,128)(2,1)S(1)}, u32[]{:S(2)}, u32[]{:S(2)}) collective-permute-start(bf16[448,128]{1,0:T(8,128)(2,1)S(1)} %get-tuple-element.403), channel_id=1, source_target_pairs={{0,24},{1,25},{2,26},{3,27},{4,28},{5,29},{6,30},{7,31},{8,16},{9,... | collective-permute-start | bytes 344072 | tf_op jit(solution)/shard_map/ppermute | solution.py:435
  17.1 8.9 %collective-permute-start.4 = (bf16[2,448,128]{2,1,0:T(8,128)(2,1)S(1)}, bf16[2,448,128]{2,1,0:T(8,128)(2,1)S(1)}, u32[]{:S(2)}, u32[]{:S(2)}) collective-permute-start(bf16[2,448,128]{2,1,0:T(8,128)(2,1)S(1)} %get-tuple-element.379), channel_id=1, source_target_pairs={{0,2},{1,3},{2,0},{3,1},{4,6},{5,7},{6,4},{7,5},{8,10},{9,11},{10,... | collective-permute-start | bytes 688136 | tf_op jit(solution)/shard_map/ppermute | solution.py:435
  18.7 7.4 %collective-permute-start.5 = (bf16[2,448,128]{2,1,0:T(8,128)(2,1)S(1)}, bf16[2,448,128]{2,1,0:T(8,128)(2,1)S(1)}, u32[]{:S(2)}, u32[]{:S(2)}) collective-permute-start(bf16[2,448,128]{2,1,0:T(8,128)(2,1)S(1)} %get-tuple-element.378), channel_id=1, source_target_pairs={{0,4},{1,5},{2,6},{3,7},{4,0},{5,1},{6,2},{7,3},{8,12},{9,13},{10,... | collective-permute-start | bytes 688136 | tf_op jit(solution)/shard_map/ppermute | solution.py:435
  26.1 14.2 %collective-permute-start.10 = (bf16[4,448,128]{2,1,0:T(8,128)(2,1)S(1)}, bf16[4,448,128]{2,1,0:T(8,128)(2,1)S(1)}, u32[]{:S(2)}, u32[]{:S(2)}) collective-permute-start(bf16[4,448,128]{2,1,0:T(8,128)(2,1)S(1)} %pad_maximum_fusion.6), channel_id=1, source_target_pairs={{0,2},{1,3},{2,0},{3,1},{4,6},{5,7},{6,4},{7,5},{8,10},{9,11},{10,... | collective-permute-start | bytes 1376264 | tf_op jit(solution)/shard_map/ppermute | solution.py:435
  26.8 13.6 %collective-permute-start.9 = (bf16[4,448,128]{2,1,0:T(8,128)(2,1)S(1)}, bf16[4,448,128]{2,1,0:T(8,128)(2,1)S(1)}, u32[]{:S(2)}, u32[]{:S(2)}) collective-permute-start(bf16[4,448,128]{2,1,0:T(8,128)(2,1)S(1)} %pad_maximum_fusion.5), channel_id=1, source_target_pairs={{0,4},{1,5},{2,6},{3,7},{4,0},{5,1},{6,2},{7,3},{8,12},{9,13},{10,... | collective-permute-start | bytes 1376264 | tf_op jit(solution)/shard_map/ppermute | solution.py:435
  30.4 8.0 %collective-permute-start.13 = (bf16[4,160,128]{2,1,0:T(8,128)(2,1)S(1)}, bf16[4,160,128]{2,1,0:T(8,128)(2,1)S(1)}, u32[]{:S(2)}, u32[]{:S(2)}) collective-permute-start(bf16[4,160,128]{2,1,0:T(8,128)(2,1)S(1)} %pad_maximum_fusion.13), channel_id=1, source_target_pairs={{0,16},{1,17},{2,18},{3,19},{4,20},{5,21},{6,22},{7,23},{8,24},{9,... | collective-permute-start | bytes 491528 | tf_op jit(solution)/shard_map/ppermute | solution.py:435
  40.6 11.7 %collective-permute-start.17 = (bf16[4,2,160,128]{3,2,0,1:T(8,128)(2,1)S(1)}, bf16[4,2,160,128]{3,2,0,1:T(8,128)(2,1)S(1)}, u32[]{:S(2)}, u32[]{:S(2)}) collective-permute-start(bf16[4,2,160,128]{3,2,0,1:T(8,128)(2,1)S(1)} %pad_maximum_fusion.7), channel_id=1, source_target_pairs={{0,8},{1,9},{2,10},{3,11},{4,12},{5,13},{6,14},{7,15},{8,0},{9,1},... | collective-permute-start | bytes 983048 | tf_op jit(solution)/shard_map/ppermute | solution.py:435
  42.6 9.2 %collective-permute-start.15 = (bf16[4,288,128]{2,1,0:T(8,128)(2,1)S(1)}, bf16[4,288,128]{2,1,0:T(8,128)(2,1)S(1)}, u32[]{:S(2)}, u32[]{:S(2)}) collective-permute-start(bf16[4,288,128]{2,1,0:T(8,128)(2,1)S(1)} %pad_maximum_fusion.8), channel_id=1, source_target_pairs={{0,4},{1,5},{2,6},{3,7},{4,0},{5,1},{6,2},{7,3},{8,12},{9,13},{10,... | collective-permute-start | bytes 884744 | tf_op jit(solution)/shard_map/ppermute | solution.py:435
  43.4 8.9 %collective-permute-start.16 = (bf16[4,288,128]{2,1,0:T(8,128)(2,1)S(1)}, bf16[4,288,128]{2,1,0:T(8,128)(2,1)S(1)}, u32[]{:S(2)}, u32[]{:S(2)}) collective-permute-start(bf16[4,288,128]{2,1,0:T(8,128)(2,1)S(1)} %pad_maximum_fusion.9), channel_id=1, source_target_pairs={{0,2},{1,3},{2,0},{3,1},{4,6},{5,7},{6,4},{7,5},{8,10},{9,11},{10,... | collective-permute-start | bytes 884744 | tf_op jit(solution)/shard_map/ppermute | solution.py:435
  45.1 8.7 %collective-permute-start.18 = (bf16[8,448,128]{2,1,0:T(8,128)(2,1)S(1)}, bf16[8,448,128]{2,1,0:T(8,128)(2,1)S(1)}, u32[]{:S(2)}, u32[]{:S(2)}) collective-permute-start(bf16[8,448,128]{2,1,0:T(8,128)(2,1)S(1)} %pad_maximum_fusion.1.refs_4_), channel_id=1, source_target_pairs={{0,1},{1,0},{2,3},{3,2},{4,5},{5,4},{6,7},{7,6},{8,9},{9,8},{10,11... | collective-permute-start | bytes 2752520 | tf_op jit(solution)/shard_map/ppermute | solution.py:435
  78.7 7.5 %collective-permute-start.26 = (bf16[2,4,448,128]{3,2,1,0:T(8,128)(2,1)S(1)}, bf16[2,4,448,128]{3,2,1,0:T(8,128)(2,1)S(1)}, u32[]{:S(2)}, u32[]{:S(2)}) collective-permute-start(bf16[2,4,448,128]{3,2,1,0:T(8,128)(2,1)S(1)} %get-tuple-element.226), channel_id=1, source_target_pairs={{0,1},{1,0},{2,3},{3,2},{4,5},{5,4},{6,7},{7,6},{8,9},{9,8},{10,11... | collective-permute-start | bytes 2752520 | tf_op jit(solution)/shard_map/ppermute | solution.py:435
  79.3 7.7 %collective-permute-start.25 = (bf16[2,448,128]{2,1,0:T(8,128)(2,1)S(1)}, bf16[2,448,128]{2,1,0:T(8,128)(2,1)S(1)}, u32[]{:S(2)}, u32[]{:S(2)}) collective-permute-start(bf16[2,448,128]{2,1,0:T(8,128)(2,1)S(1)} %get-tuple-element.374), channel_id=1, source_target_pairs={{0,2},{1,3},{2,0},{3,1},{4,6},{5,7},{6,4},{7,5},{8,10},{9,11},{10,... | collective-permute-start | bytes 688136 | tf_op jit(solution)/shard_map/ppermute | solution.py:435
  81.0 7.5 %collective-permute-start.24 = (bf16[2,448,128]{2,1,0:T(8,128)(2,1)S(1)}, bf16[2,448,128]{2,1,0:T(8,128)(2,1)S(1)}, u32[]{:S(2)}, u32[]{:S(2)}) collective-permute-start(bf16[2,448,128]{2,1,0:T(8,128)(2,1)S(1)} %get-tuple-element.376), channel_id=1, source_target_pairs={{0,4},{1,5},{2,6},{3,7},{4,0},{5,1},{6,2},{7,3},{8,12},{9,13},{10,... | collective-permute-start | bytes 688136 | tf_op jit(solution)/shard_map/ppermute | solution.py:435
  86.0 7.3 %collective-permute-start.31 = (bf16[2,4,448,128]{3,2,1,0:T(8,128)(2,1)S(1)}, bf16[2,4,448,128]{3,2,1,0:T(8,128)(2,1)S(1)}, u32[]{:S(2)}, u32[]{:S(2)}) collective-permute-start(bf16[2,4,448,128]{3,2,1,0:T(8,128)(2,1)S(1)} %get-tuple-element.244), channel_id=1, source_target_pairs={{0,1},{1,0},{2,3},{3,2},{4,5},{5,4},{6,7},{7,6},{8,9},{9,8},{10,11... | collective-permute-start | bytes 2752520 | tf_op jit(solution)/shard_map/ppermute | solution.py:435
  88.6 10.0 %collective-permute-start.30 = (bf16[2,448,128]{2,1,0:T(8,128)(2,1)S(1)}, bf16[2,448,128]{2,1,0:T(8,128)(2,1)S(1)}, u32[]{:S(2)}, u32[]{:S(2)}) collective-permute-start(bf16[2,448,128]{2,1,0:T(8,128)(2,1)S(1)} %get-tuple-element.370), channel_id=1, source_target_pairs={{0,2},{1,3},{2,0},{3,1},{4,6},{5,7},{6,4},{7,5},{8,10},{9,11},{10,... | collective-permute-start | bytes 688136 | tf_op jit(solution)/shard_map/ppermute | solution.py:435
  89.4 9.3 %collective-permute-start.29 = (bf16[2,448,128]{2,1,0:T(8,128)(2,1)S(1)}, bf16[2,448,128]{2,1,0:T(8,128)(2,1)S(1)}, u32[]{:S(2)}, u32[]{:S(2)}) collective-permute-start(bf16[2,448,128]{2,1,0:T(8,128)(2,1)S(1)} %get-tuple-element.372), channel_id=1, source_target_pairs={{0,4},{1,5},{2,6},{3,7},{4,0},{5,1},{6,2},{7,3},{8,12},{9,13},{10,... | collective-permute-start | bytes 688136 | tf_op jit(solution)/shard_map/ppermute | solution.py:435
  90.9 7.7 %collective-permute-start.28 = (bf16[1,448,128]{2,1,0:T(8,128)(2,1)S(1)}, bf16[1,448,128]{2,1,0:T(8,128)(2,1)S(1)}, u32[]{:S(2)}, u32[]{:S(2)}) collective-permute-start(bf16[1,448,128]{2,1,0:T(8,128)(2,1)S(1)} %get-tuple-element.398), channel_id=1, source_target_pairs={{0,4},{1,5},{2,6},{3,7},{4,0},{5,1},{6,2},{7,3},{8,12},{9,13},{10,... | collective-permute-start | bytes 344072 | tf_op jit(solution)/shard_map/ppermute | solution.py:435
  98.8 7.7 %collective-permute-start.33 = (bf16[1,448,128]{2,1,0:T(8,128)(2,1)S(1)}, bf16[1,448,128]{2,1,0:T(8,128)(2,1)S(1)}, u32[]{:S(2)}, u32[]{:S(2)}) collective-permute-start(bf16[1,448,128]{2,1,0:T(8,128)(2,1)S(1)} %get-tuple-element.394), channel_id=1, source_target_pairs={{0,4},{1,5},{2,6},{3,7},{4,0},{5,1},{6,2},{7,3},{8,12},{9,13},{10,... | collective-permute-start | bytes 344072 | tf_op jit(solution)/shard_map/ppermute | solution.py:435
  107.5 10.3 %collective-permute-start.40 = (bf16[1,448,128]{2,1,0:T(8,128)(2,1)S(1)}, bf16[1,448,128]{2,1,0:T(8,128)(2,1)S(1)}, u32[]{:S(2)}, u32[]{:S(2)}) collective-permute-start(bf16[1,448,128]{2,1,0:T(8,128)(2,1)S(1)} %get-tuple-element.390), channel_id=1, source_target_pairs={{0,4},{1,5},{2,6},{3,7},{4,0},{5,1},{6,2},{7,3},{8,12},{9,13},{10,... | collective-permute-start | bytes 344072 | tf_op jit(solution)/shard_map/ppermute | solution.py:435
  108.9 9.0 %collective-permute-start.38 = (bf16[1,448,128]{2,1,0:T(8,128)(2,1)S(1)}, bf16[1,448,128]{2,1,0:T(8,128)(2,1)S(1)}, u32[]{:S(2)}, u32[]{:S(2)}) collective-permute-start(bf16[1,448,128]{2,1,0:T(8,128)(2,1)S(1)} %get-tuple-element.392), channel_id=1, source_target_pairs={{0,2},{1,3},{2,0},{3,1},{4,6},{5,7},{6,4},{7,5},{8,10},{9,11},{10,... | collective-permute-start | bytes 344072 | tf_op jit(solution)/shard_map/ppermute | solution.py:435
  113.0 8.9 %collective-permute-start.36 = (bf16[2,448,128]{2,1,0:T(8,128)(2,1)S(1)}, bf16[2,448,128]{2,1,0:T(8,128)(2,1)S(1)}, u32[]{:S(2)}, u32[]{:S(2)}) collective-permute-start(bf16[2,448,128]{2,1,0:T(8,128)(2,1)S(1)} %get-tuple-element.366), channel_id=1, source_target_pairs={{0,2},{1,3},{2,0},{3,1},{4,6},{5,7},{6,4},{7,5},{8,10},{9,11},{10,... | collective-permute-start | bytes 688136 | tf_op jit(solution)/shard_map/ppermute | solution.py:435
  114.3 7.7 %collective-permute-start.35 = (bf16[2,448,128]{2,1,0:T(8,128)(2,1)S(1)}, bf16[2,448,128]{2,1,0:T(8,128)(2,1)S(1)}, u32[]{:S(2)}, u32[]{:S(2)}) collective-permute-start(bf16[2,448,128]{2,1,0:T(8,128)(2,1)S(1)} %get-tuple-element.368), channel_id=1, source_target_pairs={{0,4},{1,5},{2,6},{3,7},{4,0},{5,1},{6,2},{7,3},{8,12},{9,13},{10,... | collective-permute-start | bytes 688136 | tf_op jit(solution)/shard_map/ppermute | solution.py:435
  (30 other events, 152.8 us)

commit v5 on v4

--- a/solution.py
+++ b/solution.py
@@ -25,7 +25,7 @@
 FORWARD_UNROLL = 6
 BACKWARD_UNROLL = 3
 VMEM_LIMIT = 14 * 1024 * 1024
-BLOCK = 768
+BLOCK = 1536
 
 eps_norm = 1e-06
 beta_one = 0.9

time: 140 us -> 140 us (level)
  no operation moved by 1% of the time
where the time goes in v5:
time: 140 us
  starting transfers between devices  52.5 us (38%)
  Pallas kernels  43.7 us (31%)
  waiting for transfers between devices  35.1 us (25%)
  other arithmetic  3.91 us (3%)
  local copies, waits for them, and re-layouts  3.68 us (3%)
  between operations  1.43 us (1%)
    ppermute x48, starting transfers between devices, swap(): return lax.ppermute(values, 'dp', [(i, i ^ mask) for i in range(size)])  52.5 us
    pallas_call x12, Pallas kernels, call(): pl.pallas_call(body, name=name, out_shape=shapes, in_specs=in_specs, out_...  43.7 us
    ppermute x48, waiting for transfers between devices, swap(): return lax.ppermute(values, 'dp', [(i, i ^ mask) for i in range(size)])  35.1 us
  transfers between devices with their start and end apart: 48, of which 19 were waited for; matrix products, arithmetic and copies ran while one was open for 4% of the time, Pallas kernels for 19%

profile of v5, /device:TPU:0, one launch (start us, length us, event | category | flops | bytes accessed | tf_op | source)
XLA Modules:
  0.0 140.2 jit_solution(13298587126259852368)
XLA Ops:
  2.3 3.1 %collective-permute-start = (bf16[448,128]{1,0:T(8,128)(2,1)S(1)}, bf16[448,128]{1,0:T(8,128)(2,1)S(1)}, u32[]{:S(2)}, u32[]{:S(2)}) collective-permute-start(bf16[448,128]{1,0:T(8,128)(2,1)S(1)} %get-tuple-element.403), channel_id=1, source_target_pairs={{0,8},{1,9},{2,10},{3,11},{4,12},{5,13},{6,14},{7,15},{8,0},{9,1},... | collective-permute-start | bytes 344072 | tf_op jit(solution)/shard_map/ppermute | solution.py:435
  5.4 2.6 %collective-permute-start.1 = (bf16[448,128]{1,0:T(8,128)(2,1)S(1)}, bf16[448,128]{1,0:T(8,128)(2,1)S(1)}, u32[]{:S(2)}, u32[]{:S(2)}) collective-permute-start(bf16[448,128]{1,0:T(8,128)(2,1)S(1)} %get-tuple-element.403), channel_id=1, source_target_pairs={{0,16},{1,17},{2,18},{3,19},{4,20},{5,21},{6,22},{7,23},{8,24},{9,... | collective-permute-start | bytes 344072 | tf_op jit(solution)/shard_map/ppermute | solution.py:435
  9.7 2.4 %collective-permute-done.3 = bf16[1,160,128]{2,1,0:T(8,128)(2,1)S(1)} collective-permute-done((bf16[1,160,128]{2,1,0:T(8,128)(2,1)S(1)}, bf16[1,160,128]{2,1,0:T(8,128)(2,1)S(1)}, u32[]{:S(2)}, u32[]{:S(2)}) %collective-permute-start.3) | collective-permute-done | bytes 40992 | tf_op jit(solution)/shard_map/ppermute | solution.py:435
  12.0 5.0 %collective-permute-done.1 = bf16[448,128]{1,0:T(8,128)(2,1)S(1)} collective-permute-done((bf16[448,128]{1,0:T(8,128)(2,1)S(1)}, bf16[448,128]{1,0:T(8,128)(2,1)S(1)}, u32[]{:S(2)}, u32[]{:S(2)}) %collective-permute-start.1) | collective-permute-done | bytes 114720 | tf_op jit(solution)/shard_map/ppermute | solution.py:435
  20.8 2.8 %collective-permute-start.6 = (bf16[288,128]{1,0:T(8,128)(2,1)S(1)}, bf16[288,128]{1,0:T(8,128)(2,1)S(1)}, u32[]{:S(2)}, u32[]{:S(2)}) collective-permute-start(bf16[288,128]{1,0:T(8,128)(2,1)S(1)} %slice_bitcast_fusion.18), channel_id=1, source_target_pairs={{0,16},{1,17},{2,18},{3,19},{4,20},{5,21},{6,22},{7,23},{8,24},{9,... | collective-permute-start | bytes 221192 | tf_op jit(solution)/shard_map/ppermute | solution.py:435
  23.6 2.5 %collective-permute-done.6 = bf16[288,128]{1,0:T(8,128)(2,1)S(1)} collective-permute-done((bf16[288,128]{1,0:T(8,128)(2,1)S(1)}, bf16[288,128]{1,0:T(8,128)(2,1)S(1)}, u32[]{:S(2)}, u32[]{:S(2)}) %collective-permute-start.6) | collective-permute-done | bytes 73760 | tf_op jit(solution)/shard_map/ppermute | solution.py:435
  28.4 2.0 %collective-permute-start.8 = (bf16[1,2,288,128]{3,2,0,1:T(8,128)(2,1)S(1)}, bf16[1,2,288,128]{3,2,0,1:T(8,128)(2,1)S(1)}, u32[]{:S(2)}, u32[]{:S(2)}) collective-permute-start(bf16[1,2,288,128]{3,2,0,1:T(8,128)(2,1)S(1)} %maximum_bitcast_fusion), channel_id=1, source_target_pairs={{0,8},{1,9},{2,10},{3,11},{4,12},{5,13},{6,14},{7,15},{8,0},{9,1},... | collective-permute-start | bytes 442376 | tf_op jit(solution)/shard_map/ppermute | solution.py:435
  31.6 2.0 %collective-permute-done.8 = bf16[1,2,288,128]{3,2,0,1:T(8,128)(2,1)S(1)} collective-permute-done((bf16[1,2,288,128]{3,2,0,1:T(8,128)(2,1)S(1)}, bf16[1,2,288,128]{3,2,0,1:T(8,128)(2,1)S(1)}, u32[]{:S(2)}, u32[]{:S(2)}) %collective-permute-start.8) | collective-permute-done | bytes 147488 | tf_op jit(solution)/shard_map/ppermute | solution.py:435
  35.7 2.8 %collective-permute-done.13 = bf16[4,160,128]{2,1,0:T(8,128)(2,1)S(1)} collective-permute-done((bf16[4,160,128]{2,1,0:T(8,128)(2,1)S(1)}, bf16[4,160,128]{2,1,0:T(8,128)(2,1)S(1)}, u32[]{:S(2)}, u32[]{:S(2)}) %collective-permute-start.13) | collective-permute-done | bytes 163872 | tf_op jit(solution)/shard_map/ppermute | solution.py:435
  45.2 3.6 %attention_forward.2 = (f32[416,384]{1,0:T(8,128)S(1)}, bf16[384,1152]{1,0:T(8,128)(2,1)S(1)}, bf16[384,384]{1,0:T(8,128)(2,1)S(1)}, f32[8,384]{1,0:T(8,128)S(1)...) custom-call(s32[16]{0:T(128)S(1)} %get-tuple-element.167.refs_0_, ...), custom_call_target="tpu_custom_call" | custom-call | flops 623640576 | bytes 7243328 | tf_op jit(solution)/shard_map/attention_forward/pallas_call | solution.py:414
  48.8 3.0 %collective-permute-done.15 = bf16[4,288,128]{2,1,0:T(8,128)(2,1)S(1)} collective-permute-done((bf16[4,288,128]{2,1,0:T(8,128)(2,1)S(1)}, bf16[4,288,128]{2,1,0:T(8,128)(2,1)S(1)}, u32[]{:S(2)}, u32[]{:S(2)}) %collective-permute-start.15) | collective-permute-done | bytes 294944 | tf_op jit(solution)/shard_map/ppermute | solution.py:435
  53.8 4.0 %mlp_forward.2 = (bf16[384,1536]{1,0:T(8,128)(2,1)S(1)}, bf16[1536,384]{1,0:T(8,128)(2,1)S(1)}, f32[8,384]{1,0:T(8,128)S(1)}, bf16[416,384]{1,0:T(8,128)(2,1)S(1...) custom-call(s32[16]{0:T(128)S(1)} %get-tuple-element.167.refs_0_, ...), custom_call_target="tpu_custom_call" | custom-call | flops 981467136 | bytes 10195072 | tf_op jit(solution)/shard_map/mlp_forward/pallas_call | solution.py:414
  57.9 3.6 %attention_forward.3 = (bf16[384,1152]{1,0:T(8,128)(2,1)S(1)}, bf16[384,384]{1,0:T(8,128)(2,1)S(1)}, f32[8,384]{1,0:T(8,128)S(1)}, bf16[416,384]{1,0:T(8,128)(2,...) custom-call(s32[16]{0:T(128)S(1)} %get-tuple-element.167.refs_0_, ...), custom_call_target="tpu_custom_call" | custom-call | flops 623640576 | bytes 6940800 | tf_op jit(solution)/shard_map/attention_forward/pallas_call | solution.py:414
  61.5 4.3 %mlp_forward.3 = (bf16[384,1536]{1,0:T(8,128)(2,1)S(1)}, bf16[1536,384]{1,0:T(8,128)(2,1)S(1)}, f32[8,384]{1,0:T(8,128)S(1)}, bf16[416,384]{1,0:T(8,128)(2,1)S(1...) custom-call(s32[16]{0:T(128)S(1)} %get-tuple-element.167.refs_0_, ...), custom_call_target="tpu_custom_call" | custom-call | flops 981467136 | bytes 10161408 | tf_op jit(solution)/shard_map/mlp_forward/pallas_call | solution.py:414
  65.8 4.4 %mlp_backward.2 = (f32[2336,128]{1,0:T(8,128)S(1)}, bf16[2,4,448,128]{3,2,1,0:T(8,128)(2,1)S(1)}, bf16[2,4,448,128]{3,2,1,0:T(8,128)(2,1)S(1)}, f32[416,384]{1,0:T(8,128)S(1)}) custom-call(s32[2]{0:T(128)S(1)} %copy-done.3, s32[8]{0:T(128)S(1)} %get-tuple-element.165.refs_1_.refs_0_, s32[8]{0:T(128)S(1)} %get-tuple-element.166.refs_2_.refs_1_, ...), custom_call_target="tpu_custom_call" | custom-call | flops 1962934272 | bytes 9858632 | tf_op jit(solution)/shard_map/mlp_backward/pallas_call | solution.py:414
  70.4 5.3 %attention_backward.2 = (bf16[416,1152]{1,0:T(8,128)(2,1)S(1)}, f32[384,384]{1,0:T(8,128)S(1)}, f32[8,384]{1,0:T(8,128)S(1)}) custom-call(f32[416,384]{1,0:T(8,128)S(1)} %get-tuple-element.206.g_hidden.refs_2_, bf16[384,384]{1,0:T(8,128)(2,1)S(1)} %get-tuple-element.207.w_out, bf16[416,1152]{1,0:T(8,128)(2,1)S(1)} %get-tuple-element.208.qkv, ...), custom_call_target="tpu_custom_call" | custom-call | flops 511180800 | bytes 4810752 | tf_op jit(solution)/shard_map/attention_backward/pallas_call | solution.py:414
  75.8 2.8 %projection_backward.2 = (bf16[2,4,448,128]{3,2,1,0:T(8,128)(2,1)S(1)}, bf16[2,4,448,128]{3,2,1,0:T(8,128)(2,1)S(1)}, f32[416,384]{1,0:T(8,128)S(1)}) custom-call(s32[8]{0:T(128)S(1)} %get-tuple-element.165.refs_1_.refs_0_, s32[8]{0:T(128)S(1)} %get-tuple-element.166.refs_2_.refs_1_, f32[416,384]{1,0:T(8,128)S(1)} %get-tuple-element.206.g_hidden.refs_2_, ...), custom_call_target="tpu_custom_call" | custom-call | flops 736100352 | bytes 7725120 | tf_op jit(solution)/shard_map/projection_backward/pallas_call | solution.py:414
  81.5 4.3 %mlp_backward.3 = (f32[2336,128]{1,0:T(8,128)S(1)}, bf16[2,4,448,128]{3,2,1,0:T(8,128)(2,1)S(1)}, bf16[2,4,448,128]{3,2,1,0:T(8,128)(2,1)S(1)}, f32[416,384]{1,0:T(8,128)S(1)}) custom-call(s32[8]{0:T(128)S(1)} %get-tuple-element.165.refs_1_.refs_0_, s32[8]{0:T(128)S(1)} %get-tuple-element.166.refs_2_.refs_1_, f32[416,384]{1,0:T(8,128)S(1)} %get-tuple-element.227.refs_2_, ...), custom_call_target="tpu_custom_call" | custom-call | flops 1962934272 | bytes 10195008 | tf_op jit(solution)/shard_map/mlp_backward/pallas_call | solution.py:414
  93.3 5.3 %attention_backward.3 = (bf16[416,1152]{1,0:T(8,128)(2,1)S(1)}, f32[384,384]{1,0:T(8,128)S(1)}, f32[8,384]{1,0:T(8,128)S(1)}) custom-call(f32[416,384]{1,0:T(8,128)S(1)} %get-tuple-element.245.g_hidden.refs_2_, bf16[384,384]{1,0:T(8,128)(2,1)S(1)} %get-tuple-element.246.w_out, bf16[416,1152]{1,0:T(8,128)(2,1)S(1)} %get-tuple-element.247.qkv, ...), custom_call_target="tpu_custom_call" | custom-call | flops 511180800 | bytes 4810752 | tf_op jit(solution)/shard_map/attention_backward/pallas_call | solution.py:414
  103.5 2.9 %projection_backward.3 = (bf16[2,4,448,128]{3,2,1,0:T(8,128)(2,1)S(1)}, bf16[2,4,448,128]{3,2,1,0:T(8,128)(2,1)S(1)}, f32[2,197,384]{2,1,0:T(8,128)S(1)}) custom-call(s32[8]{0:T(128)S(1)} %get-tuple-element.165.refs_1_.refs_0_, s32[8]{0:T(128)S(1)} %get-tuple-element.166.refs_2_.refs_1_, f32[416,384]{1,0:T(8,128)S(1)} %get-tuple-element.245.g_hidden.refs_2_, ...), custom_call_target="tpu_custom_call" | custom-call | flops 736100352 | bytes 7691328 | tf_op jit(solution)/shard_map/projection_backward/pallas_call | solution.py:414
  109.9 2.7 %collective-permute-done.41 = bf16[2,448,128]{2,1,0:T(8,128)(2,1)S(1)} collective-permute-done((bf16[2,448,128]{2,1,0:T(8,128)(2,1)S(1)}, bf16[2,448,128]{2,1,0:T(8,128)(2,1)S(1)}, u32[]{:S(2)}, u32[]{:S(2)}) %collective-permute-start.41) | collective-permute-done | bytes 229408 | tf_op jit(solution)/shard_map/ppermute | solution.py:435
  115.1 2.7 %collective-permute-start.42 = (bf16[448,128]{1,0:T(8,128)(2,1)S(1)}, bf16[448,128]{1,0:T(8,128)(2,1)S(1)}, u32[]{:S(2)}, u32[]{:S(2)}) collective-permute-start(bf16[448,128]{1,0:T(8,128)(2,1)S(1)} %get-tuple-element.388), channel_id=1, source_target_pairs={{0,16},{1,17},{2,18},{3,19},{4,20},{5,21},{6,22},{7,23},{8,24},{9,... | collective-permute-start | bytes 344072 | tf_op jit(solution)/shard_map/ppermute | solution.py:435
  117.8 4.1 %collective-permute-done.42.received = bf16[448,128]{1,0:T(8,128)(2,1)S(1)} collective-permute-done((bf16[448,128]{1,0:T(8,128)(2,1)S(1)}, bf16[448,128]{1,0:T(8,128)(2,1)S(1)}, u32[]{:S(2)}, u32[]{:S(2)}) %collective-permute-start.42) | collective-permute-done | bytes 114720 | tf_op jit(solution)/shard_map/ppermute | solution.py:435
  135.9 2.5 %collective-permute-done.47.refs_3_ = bf16[448,128]{1,0:T(8,128)(2,1)S(1)} collective-permute-done((bf16[448,128]{1,0:T(8,128)(2,1)S(1)}, bf16[448,128]{1,0:T(8,128)(2,1)S(1)}, u32[]{:S(2)}, u32[]{:S(2)}) %collective-permute-start.47) | collective-permute-done | bytes 114720 | tf_op jit(solution)/shard_map/ppermute | solution.py:435
  (176 shorter events, 58.4 us)
Async XLA Ops:
  2.3 9.8 %collective-permute-start = (bf16[448,128]{1,0:T(8,128)(2,1)S(1)}, bf16[448,128]{1,0:T(8,128)(2,1)S(1)}, u32[]{:S(2)}, u32[]{:S(2)}) collective-permute-start(bf16[448,128]{1,0:T(8,128)(2,1)S(1)} %get-tuple-element.403), channel_id=1, source_target_pairs={{0,8},{1,9},{2,10},{3,11},{4,12},{5,13},{6,14},{7,15},{8,0},{9,1},... | collective-permute-start | bytes 344072 | tf_op jit(solution)/shard_map/ppermute | solution.py:435
  5.4 11.7 %collective-permute-start.1 = (bf16[448,128]{1,0:T(8,128)(2,1)S(1)}, bf16[448,128]{1,0:T(8,128)(2,1)S(1)}, u32[]{:S(2)}, u32[]{:S(2)}) collective-permute-start(bf16[448,128]{1,0:T(8,128)(2,1)S(1)} %get-tuple-element.403), channel_id=1, source_target_pairs={{0,16},{1,17},{2,18},{3,19},{4,20},{5,21},{6,22},{7,23},{8,24},{9,... | collective-permute-start | bytes 344072 | tf_op jit(solution)/shard_map/ppermute | solution.py:435
  8.0 9.1 %collective-permute-start.2 = (bf16[448,128]{1,0:T(8,128)(2,1)S(1)}, bf16[448,128]{1,0:T(8,128)(2,1)S(1)}, u32[]{:S(2)}, u32[]{:S(2)}) collective-permute-start(bf16[448,128]{1,0:T(8,128)(2,1)S(1)} %get-tuple-element.403), channel_id=1, source_target_pairs={{0,24},{1,25},{2,26},{3,27},{4,28},{5,29},{6,30},{7,31},{8,16},{9,... | collective-permute-start | bytes 344072 | tf_op jit(solution)/shard_map/ppermute | solution.py:435
  17.1 8.9 %collective-permute-start.4 = (bf16[2,448,128]{2,1,0:T(8,128)(2,1)S(1)}, bf16[2,448,128]{2,1,0:T(8,128)(2,1)S(1)}, u32[]{:S(2)}, u32[]{:S(2)}) collective-permute-start(bf16[2,448,128]{2,1,0:T(8,128)(2,1)S(1)} %get-tuple-element.379), channel_id=1, source_target_pairs={{0,2},{1,3},{2,0},{3,1},{4,6},{5,7},{6,4},{7,5},{8,10},{9,11},{10,... | collective-permute-start | bytes 688136 | tf_op jit(solution)/shard_map/ppermute | solution.py:435
  18.7 7.4 %collective-permute-start.5 = (bf16[2,448,128]{2,1,0:T(8,128)(2,1)S(1)}, bf16[2,448,128]{2,1,0:T(8,128)(2,1)S(1)}, u32[]{:S(2)}, u32[]{:S(2)}) collective-permute-start(bf16[2,448,128]{2,1,0:T(8,128)(2,1)S(1)} %get-tuple-element.378), channel_id=1, source_target_pairs={{0,4},{1,5},{2,6},{3,7},{4,0},{5,1},{6,2},{7,3},{8,12},{9,13},{10,... | collective-permute-start | bytes 688136 | tf_op jit(solution)/shard_map/ppermute | solution.py:435
  26.1 14.2 %collective-permute-start.10 = (bf16[4,448,128]{2,1,0:T(8,128)(2,1)S(1)}, bf16[4,448,128]{2,1,0:T(8,128)(2,1)S(1)}, u32[]{:S(2)}, u32[]{:S(2)}) collective-permute-start(bf16[4,448,128]{2,1,0:T(8,128)(2,1)S(1)} %pad_maximum_fusion.6), channel_id=1, source_target_pairs={{0,2},{1,3},{2,0},{3,1},{4,6},{5,7},{6,4},{7,5},{8,10},{9,11},{10,... | collective-permute-start | bytes 1376264 | tf_op jit(solution)/shard_map/ppermute | solution.py:435
  26.8 13.6 %collective-permute-start.9 = (bf16[4,448,128]{2,1,0:T(8,128)(2,1)S(1)}, bf16[4,448,128]{2,1,0:T(8,128)(2,1)S(1)}, u32[]{:S(2)}, u32[]{:S(2)}) collective-permute-start(bf16[4,448,128]{2,1,0:T(8,128)(2,1)S(1)} %pad_maximum_fusion.5), channel_id=1, source_target_pairs={{0,4},{1,5},{2,6},{3,7},{4,0},{5,1},{6,2},{7,3},{8,12},{9,13},{10,... | collective-permute-start | bytes 1376264 | tf_op jit(solution)/shard_map/ppermute | solution.py:435
  30.4 8.0 %collective-permute-start.13 = (bf16[4,160,128]{2,1,0:T(8,128)(2,1)S(1)}, bf16[4,160,128]{2,1,0:T(8,128)(2,1)S(1)}, u32[]{:S(2)}, u32[]{:S(2)}) collective-permute-start(bf16[4,160,128]{2,1,0:T(8,128)(2,1)S(1)} %pad_maximum_fusion.13), channel_id=1, source_target_pairs={{0,16},{1,17},{2,18},{3,19},{4,20},{5,21},{6,22},{7,23},{8,24},{9,... | collective-permute-start | bytes 491528 | tf_op jit(solution)/shard_map/ppermute | solution.py:435
  40.6 11.7 %collective-permute-start.17 = (bf16[4,2,160,128]{3,2,0,1:T(8,128)(2,1)S(1)}, bf16[4,2,160,128]{3,2,0,1:T(8,128)(2,1)S(1)}, u32[]{:S(2)}, u32[]{:S(2)}) collective-permute-start(bf16[4,2,160,128]{3,2,0,1:T(8,128)(2,1)S(1)} %pad_maximum_fusion.7), channel_id=1, source_target_pairs={{0,8},{1,9},{2,10},{3,11},{4,12},{5,13},{6,14},{7,15},{8,0},{9,1},... | collective-permute-start | bytes 983048 | tf_op jit(solution)/shard_map/ppermute | solution.py:435
  42.6 9.2 %collective-permute-start.15 = (bf16[4,288,128]{2,1,0:T(8,128)(2,1)S(1)}, bf16[4,288,128]{2,1,0:T(8,128)(2,1)S(1)}, u32[]{:S(2)}, u32[]{:S(2)}) collective-permute-start(bf16[4,288,128]{2,1,0:T(8,128)(2,1)S(1)} %pad_maximum_fusion.8), channel_id=1, source_target_pairs={{0,4},{1,5},{2,6},{3,7},{4,0},{5,1},{6,2},{7,3},{8,12},{9,13},{10,... | collective-permute-start | bytes 884744 | tf_op jit(solution)/shard_map/ppermute | solution.py:435
  43.4 8.9 %collective-permute-start.16 = (bf16[4,288,128]{2,1,0:T(8,128)(2,1)S(1)}, bf16[4,288,128]{2,1,0:T(8,128)(2,1)S(1)}, u32[]{:S(2)}, u32[]{:S(2)}) collective-permute-start(bf16[4,288,128]{2,1,0:T(8,128)(2,1)S(1)} %pad_maximum_fusion.9), channel_id=1, source_target_pairs={{0,2},{1,3},{2,0},{3,1},{4,6},{5,7},{6,4},{7,5},{8,10},{9,11},{10,... | collective-permute-start | bytes 884744 | tf_op jit(solution)/shard_map/ppermute | solution.py:435
  45.1 8.7 %collective-permute-start.18 = (bf16[8,448,128]{2,1,0:T(8,128)(2,1)S(1)}, bf16[8,448,128]{2,1,0:T(8,128)(2,1)S(1)}, u32[]{:S(2)}, u32[]{:S(2)}) collective-permute-start(bf16[8,448,128]{2,1,0:T(8,128)(2,1)S(1)} %pad_maximum_fusion.1.refs_4_), channel_id=1, source_target_pairs={{0,1},{1,0},{2,3},{3,2},{4,5},{5,4},{6,7},{7,6},{8,9},{9,8},{10,11... | collective-permute-start | bytes 2752520 | tf_op jit(solution)/shard_map/ppermute | solution.py:435
  78.7 7.4 %collective-permute-start.26 = (bf16[2,4,448,128]{3,2,1,0:T(8,128)(2,1)S(1)}, bf16[2,4,448,128]{3,2,1,0:T(8,128)(2,1)S(1)}, u32[]{:S(2)}, u32[]{:S(2)}) collective-permute-start(bf16[2,4,448,128]{3,2,1,0:T(8,128)(2,1)S(1)} %get-tuple-element.226), channel_id=1, source_target_pairs={{0,1},{1,0},{2,3},{3,2},{4,5},{5,4},{6,7},{7,6},{8,9},{9,8},{10,11... | collective-permute-start | bytes 2752520 | tf_op jit(solution)/shard_map/ppermute | solution.py:435
  79.2 7.8 %collective-permute-start.25 = (bf16[2,448,128]{2,1,0:T(8,128)(2,1)S(1)}, bf16[2,448,128]{2,1,0:T(8,128)(2,1)S(1)}, u32[]{:S(2)}, u32[]{:S(2)}) collective-permute-start(bf16[2,448,128]{2,1,0:T(8,128)(2,1)S(1)} %get-tuple-element.374), channel_id=1, source_target_pairs={{0,2},{1,3},{2,0},{3,1},{4,6},{5,7},{6,4},{7,5},{8,10},{9,11},{10,... | collective-permute-start | bytes 688136 | tf_op jit(solution)/shard_map/ppermute | solution.py:435
  80.9 7.5 %collective-permute-start.24 = (bf16[2,448,128]{2,1,0:T(8,128)(2,1)S(1)}, bf16[2,448,128]{2,1,0:T(8,128)(2,1)S(1)}, u32[]{:S(2)}, u32[]{:S(2)}) collective-permute-start(bf16[2,448,128]{2,1,0:T(8,128)(2,1)S(1)} %get-tuple-element.376), channel_id=1, source_target_pairs={{0,4},{1,5},{2,6},{3,7},{4,0},{5,1},{6,2},{7,3},{8,12},{9,13},{10,... | collective-permute-start | bytes 688136 | tf_op jit(solution)/shard_map/ppermute | solution.py:435
  85.8 7.4 %collective-permute-start.31 = (bf16[2,4,448,128]{3,2,1,0:T(8,128)(2,1)S(1)}, bf16[2,4,448,128]{3,2,1,0:T(8,128)(2,1)S(1)}, u32[]{:S(2)}, u32[]{:S(2)}) collective-permute-start(bf16[2,4,448,128]{3,2,1,0:T(8,128)(2,1)S(1)} %get-tuple-element.244), channel_id=1, source_target_pairs={{0,1},{1,0},{2,3},{3,2},{4,5},{5,4},{6,7},{7,6},{8,9},{9,8},{10,11... | collective-permute-start | bytes 2752520 | tf_op jit(solution)/shard_map/ppermute | solution.py:435
  88.6 10.0 %collective-permute-start.30 = (bf16[2,448,128]{2,1,0:T(8,128)(2,1)S(1)}, bf16[2,448,128]{2,1,0:T(8,128)(2,1)S(1)}, u32[]{:S(2)}, u32[]{:S(2)}) collective-permute-start(bf16[2,448,128]{2,1,0:T(8,128)(2,1)S(1)} %get-tuple-element.370), channel_id=1, source_target_pairs={{0,2},{1,3},{2,0},{3,1},{4,6},{5,7},{6,4},{7,5},{8,10},{9,11},{10,... | collective-permute-start | bytes 688136 | tf_op jit(solution)/shard_map/ppermute | solution.py:435
  89.3 9.3 %collective-permute-start.29 = (bf16[2,448,128]{2,1,0:T(8,128)(2,1)S(1)}, bf16[2,448,128]{2,1,0:T(8,128)(2,1)S(1)}, u32[]{:S(2)}, u32[]{:S(2)}) collective-permute-start(bf16[2,448,128]{2,1,0:T(8,128)(2,1)S(1)} %get-tuple-element.372), channel_id=1, source_target_pairs={{0,4},{1,5},{2,6},{3,7},{4,0},{5,1},{6,2},{7,3},{8,12},{9,13},{10,... | collective-permute-start | bytes 688136 | tf_op jit(solution)/shard_map/ppermute | solution.py:435
  90.8 7.7 %collective-permute-start.28 = (bf16[1,448,128]{2,1,0:T(8,128)(2,1)S(1)}, bf16[1,448,128]{2,1,0:T(8,128)(2,1)S(1)}, u32[]{:S(2)}, u32[]{:S(2)}) collective-permute-start(bf16[1,448,128]{2,1,0:T(8,128)(2,1)S(1)} %get-tuple-element.398), channel_id=1, source_target_pairs={{0,4},{1,5},{2,6},{3,7},{4,0},{5,1},{6,2},{7,3},{8,12},{9,13},{10,... | collective-permute-start | bytes 344072 | tf_op jit(solution)/shard_map/ppermute | solution.py:435
  98.7 7.7 %collective-permute-start.33 = (bf16[1,448,128]{2,1,0:T(8,128)(2,1)S(1)}, bf16[1,448,128]{2,1,0:T(8,128)(2,1)S(1)}, u32[]{:S(2)}, u32[]{:S(2)}) collective-permute-start(bf16[1,448,128]{2,1,0:T(8,128)(2,1)S(1)} %get-tuple-element.394), channel_id=1, source_target_pairs={{0,4},{1,5},{2,6},{3,7},{4,0},{5,1},{6,2},{7,3},{8,12},{9,13},{10,... | collective-permute-start | bytes 344072 | tf_op jit(solution)/shard_map/ppermute | solution.py:435
  107.4 10.4 %collective-permute-start.40 = (bf16[1,448,128]{2,1,0:T(8,128)(2,1)S(1)}, bf16[1,448,128]{2,1,0:T(8,128)(2,1)S(1)}, u32[]{:S(2)}, u32[]{:S(2)}) collective-permute-start(bf16[1,448,128]{2,1,0:T(8,128)(2,1)S(1)} %get-tuple-element.390), channel_id=1, source_target_pairs={{0,4},{1,5},{2,6},{3,7},{4,0},{5,1},{6,2},{7,3},{8,12},{9,13},{10,... | collective-permute-start | bytes 344072 | tf_op jit(solution)/shard_map/ppermute | solution.py:435
  108.8 9.0 %collective-permute-start.38 = (bf16[1,448,128]{2,1,0:T(8,128)(2,1)S(1)}, bf16[1,448,128]{2,1,0:T(8,128)(2,1)S(1)}, u32[]{:S(2)}, u32[]{:S(2)}) collective-permute-start(bf16[1,448,128]{2,1,0:T(8,128)(2,1)S(1)} %get-tuple-element.392), channel_id=1, source_target_pairs={{0,2},{1,3},{2,0},{3,1},{4,6},{5,7},{6,4},{7,5},{8,10},{9,11},{10,... | collective-permute-start | bytes 344072 | tf_op jit(solution)/shard_map/ppermute | solution.py:435
  112.9 8.9 %collective-permute-start.36 = (bf16[2,448,128]{2,1,0:T(8,128)(2,1)S(1)}, bf16[2,448,128]{2,1,0:T(8,128)(2,1)S(1)}, u32[]{:S(2)}, u32[]{:S(2)}) collective-permute-start(bf16[2,448,128]{2,1,0:T(8,128)(2,1)S(1)} %get-tuple-element.366), channel_id=1, source_target_pairs={{0,2},{1,3},{2,0},{3,1},{4,6},{5,7},{6,4},{7,5},{8,10},{9,11},{10,... | collective-permute-start | bytes 688136 | tf_op jit(solution)/shard_map/ppermute | solution.py:435
  114.2 7.7 %collective-permute-start.35 = (bf16[2,448,128]{2,1,0:T(8,128)(2,1)S(1)}, bf16[2,448,128]{2,1,0:T(8,128)(2,1)S(1)}, u32[]{:S(2)}, u32[]{:S(2)}) collective-permute-start(bf16[2,448,128]{2,1,0:T(8,128)(2,1)S(1)} %get-tuple-element.368), channel_id=1, source_target_pairs={{0,4},{1,5},{2,6},{3,7},{4,0},{5,1},{6,2},{7,3},{8,12},{9,13},{10,... | collective-permute-start | bytes 688136 | tf_op jit(solution)/shard_map/ppermute | solution.py:435
  (30 other events, 153.0 us)
